TPU v7x, 32 devices: a whole 2x2x4 slice. The times are simulated.
32 devices in a mesh: seq: 8 (over z, x), head: 4 (over y, core).
Axes of the slice: x: 2, y: 2, z: 4, core: 2. Of those that a mesh axis runs over, the one named last changes fastest.
Arguments:
- cached_probs: bfloat16 [32, 40, 8, 128, 128], P('seq', 'head'), may hold values from 0 to 1, as said below
- out_old: bfloat16 [4096, 5120], P('seq', 'head'), may hold values from -6 to 6
- key_lists: int32 [32, 8], P('seq'), may hold values from 0 to 31, as said below
- changed_block_numbers: int32 [8], replicated, may hold values from 0 to 31, as said below
- delta_v: bfloat16 [1024, 1024], P('seq', 'head'), may hold values from -24 to 24
- w_out: bfloat16 [5120, 5120], P('head', 'seq'), may hold values from -0.078125 to 0.078125
Outputs:
- attn_new: bfloat16 [4096, 5120], P('seq', 'head')
- out_proj: bfloat16 [4096, 5120], P('seq', 'head')
Inputs may be any that keep to these rules, and one draw needn't show every extreme that they name: `changed_block_numbers`: the changed block numbers are all different; the first block and the last block are always among them. `key_lists`: each query block lists 8 different key blocks; some list many changed blocks, most list few. `cached_probs`: for each query block, head and row, the weights over the row's listed keys are positive and sum to at most 1.
All inputs are finite; a program needn't handle non-finite values.
Results may differ from a plain program's by a relative error of at most 0.017.
Values may be sent and summed in bfloat16 or wider, within the bound.
No kernel may reach another device: no remote copies, remote signals or barrier semaphores. Data moves between devices by JAX's collectives and lax.ppermute only.
A program may use at most 128 MiB of HBM per device.

v0:
```python
import jax
import jax.numpy as jnp
from jax import lax
from jax.sharding import PartitionSpec as P

HD = 128
BLK = 128
GROUP = 5


def local(cached_probs, out_old, key_lists, changed_block_numbers, delta_v, w_out):
    blocks_here = cached_probs.shape[0]
    heads_here = cached_probs.shape[1]
    topk_here = cached_probs.shape[2]
    values_here = heads_here // GROUP
    change_rows = delta_v.reshape(delta_v.shape[0] // BLK, BLK * values_here * HD)
    flat_lists = key_lists.reshape(blocks_here * topk_here)
    every_change = lax.all_gather(change_rows, "seq", axis=0, tiled=True)
    onehot = (flat_lists[:, None] == changed_block_numbers[None, :]).astype(jnp.bfloat16)
    selected = jnp.dot(onehot, every_change, preferred_element_type=jnp.float32)
    picked = selected.astype(jnp.bfloat16).reshape(blocks_here, topk_here, BLK, values_here, HD)
    tiles = cached_probs.reshape(blocks_here, values_here, GROUP, topk_here, BLK, BLK)
    delta_out = jnp.einsum("qvgkij,qkjvd->qivgd", tiles, picked, preferred_element_type=jnp.float32)
    delta_out = delta_out.reshape(blocks_here * BLK, heads_here * HD)
    attn_new = (out_old.astype(jnp.float32) + delta_out).astype(jnp.bfloat16)
    terms = jnp.dot(
        attn_new,
        lax.all_gather(w_out, "seq", axis=1, tiled=True),
        preferred_element_type=jnp.float32,
    )
    out_proj = lax.psum_scatter(terms.astype(jnp.bfloat16), "head", scatter_dimension=1, tiled=True)
    return (attn_new, out_proj)


def solution(mesh):
    placed = (
        P("seq", "head", None, None, None),
        P("seq", "head"),
        P("seq", None),
        P(),
        P("seq", "head"),
        P("head", "seq"),
    )
    return jax.shard_map(
        local,
        mesh=mesh,
        in_specs=placed,
        out_specs=(P("seq", "head"), P("seq", "head")),
        check_vma=False,
    )
```

profile of v0, /device:TPU:1, one launch (start us, length us, event | category | flops | bytes accessed | tf_op | source)
XLA Modules:
  0.0 275.1 jit_solution(1448095831073162634)
XLA Ops:
  7.2 0.0 all-gather.3.cloned.1.call-start
  7.2 0.7 all-gather.3.cloned.1.call-update
  7.9 0.0 reduce-scatter.2.cloned.1.call-start
  7.9 0.0 copy-start.1
  8.0 0.0 copy-start.2
  8.0 0.0 copy-start.3
  8.0 16.7 %copy.15 = bf16[4,2,5,8,128,128]{4,3,5,2,1,0:T(8,128)(2,1)} copy(bf16[4,2,5,8,128,128]{5,4,3,2,1,0:T(8,128)(2,1)} %bitcast.23) | data formatting | bytes 20971520 | tf_op jit(solution)/shard_map/reshape | solution.py:22
  24.7 0.0 copy-done.1
  24.8 0.0 copy-done.2
  24.8 0.1 eq.15
  24.9 35.7 %all-gather = bf16[8,1,32768]{2,1,0:T(2,128)(2,1)S(1)} all-gather(bf16[1,1,32768]{2,1,0:T(2,128)(2,1)S(1)} %reshape.22), channel_id=1, replica_groups=mesh['seq'=8,'head'=4] {'seq'}, dimensions={0}, use_global_device_ids=true | all-gather | bytes 589824 | tf_op jit(solution)/shard_map/all_gather | solution.py:18
  60.5 0.0 copy-done.3
  60.5 0.8 convolution_convert_fusion
  61.3 5.9 %fusion.3 = f32[4,128,2,5,128]{1,4,3,2,0:T(8,128)S(1)} fusion(bf16[4,2,5,8,128,128]{4,3,5,2,1,0:T(8,128)(2,1)} %copy.15, bf16[4,8,128,2,128,1]{4,1,3,2,0,5:T(8,128)(2,1)S(1)} %bitcast.25), kind=kOutput, calls=%fused_computation.6 | convolution fusion | flops 1342177280 | bytes 15204352 | tf_op jit(solution)/shard_map/qvgkij,qkjvd->qivgd/dot_general | solution.py:23
  67.2 1.7 copy.16
  68.9 2.4 copy.13
  71.4 2.9 %fusion = bf16[512,1280]{0,1:T(8,128)(2,1)} fusion(f32[160,8,4,128]{3,2,1,0:T(4,128)S(1)} %bitcast.24, bf16[512,1280]{0,1:T(8,128)(2,1)} %copy.13), kind=kLoop, calls=%fused_computation.3 | loop fusion | flops 1966080 | bytes 5242880 | tf_op jit(solution)/shard_map/convert_element_type | solution.py:25
  74.3 130.1 %all-gather.3.cloned.1.call-done = bf16[1280,5120]{1,0:T(8,128)(2,1)} async-done(((bf16[1280,640]{1,0:T(8,128)(2,1)}), bf16[1280,5120]{1,0:T(8,128)(2,1)}) %all-gather.3.cloned.1.call-update) | async-done | bytes 13107216 | tf_op jit(solution)/shard_map/all_gather | solution.py:28
  204.4 13.7 %convolution_convert_fusion.1 = bf16[512,5120]{1,0:T(8,128)(2,1)} fusion(bf16[512,1280]{0,1:T(8,128)(2,1)} %fusion, bf16[1280,5120]{1,0:T(8,128)(2,1)} %all-gather.3.cloned.1.call-done), kind=kOutput, calls=%fused_computation.1 | convolution fusion | flops 6713507840 | bytes 19660800 | tf_op jit(solution)/shard_map/dot_general | solution.py:26
  218.1 0.0 copy-start
  218.1 0.0 reduce-scatter.2.cloned.1.call-update
  218.1 1.3 copy-done
  219.4 1.4 copy.17
  220.8 47.4 %reduce-scatter.2.cloned.1.call-done = bf16[512,1280]{1,0:T(8,128)(2,1)} async-done(((bf16[512,5120]{1,0:T(8,128)(2,1)}), bf16[512,1280]{1,0:T(8,128)(2,1)}) %reduce-scatter.2.cloned.1.call-update) | async-done | bytes 1310736 | tf_op jit(solution)/shard_map/reduce_scatter | solution.py:31
  (1 shorter events, 0.0 us)
Async XLA Ops:
  7.2 197.2 %all-gather.3.cloned.1.call-start = ((), (), s32[]{:S(2)}) async-start(), calls=%async_computation.1 | async-start | bytes 14745600 | tf_op jit(solution)/shard_map/all_gather | solution.py:28
  7.9 260.4 %reduce-scatter.2.cloned.1.call-start = ((), (), s32[]{:S(2)}) async-start(), calls=%async_computation.2 | async-start | bytes 6553600 | tf_op jit(solution)/shard_map/reduce_scatter | solution.py:31
  7.9 16.8 %copy-start.1 = (bf16[128,256]{1,0:T(8,128)(2,1)S(1)}, bf16[128,256]{1,0:T(8,128)(2,1)}, u32[]{:S(2)}) copy-start(bf16[128,256]{1,0:T(8,128)(2,1)} %param.10) | copy-start | bytes 196612
  8.0 16.8 %copy-start.2 = (s32[4,8]{1,0:T(4,128)S(1)}, s32[4,8]{1,0:T(4,128)}, u32[]{:S(2)}) copy-start(s32[4,8]{1,0:T(4,128)} %param.8) | copy-start | bytes 388
  8.0 52.5 %copy-start.3 = (s32[8]{0:T(128)S(1)}, s32[8]{0:T(128)}, u32[]{:S(2)}) copy-start(s32[8]{0:T(128)} %param.9) | copy-start | bytes 100
  218.1 1.3 copy-start
Sparse Core Ops, SparseCore 0:
  10.2 194.1 all-gather.2
  218.2 49.9 reduce-scatter.1
where the time goes:
time: 276 us; the launch traced here: 275 us
  waiting for transfers between devices  178 us (64%)
  blocking collectives  35.7 us (13%)
  local copies, waits for them, and re-layouts  23.7 us (9%)
  matrix products  20.4 us (7%)
  between operations  14.1 us (5%)
  other arithmetic  2.9 us (1%)
    all_gather x1, waiting for transfers between devices, local(): lax.all_gather(w_out, 'seq', axis=1, tiled=True)  130 us
    reduce_scatter x1, waiting for transfers between devices, local(): lax.psum_scatter(terms.astype(jnp.bfloat16), 'head', scatter_dimension=1,...  47.4 us
    all_gather x1, blocking collectives, local(): every_change = lax.all_gather(change_rows, 'seq', axis=0, tiled=True)  35.7 us
    reshape x1, local copies, waits for them, and re-layouts, local(): cached_probs.reshape(blocks_here, values_here, GROUP, topk_here, BLK, BLK)  16.7 us
    dot_general x1, matrix products, local(): jnp.dot(attn_new, lax.all_gather(w_out, 'seq', axis=1, tiled=True), prefe...  13.7 us
    dot_general x1, matrix products, local(): jnp.einsum('qvgkij,qkjvd->qivgd', tiles, picked, preferred_element_type=j...  5.86 us
  transfers between devices with their start and end apart: 2, of which 2 were waited for; matrix products, arithmetic and copies ran while one was open for 12% of the time, Pallas kernels for 0%

commit v1 on v0

v1 whole, which is shorter than its diff:
```python
import functools

import jax
import jax.numpy as jnp
from jax import lax
from jax.experimental import pallas as pl
from jax.experimental.pallas import tpu as pltpu
from jax.sharding import PartitionSpec as P

BLK = 128
GROUP = 5
BOTH = ("seq", "head")
MIB = 1 << 20


def attention_kernel(slot_ref, probs_ref, old_ref, near_ref, far_ref, new_ref, held, total, arrived):
    blocks, heads, topk = probs_ref.shape[:3]
    values = heads // GROUP

    def copy(q, k):
        at = q * topk + k
        return pltpu.make_async_copy(probs_ref.at[q, :, k], held.at[at], arrived.at[at])

    for q in range(blocks):
        for k in range(topk):

            @pl.when(slot_ref[q * topk + k] >= 0)
            def _():
                copy(q, k).start()

    total[...] = old_ref[...].astype(jnp.float32)

    @pl.loop(0, blocks)
    def _(q):
        rows = pl.ds(pl.multiple_of(q * BLK, BLK), BLK)

        @pl.loop(0, topk)
        def _(k):
            slot = slot_ref[q * topk + k]

            @pl.when(slot >= 0)
            def _():
                copy(q, k).wait()
                place = lax.shift_right_logical(slot, 1)
                change = jnp.where(lax.bitwise_and(slot, 1) == 1, far_ref[place], near_ref[place])
                for v in range(values):
                    weights = held[q * topk + k, v * GROUP:(v + 1) * GROUP].reshape(GROUP * BLK, BLK)
                    part = jnp.dot(weights, change[:, v * BLK:(v + 1) * BLK], preferred_element_type=jnp.float32)
                    for g in range(GROUP):
                        at = (v * GROUP + g) * BLK
                        total[rows, at:at + BLK] += part[g * BLK:(g + 1) * BLK]

    new_ref[...] = total[...].astype(jnp.bfloat16)


def refresh(slots, cached_probs, out_old, near, far):
    blocks, heads, topk = cached_probs.shape[:3]
    near = near.reshape(-1, BLK, near.shape[-1])
    far = far.reshape(-1, BLK, far.shape[-1])
    flops = 2 * cached_probs.size * BLK // 4
    return pl.pallas_call(
        attention_kernel,
        out_shape=jax.ShapeDtypeStruct(out_old.shape, jnp.bfloat16),
        grid_spec=pltpu.PrefetchScalarGridSpec(
            num_scalar_prefetch=1,
            grid=(),
            in_specs=[pl.BlockSpec(memory_space=pl.ANY)] + [pl.BlockSpec(memory_space=pltpu.VMEM)] * 3,
            out_specs=pl.BlockSpec(memory_space=pltpu.VMEM),
            scratch_shapes=[
                pltpu.VMEM((blocks * topk, heads, BLK, BLK), jnp.bfloat16),
                pltpu.VMEM(out_old.shape, jnp.float32),
                pltpu.SemaphoreType.DMA((blocks * topk,)),
            ],
        ),
        compiler_params=pltpu.CompilerParams(vmem_limit_bytes=32 * MIB),
        cost_estimate=pl.CostEstimate(flops=flops, bytes_accessed=cached_probs.size, transcendentals=0),
        name="attention",
    )(slots, cached_probs, out_old, near, far)


def product_kernel(count, *refs):
    lefts, right_ref, out_ref = refs[:count], refs[count], refs[count + 1]
    base = 0
    for left in lefts:
        step = min(256, left.shape[0])

        @pl.loop(0, left.shape[0] // step)
        def _(i, left=left, base=base, step=step):
            at = pl.multiple_of(i * step, step)
            out_ref[pl.ds(base + at, step), :] = jnp.dot(
                left[pl.ds(at, step), :], right_ref[...], preferred_element_type=jnp.float32
            ).astype(jnp.bfloat16)

        base += left.shape[0]


def product(lefts, right):
    rows, depth, width = sum(left.shape[0] for left in lefts), right.shape[0], right.shape[1]
    return pl.pallas_call(
        functools.partial(product_kernel, len(lefts)),
        out_shape=jax.ShapeDtypeStruct((rows, width), jnp.bfloat16),
        in_specs=[pl.BlockSpec(memory_space=pltpu.VMEM)] * (len(lefts) + 1),
        out_specs=pl.BlockSpec(memory_space=pltpu.VMEM),
        compiler_params=pltpu.CompilerParams(vmem_limit_bytes=32 * MIB),
        cost_estimate=pl.CostEstimate(
            flops=2 * rows * depth * width,
            bytes_accessed=2 * (rows * depth + depth * width + rows * width),
            transcendentals=0,
        ),
        name="product",
    )(*lefts, right)


def add(a, b):
    return (a.astype(jnp.float32) + b.astype(jnp.float32)).astype(jnp.bfloat16)


def slots_of(key_lists, changed_block_numbers, me):
    count = changed_block_numbers.shape[0]
    places = jnp.bitwise_xor(jnp.arange(count, dtype=jnp.int32), me)
    hit = key_lists.reshape(-1)[:, None] == changed_block_numbers[None, :]
    return jnp.max(jnp.where(hit, places[None, :], -1), axis=1)


def local_any(cached_probs, out_old, key_lists, changed_block_numbers, delta_v, w_out):
    every = lax.all_gather(delta_v, "seq", axis=0, tiled=True)
    every = every.reshape(-1, 2, BLK, every.shape[-1])
    slots = slots_of(key_lists, changed_block_numbers, jnp.int32(0))
    attn_new = refresh(slots, cached_probs, out_old, every[:, 0], every[:, 1])
    terms = jnp.dot(
        attn_new, lax.all_gather(w_out, "seq", axis=1, tiled=True), preferred_element_type=jnp.float32
    )
    out_proj = lax.psum_scatter(terms.astype(jnp.bfloat16), "head", scatter_dimension=1, tiled=True)
    return attn_new, out_proj


def move(value, where):
    pairs = []
    for z in range(4):
        for x in range(2):
            for y in range(2):
                for c in range(2):
                    to = where(z, x, y, c)
                    if to is not None:
                        tz, tx, ty, tc = to
                        pairs.append((((z * 2 + x) * 2 + y) * 2 + c, ((tz * 2 + tx) * 2 + ty) * 2 + tc))
    return lax.ppermute(value, BOTH, pairs)


def inner(z):
    return z in (1, 2)


CUTS = (384, 256)


def local_line(cached_probs, out_old, key_lists, changed_block_numbers, delta_v, w_out):
    s, h = lax.axis_index("seq"), lax.axis_index("head")
    z, x, y, c = s // 2, s % 2, h // 2, h % 2
    half = z // 2
    is_inner = (z == 1) | (z == 2)
    rows = out_old.shape[0]

    line = [delta_v] + [move(delta_v, lambda z, x, y, c, k=k: (z ^ k, x, y, c)) for k in (1, 2, 3)]
    near = jnp.concatenate(line, axis=0)
    far = move(near, lambda z, x, y, c: (z, 1 - x, y, c))

    pair = move(w_out, lambda z, x, y, c: (z ^ 1, x, y, c))
    cross = move(w_out, lambda z, x, y, c: (3 - z, x, y, c) if inner(z) else None)
    cross_end = move(cross, lambda z, x, y, c: (z ^ 1, x, y, c) if inner(z) else None)
    lasts, at = [], 0
    for width in CUTS:
        lasts.append(move(pair[:, at:at + width], lambda z, x, y, c: (3 - z, x, y, c) if inner(z) else None))
        at += width

    slots = slots_of(key_lists, changed_block_numbers, s.astype(jnp.int32))
    attn_new = refresh(slots, cached_probs, out_old, near, far)

    other = move(attn_new, lambda z, x, y, c: (z, 1 - x, y, c))
    ends = [
        move(attn_new[r:r + rows // 2], lambda z, x, y, c: None if inner(z) else (z ^ 1, x, y, c))
        for r in (0, rows // 2)
    ]
    ends_other = [move(v, lambda z, x, y, c: (z, 1 - x, y, c) if inner(z) else None) for v in ends]

    mine = [attn_new, other]
    p_own, p_pair = product(mine, w_out), product(mine, pair)
    keep = z % 2 == c
    s_half = add(
        jnp.where(keep, p_own, p_pair),
        move(jnp.where(keep, p_pair, p_own), lambda z, x, y, c: (z, x, y, 1 - c)),
    )
    p_cross = product(mine, jnp.where(is_inner, cross, cross_end))
    s_cross = add(p_cross, move(p_cross, lambda z, x, y, c: (z, x, y, 1 - c) if c != z // 2 else None))
    over = move(
        jnp.where(y == half, s_cross, s_half),
        lambda z, x, y, c: (z, x, 1 - y, c) if y != z // 2 or c == z // 2 else None,
    )
    done = add(jnp.where(y == half, s_half, s_cross), over)
    done_far = move(
        done[rows:], lambda z, x, y, c: (z, 1 - x, y, c) if y == z // 2 or c == z // 2 else None
    )

    nears, fars = [], []
    for last in lasts:
        p = product(mine + ends + ends_other, last)
        sums = add(p, move(p, lambda z, x, y, c: (z, x, y, 1 - c) if inner(z) and c == z // 2 else None))
        full = add(
            sums,
            move(
                sums,
                lambda z, x, y, c: (z, x, 1 - y, c) if inner(z) and y == z // 2 and c != z // 2 else None,
            ),
        )

        def send(value, to):
            return move(
                value,
                lambda z, x, y, c: to(z, x, y, c) if inner(z) and y != z // 2 and c != z // 2 else None,
            )

        far_inner = send(full[rows:2 * rows], lambda z, x, y, c: (z, 1 - x, y, c))
        near_end = send(full[2 * rows:3 * rows], lambda z, x, y, c: (z ^ 1, x, y, c))
        far_end = send(full[3 * rows:], lambda z, x, y, c: (z ^ 1, 1 - x, y, c))
        nears.append(jnp.where(is_inner, full[:rows], near_end))
        fars.append(jnp.where(is_inner, far_inner, far_end))

    is_last = (y != half) & (c != half)
    near_half = jnp.where(is_last, jnp.concatenate(nears, axis=1), done[:rows])
    far_half = jnp.where(is_last, jnp.concatenate(fars, axis=1), done_far)
    first = jnp.where(x == 0, near_half, far_half)
    second = jnp.where(x == 0, far_half, near_half)
    return attn_new, jnp.concatenate([first, second], axis=1)


def solution(mesh):
    placed = (
        P("seq", "head", None, None, None),
        P("seq", "head"),
        P("seq", None),
        P(),
        P("seq", "head"),
        P("head", "seq"),
    )
    on_line = mesh.shape["seq"] == 8 and mesh.shape["head"] == 4
    return jax.shard_map(
        local_line if on_line else local_any,
        mesh=mesh,
        in_specs=placed,
        out_specs=(P("seq", "head"), P("seq", "head")),
        check_vma=False,
    )
```

time: 276 us -> 196 us (0.71)
  the two profiles are of different devices: /device:TPU:1 before, /device:TPU:26 now
where the time goes in v1:
time: 196 us; the launch traced here: 195 us
  waiting for transfers between devices  89.2 us (46%)
  starting transfers between devices  44.2 us (23%)
  Pallas kernels  24.4 us (12%)
  other arithmetic  21.4 us (11%)
  local copies, waits for them, and re-layouts  15.1 us (8%)
    ppermute x28, waiting for transfers between devices, move(): return lax.ppermute(value, BOTH, pairs)  89.2 us
    ppermute x28, starting transfers between devices, move(): return lax.ppermute(value, BOTH, pairs)  44.2 us
    pallas_call x5, Pallas kernels, product(): pl.pallas_call(functools.partial(product_kernel, len(lefts)), out_shape=j...  20.5 us
    convert_element_type x5, other arithmetic, add(): return (a.astype(jnp.float32) + b.astype(jnp.float32)).astype(jnp.bfloat16)  9.36 us
    unnamed x21, local copies, waits for them, and re-layouts  8.57 us
    slice x2, local copies, waits for them, and re-layouts, local_line(): pair[:, at:at + width]  4.24 us
  transfers between devices with their start and end apart: 28, of which 9 were waited for; matrix products, arithmetic and copies ran while one was open for 14% of the time, Pallas kernels for 12%

profile of v1, /device:TPU:26, one launch (start us, length us, event | category | flops | bytes accessed | tf_op | source)
XLA Modules:
  0.0 195.2 jit_solution(8800208507265880719)
XLA Ops:
  1.5 3.6 %collective-permute-start.2 = (bf16[128,256]{1,0:T(8,128)(2,1)}, bf16[128,256]{1,0:T(8,128)(2,1)S(1)}, u32[]{:S(2)}, u32[]{:S(2)}) collective-permute-start(bf16[128,256]{1,0:T(8,128)(2,1)} %param.10), channel_id=1, source_target_pairs={{0,24},{1,25},{2,26},{3,27},{4,28},{5,29},{6,30},{7,31},{8,16},{9,... | collective-permute-start | bytes 196616 | tf_op jit(solution)/shard_map/ppermute | solution.py:147
  5.1 1.9 collective-permute-start.19
  7.9 1.9 collective-permute-done.1
  11.9 4.3 %collective-permute-done.3 = bf16[512,256]{1,0:T(8,128)(2,1)S(1)} collective-permute-done((bf16[512,256]{1,0:T(8,128)(2,1)S(1)}, bf16[512,256]{1,0:T(8,128)(2,1)S(1)}, u32[]{:S(2)}, u32[]{:S(2)}) %collective-permute-start.3) | collective-permute-done | bytes 262176 | tf_op jit(solution)/shard_map/ppermute | solution.py:147
  16.2 4.0 %copy-done.1 = bf16[4,10,8,128,128]{4,3,2,1,0:T(8,128)(2,1)S(1)} copy-done((bf16[4,10,8,128,128]{4,3,2,1,0:T(8,128)(2,1)S(1)}, bf16[4,10,8,128,128]{4,3,2,1,0:T(8,128)(2,1)}, u32[]{:S(2)}) %copy-start.1) | copy-done | bytes 10485784
  20.2 1.3 copy-done.7
  21.6 3.9 %attention.1.refs_0_ = bf16[512,1280]{1,0:T(8,128)(2,1)} custom-call(s32[32]{0:T(128)S(1)} %select_reduce_fusion.slot_ref, bf16[4,10,8,128,128]{4,3,2,1,0:T(8,128)(2,1)S(1)} %copy-done.1, bf16[512,1280]{1,0:T(8,128)(2,1)S(1)} %copy-done.7, bf16[4,128,256]{2,1,0:T(8,128)(2,1)S(1)} %bitcast.2, bf16[4,128,256]{2,1,0:T(8,128)(2,1)S(1)} %bitcast.3), custom_call_target="tpu_custom_call" | custom-call | flops 335544320 | bytes 5242880 | tf_op jit(solution)/shard_map/attention/pallas_call | solution.py:61
  26.3 1.4 fusion
  27.7 5.7 %collective-permute-start.5 = (bf16[256,1280]{1,0:T(8,128)(2,1)S(1)}, bf16[256,1280]{1,0:T(8,128)(2,1)S(1)}, u32[]{:S(2)}, u32[]{:S(2)}) collective-permute-start(bf16[256,1280]{1,0:T(8,128)(2,1)S(1)} %get-tuple-element.10), channel_id=1, source_target_pairs={{0,8},{1,9},{2,10},{3,11},{4,12},{5,13},{6,14},{7,15},{24,16},{25,... | collective-permute-start | bytes 1966088 | tf_op jit(solution)/shard_map/ppermute | solution.py:147
  33.5 2.3 %collective-permute-start.6 = (bf16[256,1280]{1,0:T(8,128)(2,1)S(1)}, bf16[256,1280]{1,0:T(8,128)(2,1)}, u32[]{:S(2)}, u32[]{:S(2)}) collective-permute-start(bf16[256,1280]{1,0:T(8,128)(2,1)S(1)} %get-tuple-element.9), channel_id=1, source_target_pairs={{0,8},{1,9},{2,10},{3,11},{4,12},{5,13},{6,14},{7,15},{24,16},{25,... | collective-permute-start | bytes 1966088 | tf_op jit(solution)/shard_map/ppermute | solution.py:147
  35.8 1.3 collective-permute-start.20
  37.0 7.4 %collective-permute-done.9.refs_2_ = bf16[1280,640]{1,0:T(8,128)(2,1)} collective-permute-done((bf16[1280,640]{1,0:T(8,128)(2,1)}, bf16[1280,640]{1,0:T(8,128)(2,1)}, u32[]{:S(2)}, u32[]{:S(2)}) %collective-permute-start.9) | collective-permute-done | bytes 1638432 | tf_op jit(solution)/shard_map/ppermute | solution.py:147
  44.5 2.3 %slice.58 = bf16[1280,384]{1,0:T(8,128)(2,1)} slice(bf16[1280,640]{1,0:T(8,128)(2,1)} %collective-permute-done.9.refs_2_), slice={[0:1280], [0:384]} | slice | bytes 1966080 | tf_op jit(solution)/shard_map/slice | solution.py:173
  46.7 1.6 collective-permute-start.10
  48.4 9.2 %collective-permute-done.5.refs_2_ = bf16[256,1280]{1,0:T(8,128)(2,1)S(1)} collective-permute-done((bf16[256,1280]{1,0:T(8,128)(2,1)S(1)}, bf16[256,1280]{1,0:T(8,128)(2,1)S(1)}, u32[]{:S(2)}, u32[]{:S(2)}) %collective-permute-start.5) | collective-permute-done | bytes 655392 | tf_op jit(solution)/shard_map/ppermute | solution.py:147
  57.6 1.6 collective-permute-start.7
  59.1 11.1 %collective-permute-done.6.refs_3_ = bf16[256,1280]{1,0:T(8,128)(2,1)} collective-permute-done((bf16[256,1280]{1,0:T(8,128)(2,1)S(1)}, bf16[256,1280]{1,0:T(8,128)(2,1)}, u32[]{:S(2)}, u32[]{:S(2)}) %collective-permute-start.6) | collective-permute-done | bytes 655392 | tf_op jit(solution)/shard_map/ppermute | solution.py:147
  70.3 1.6 collective-permute-start.8
  71.9 2.0 %slice.61 = bf16[1280,256]{1,0:T(8,128)(2,1)} slice(bf16[1280,640]{1,0:T(8,128)(2,1)} %collective-permute-done.9.refs_2_), slice={[0:1280], [384:640]} | slice | bytes 1310720 | tf_op jit(solution)/shard_map/slice | solution.py:173
  74.9 1.5 collective-permute-start.14
  76.4 1.3 copy-done.5
  77.7 4.3 %product.8 = bf16[1024,640]{1,0:T(8,128)(2,1)S(1)} custom-call(bf16[512,1280]{1,0:T(8,128)(2,1)S(1)} %copy-done, bf16[512,1280]{1,0:T(8,128)(2,1)S(1)} %copy-done.5, bf16[1280,640]{1,0:T(8,128)(2,1)} %collective-permute-done.9.refs_2_), custom_call_target="tpu_custom_call" | custom-call | flops 1677721600 | bytes 5570560 | tf_op jit(solution)/shard_map/product/pallas_call | solution.py:99
  82.0 2.7 %product.7 = bf16[1024,640]{1,0:T(8,128)(2,1)S(1)} custom-call(bf16[512,1280]{1,0:T(8,128)(2,1)S(1)} %copy-done, bf16[512,1280]{1,0:T(8,128)(2,1)S(1)} %copy-done.5, bf16[1280,640]{1,0:T(8,128)(2,1)S(1)} %copy-done.8), custom_call_target="tpu_custom_call" | custom-call | flops 1677721600 | bytes 5570560 | tf_op jit(solution)/shard_map/product/pallas_call | solution.py:99
  84.8 4.3 %product.6 = bf16[2048,256]{1,0:T(8,128)(2,1)S(1)} custom-call(bf16[512,1280]{1,0:T(8,128)(2,1)S(1)} %copy-done, bf16[512,1280]{1,0:T(8,128)(2,1)S(1)} %copy-done.6, bf16[256,1280]{1,0:T(8,128)(2,1)S(1)} %collective-permute-done.5.refs_2_, bf16[256,1280]{1,0:T(8,128)(2,1)} %collective-permute-done.6.refs_3_, ...), custom_call_target="tpu_custom_call" | custom-call | flops 1342177280 | bytes 6946816 | tf_op jit(solution)/shard_map/product/pallas_call | solution.py:99
  89.9 5.3 %product.5 = bf16[2048,384]{1,0:T(8,128)(2,1)S(1)} custom-call(bf16[512,1280]{1,0:T(8,128)(2,1)S(1)} %copy-done, bf16[512,1280]{1,0:T(8,128)(2,1)S(1)} %copy-done.6, bf16[256,1280]{1,0:T(8,128)(2,1)S(1)} %collective-permute-done.5.refs_2_, bf16[256,1280]{1,0:T(8,128)(2,1)} %collective-permute-done.6.refs_3_, ...), custom_call_target="tpu_custom_call" | custom-call | flops 2013265920 | bytes 7798784 | tf_op jit(solution)/shard_map/product/pallas_call | solution.py:99
  96.0 1.3 broadcast_select_fusion.1
  97.3 1.6 broadcast_select_fusion.refs_2_
  98.9 3.8 %product.9 = bf16[1024,640]{1,0:T(8,128)(2,1)} custom-call(bf16[512,1280]{1,0:T(8,128)(2,1)S(1)} %copy-done, bf16[512,1280]{1,0:T(8,128)(2,1)S(1)} %copy-done.6, bf16[1280,640]{1,0:T(8,128)(2,1)S(1)} %broadcast_select_fusion.refs_2_), custom_call_target="tpu_custom_call" | custom-call | flops 1677721600 | bytes 5570560 | tf_op jit(solution)/shard_map/product/pallas_call | solution.py:99
  102.7 3.5 %collective-permute-start.21 = (bf16[1024,640]{1,0:T(8,128)(2,1)}, bf16[1024,640]{1,0:T(8,128)(2,1)}, u32[]{:S(2)}, u32[]{:S(2)}) collective-permute-start(bf16[1024,640]{1,0:T(8,128)(2,1)} %product.9), channel_id=1, source_target_pairs={{1,0},{3,2},{5,4},{7,6},{9,8},{11,10},{13,12},{15,14},{16,17},{18,... | collective-permute-start | bytes 3932168 | tf_op jit(solution)/shard_map/ppermute | solution.py:147
  106.2 1.2 add_convert_fusion.6
  107.5 1.8 collective-permute-start.16
  109.2 1.6 add_convert_fusion.1
  110.8 1.8 collective-permute-start.12
  112.6 3.0 %broadcast_select_fusion.2 = (bf16[1024,640]{1,0:T(8,128)(2,1)S(1)}, bf16[1024,640]{1,0:T(8,128)(2,1)S(1)}) fusion(pred[]{:T(512)S(6)} %eq.43, bf16[1024,640]{1,0:T(8,128)(2,1)} %collective-permute-done.21, bf16[1024,640]{1,0:T(8,128)(2,1)} %product.9, bf16[1024,640]{1,0:T(8,128)(2,1)} %collective-permute-done.18, bf16[1024,640]{1,0:T(8,128)(2,1)S(1)} %copy-done.3, ...), kind=kLoop, calls=%fused_computation.10 | loop fusion | flops 6553600 | bytes 9175042 | tf_op jit(solution)/shard_map/jit(_where)/select_n | solution.py:196
  115.6 3.5 %collective-permute-start.22 = (bf16[1024,640]{1,0:T(8,128)(2,1)S(1)}, bf16[1024,640]{1,0:T(8,128)(2,1)S(1)}, u32[]{:S(2)}, u32[]{:S(2)}) collective-permute-start(bf16[1024,640]{1,0:T(8,128)(2,1)S(1)} %get-tuple-element.2), channel_id=1, source_target_pairs={{0,2},{2,0},{3,1},{4,6},{6,4},{7,5},{8,10},{10,8},{11,9},{12,14},{... | collective-permute-start | bytes 3932168 | tf_op jit(solution)/shard_map/ppermute | solution.py:147
  119.1 1.8 add_convert_fusion.5
  121.0 1.3 collective-permute-start.17
  122.3 2.3 %add_convert_fusion = bf16[2048,384]{1,0:T(8,128)(2,1)S(1)} fusion(bf16[2048,384]{1,0:T(8,128)(2,1)} %collective-permute-done.12, bf16[2048,384]{1,0:T(8,128)(2,1)} %add_convert_fusion.1), kind=kLoop, calls=%fused_computation | loop fusion | flops 3145728 | bytes 4718592 | tf_op jit(solution)/shard_map/convert_element_type | solution.py:115
  124.6 1.3 collective-permute-start.13
  125.9 24.4 %collective-permute-done.17 = bf16[512,256]{1,0:T(8,128)(2,1)S(1)} collective-permute-done((bf16[512,256]{1,0:T(8,128)(2,1)S(1)}, bf16[512,256]{1,0:T(8,128)(2,1)S(1)}, u32[]{:S(2)}, u32[]{:S(2)}) %collective-permute-start.17) | collective-permute-done | bytes 262176 | tf_op jit(solution)/shard_map/ppermute | solution.py:147
  151.1 1.4 collective-permute-start.25
  152.5 1.3 collective-permute-start.26
  153.8 2.4 %add_convert_fusion.2 = bf16[1024,640]{1,0:T(8,128)(2,1)S(1)} fusion(bf16[1024,640]{1,0:T(8,128)(2,1)S(1)} %collective-permute-done.22, bf16[1024,640]{1,0:T(8,128)(2,1)S(1)} %get-tuple-element.3, pred[]{:T(512)S(6)} %eq.43, bf16[1024,640]{1,0:T(8,128)(2,1)} %collective-permute-done.21, bf16[1024,640]{1,0:T(8,128)(2,1)} %product.9), kind=kLoop, calls=%fused_computation.2 | loop fusion | flops 5898240 | bytes 6553601 | tf_op jit(solution)/shard_map/convert_element_type | solution.py:115
  157.0 20.1 %collective-permute-done.13 = bf16[512,384]{1,0:T(8,128)(2,1)S(1)} collective-permute-done((bf16[512,384]{1,0:T(8,128)(2,1)S(1)}, bf16[512,384]{1,0:T(8,128)(2,1)S(1)}, u32[]{:S(2)}, u32[]{:S(2)}) %collective-permute-start.13) | collective-permute-done | bytes 393248 | tf_op jit(solution)/shard_map/ppermute | solution.py:147
  178.1 1.4 collective-permute-start.23
  179.5 1.3 collective-permute-start.24
  182.3 10.3 %collective-permute-done.24 = bf16[512,384]{1,0:T(8,128)(2,1)} collective-permute-done((bf16[512,384]{1,0:T(8,128)(2,1)}, bf16[512,384]{1,0:T(8,128)(2,1)}, u32[]{:S(2)}, u32[]{:S(2)}) %collective-permute-start.24) | collective-permute-done | bytes 393248 | tf_op jit(solution)/shard_map/ppermute | solution.py:147
  194.1 1.2 pad_maximum_fusion
  (59 shorter events, 13.0 us)
Async XLA Ops:
  0.6 7.3 %collective-permute-start = (bf16[128,256]{1,0:T(8,128)(2,1)}, bf16[128,256]{1,0:T(8,128)(2,1)S(1)}, u32[]{:S(2)}, u32[]{:S(2)}) collective-permute-start(bf16[128,256]{1,0:T(8,128)(2,1)} %param.10), channel_id=1, source_target_pairs={{0,8},{1,9},{2,10},{3,11},{4,12},{5,13},{6,14},{7,15},{8,0},{9,1},... | collective-permute-start | bytes 196616 | tf_op jit(solution)/shard_map/ppermute | solution.py:147
  1.1 8.6 %collective-permute-start.1 = (bf16[128,256]{1,0:T(8,128)(2,1)}, bf16[128,256]{1,0:T(8,128)(2,1)S(1)}, u32[]{:S(2)}, u32[]{:S(2)}) collective-permute-start(bf16[128,256]{1,0:T(8,128)(2,1)} %param.10), channel_id=1, source_target_pairs={{0,16},{1,17},{2,18},{3,19},{4,20},{5,21},{6,22},{7,23},{8,24},{9,... | collective-permute-start | bytes 196616 | tf_op jit(solution)/shard_map/ppermute | solution.py:147
  1.5 8.3 %collective-permute-start.2 = (bf16[128,256]{1,0:T(8,128)(2,1)}, bf16[128,256]{1,0:T(8,128)(2,1)S(1)}, u32[]{:S(2)}, u32[]{:S(2)}) collective-permute-start(bf16[128,256]{1,0:T(8,128)(2,1)} %param.10), channel_id=1, source_target_pairs={{0,24},{1,25},{2,26},{3,27},{4,28},{5,29},{6,30},{7,31},{8,16},{9,... | collective-permute-start | bytes 196616 | tf_op jit(solution)/shard_map/ppermute | solution.py:147
  5.1 30.7 %collective-permute-start.19 = (bf16[1280,640]{1,0:T(8,128)(2,1)}, bf16[1280,640]{1,0:T(8,128)(2,1)}, u32[]{:S(2)}, u32[]{:S(2)}) collective-permute-start(bf16[1280,640]{1,0:T(8,128)(2,1)} %refs_2_.1), channel_id=1, source_target_pairs={{8,16},{9,17},{10,18},{11,19},{12,20},{13,21},{14,22},{15,23},{16,... | collective-permute-start | bytes 4915208 | tf_op jit(solution)/shard_map/ppermute | solution.py:147
  6.9 37.5 %collective-permute-start.9 = (bf16[1280,640]{1,0:T(8,128)(2,1)}, bf16[1280,640]{1,0:T(8,128)(2,1)}, u32[]{:S(2)}, u32[]{:S(2)}) collective-permute-start(bf16[1280,640]{1,0:T(8,128)(2,1)} %refs_2_.1), channel_id=1, source_target_pairs={{0,8},{1,9},{2,10},{3,11},{4,12},{5,13},{6,14},{7,15},{8,0},{9,1},... | collective-permute-start | bytes 4915208 | tf_op jit(solution)/shard_map/ppermute | solution.py:147
  9.8 6.4 %collective-permute-start.3 = (bf16[512,256]{1,0:T(8,128)(2,1)S(1)}, bf16[512,256]{1,0:T(8,128)(2,1)S(1)}, u32[]{:S(2)}, u32[]{:S(2)}) collective-permute-start(bf16[512,256]{1,0:T(8,128)(2,1)S(1)} %constant_dynamic-update-slice_fusion), channel_id=1, source_target_pairs={{0,4},{1,5},{2,6},{3,7},{4,0},{5,1},{6,2},{7,3},{8,12},{9,13},{10,... | collective-permute-start | bytes 786440 | tf_op jit(solution)/shard_map/ppermute | solution.py:147
  16.2 4.0 %copy-start.1 = (bf16[4,10,8,128,128]{4,3,2,1,0:T(8,128)(2,1)S(1)}, bf16[4,10,8,128,128]{4,3,2,1,0:T(8,128)(2,1)}, u32[]{:S(2)}) copy-start(bf16[4,10,8,128,128]{4,3,2,1,0:T(8,128)(2,1)} %probs_ref.1) | copy-start | bytes 31457284
  20.2 1.3 copy-start.7
  25.5 48.4 %collective-permute-start.4 = (bf16[512,1280]{1,0:T(8,128)(2,1)}, bf16[512,1280]{1,0:T(8,128)(2,1)S(1)}, u32[]{:S(2)}, u32[]{:S(2)}) collective-permute-start(bf16[512,1280]{1,0:T(8,128)(2,1)} %attention.1.refs_0_), channel_id=1, source_target_pairs={{0,4},{1,5},{2,6},{3,7},{4,0},{5,1},{6,2},{7,3},{8,12},{9,13},{10,... | collective-permute-start | bytes 3932168 | tf_op jit(solution)/shard_map/ppermute | solution.py:147
  27.7 29.8 %collective-permute-start.5 = (bf16[256,1280]{1,0:T(8,128)(2,1)S(1)}, bf16[256,1280]{1,0:T(8,128)(2,1)S(1)}, u32[]{:S(2)}, u32[]{:S(2)}) collective-permute-start(bf16[256,1280]{1,0:T(8,128)(2,1)S(1)} %get-tuple-element.10), channel_id=1, source_target_pairs={{0,8},{1,9},{2,10},{3,11},{4,12},{5,13},{6,14},{7,15},{24,16},{25,... | collective-permute-start | bytes 1966088 | tf_op jit(solution)/shard_map/ppermute | solution.py:147
  33.5 42.9 %copy-start = (bf16[512,1280]{1,0:T(8,128)(2,1)S(1)}, bf16[512,1280]{1,0:T(8,128)(2,1)}, u32[]{:S(2)}) copy-start(bf16[512,1280]{1,0:T(8,128)(2,1)} %attention.1.refs_0_) | copy-start | bytes 3932164
  33.5 36.8 %collective-permute-start.6 = (bf16[256,1280]{1,0:T(8,128)(2,1)S(1)}, bf16[256,1280]{1,0:T(8,128)(2,1)}, u32[]{:S(2)}, u32[]{:S(2)}) collective-permute-start(bf16[256,1280]{1,0:T(8,128)(2,1)S(1)} %get-tuple-element.9), channel_id=1, source_target_pairs={{0,8},{1,9},{2,10},{3,11},{4,12},{5,13},{6,14},{7,15},{24,16},{25,... | collective-permute-start | bytes 1966088 | tf_op jit(solution)/shard_map/ppermute | solution.py:147
  35.8 61.6 %collective-permute-start.20 = (bf16[1280,640]{1,0:T(8,128)(2,1)}, bf16[1280,640]{1,0:T(8,128)(2,1)}, u32[]{:S(2)}, u32[]{:S(2)}) collective-permute-start(bf16[1280,640]{1,0:T(8,128)(2,1)} %collective-permute-done.19), channel_id=1, source_target_pairs={{8,0},{9,1},{10,2},{11,3},{12,4},{13,5},{14,6},{15,7},{16,24},{17,... | collective-permute-start | bytes 4915208 | tf_op jit(solution)/shard_map/ppermute | solution.py:147
  46.7 43.2 %collective-permute-start.10 = (bf16[1280,384]{1,0:T(8,128)(2,1)}, bf16[1280,384]{1,0:T(8,128)(2,1)}, u32[]{:S(2)}, u32[]{:S(2)}) collective-permute-start(bf16[1280,384]{1,0:T(8,128)(2,1)} %slice.58), channel_id=1, source_target_pairs={{8,16},{9,17},{10,18},{11,19},{12,20},{13,21},{14,22},{15,23},{16,... | collective-permute-start | bytes 2949128 | tf_op jit(solution)/shard_map/ppermute | solution.py:147
  57.6 27.2 %collective-permute-start.7 = (bf16[256,1280]{1,0:T(8,128)(2,1)S(1)}, bf16[256,1280]{1,0:T(8,128)(2,1)}, u32[]{:S(2)}, u32[]{:S(2)}) collective-permute-start(bf16[256,1280]{1,0:T(8,128)(2,1)S(1)} %collective-permute-done.5.refs_2_), channel_id=1, source_target_pairs={{8,12},{9,13},{10,14},{11,15},{12,8},{13,9},{14,10},{15,11},{16,20... | collective-permute-start | bytes 1966088 | tf_op jit(solution)/shard_map/ppermute | solution.py:147
  70.3 14.5 %collective-permute-start.8 = (bf16[256,1280]{1,0:T(8,128)(2,1)}, bf16[256,1280]{1,0:T(8,128)(2,1)}, u32[]{:S(2)}, u32[]{:S(2)}) collective-permute-start(bf16[256,1280]{1,0:T(8,128)(2,1)} %collective-permute-done.6.refs_3_), channel_id=1, source_target_pairs={{8,12},{9,13},{10,14},{11,15},{12,8},{13,9},{14,10},{15,11},{16,20... | collective-permute-start | bytes 1966088 | tf_op jit(solution)/shard_map/ppermute | solution.py:147
  73.8 1.1 copy-start.4
  74.9 9.9 %collective-permute-start.14 = (bf16[1280,256]{1,0:T(8,128)(2,1)}, bf16[1280,256]{1,0:T(8,128)(2,1)}, u32[]{:S(2)}, u32[]{:S(2)}) collective-permute-start(bf16[1280,256]{1,0:T(8,128)(2,1)} %slice.61), channel_id=1, source_target_pairs={{8,16},{9,17},{10,18},{11,19},{12,20},{13,21},{14,22},{15,23},{16,... | collective-permute-start | bytes 1966088 | tf_op jit(solution)/shard_map/ppermute | solution.py:147
  76.4 1.3 copy-start.5
  77.7 4.3 %copy-start.8 = (bf16[1280,640]{1,0:T(8,128)(2,1)S(1)}, bf16[1280,640]{1,0:T(8,128)(2,1)}, u32[]{:S(2)}) copy-start(bf16[1280,640]{1,0:T(8,128)(2,1)} %refs_2_.1) | copy-start | bytes 4915204
  82.0 2.8 %copy-start.6 = (bf16[512,1280]{1,0:T(8,128)(2,1)S(1)}, bf16[512,1280]{1,0:T(8,128)(2,1)}, u32[]{:S(2)}) copy-start(bf16[512,1280]{1,0:T(8,128)(2,1)} %copy-done.4) | copy-start | bytes 3932164
  84.8 11.2 %copy-start.2 = (bf16[1024,640]{1,0:T(8,128)(2,1)}, bf16[1024,640]{1,0:T(8,128)(2,1)S(1)}, u32[]{:S(2)}) copy-start(bf16[1024,640]{1,0:T(8,128)(2,1)S(1)} %product.7) | copy-start | bytes 3932164
  89.2 17.1 %collective-permute-start.15 = (bf16[2048,256]{1,0:T(8,128)(2,1)S(1)}, bf16[2048,256]{1,0:T(8,128)(2,1)S(1)}, u32[]{:S(2)}, u32[]{:S(2)}) collective-permute-start(bf16[2048,256]{1,0:T(8,128)(2,1)S(1)} %product.6), channel_id=1, source_target_pairs={{8,9},{10,11},{12,13},{14,15},{17,16},{19,18},{21,20},{23,22}} | collective-permute-start | bytes 3145736 | tf_op jit(solution)/shard_map/ppermute | solution.py:147
  95.2 14.0 %collective-permute-start.11 = (bf16[2048,384]{1,0:T(8,128)(2,1)S(1)}, bf16[2048,384]{1,0:T(8,128)(2,1)S(1)}, u32[]{:S(2)}, u32[]{:S(2)}) collective-permute-start(bf16[2048,384]{1,0:T(8,128)(2,1)S(1)} %product.5), channel_id=1, source_target_pairs={{8,9},{10,11},{12,13},{14,15},{17,16},{19,18},{21,20},{23,22}} | collective-permute-start | bytes 4718600 | tf_op jit(solution)/shard_map/ppermute | solution.py:147
  97.3 15.3 %collective-permute-start.18 = (bf16[1024,640]{1,0:T(8,128)(2,1)}, bf16[1024,640]{1,0:T(8,128)(2,1)}, u32[]{:S(2)}, u32[]{:S(2)}) collective-permute-start(bf16[1024,640]{1,0:T(8,128)(2,1)} %broadcast_select_fusion.1), channel_id=1, source_target_pairs={{0,1},{1,0},{2,3},{3,2},{4,5},{5,4},{6,7},{7,6},{8,9},{9,8},{10,11... | collective-permute-start | bytes 3932168 | tf_op jit(solution)/shard_map/ppermute | solution.py:147
  102.7 9.9 %collective-permute-start.21 = (bf16[1024,640]{1,0:T(8,128)(2,1)}, bf16[1024,640]{1,0:T(8,128)(2,1)}, u32[]{:S(2)}, u32[]{:S(2)}) collective-permute-start(bf16[1024,640]{1,0:T(8,128)(2,1)} %product.9), channel_id=1, source_target_pairs={{1,0},{3,2},{5,4},{7,6},{9,8},{11,10},{13,12},{15,14},{16,17},{18,... | collective-permute-start | bytes 3932168 | tf_op jit(solution)/shard_map/ppermute | solution.py:147
  107.5 5.2 %copy-start.3 = (bf16[1024,640]{1,0:T(8,128)(2,1)S(1)}, bf16[1024,640]{1,0:T(8,128)(2,1)}, u32[]{:S(2)}) copy-start(bf16[1024,640]{1,0:T(8,128)(2,1)} %copy-done.2) | copy-start | bytes 3932164
  107.5 11.7 %collective-permute-start.16 = (bf16[2048,256]{1,0:T(8,128)(2,1)}, bf16[2048,256]{1,0:T(8,128)(2,1)}, u32[]{:S(2)}, u32[]{:S(2)}) collective-permute-start(bf16[2048,256]{1,0:T(8,128)(2,1)} %add_convert_fusion.6), channel_id=1, source_target_pairs={{9,11},{13,15},{18,16},{22,20}} | collective-permute-start | bytes 3145736 | tf_op jit(solution)/shard_map/ppermute | solution.py:147
  110.8 11.5 %collective-permute-start.12 = (bf16[2048,384]{1,0:T(8,128)(2,1)}, bf16[2048,384]{1,0:T(8,128)(2,1)}, u32[]{:S(2)}, u32[]{:S(2)}) collective-permute-start(bf16[2048,384]{1,0:T(8,128)(2,1)} %add_convert_fusion.1), channel_id=1, source_target_pairs={{9,11},{13,15},{18,16},{22,20}} | collective-permute-start | bytes 4718600 | tf_op jit(solution)/shard_map/ppermute | solution.py:147
  115.6 38.2 %collective-permute-start.22 = (bf16[1024,640]{1,0:T(8,128)(2,1)S(1)}, bf16[1024,640]{1,0:T(8,128)(2,1)S(1)}, u32[]{:S(2)}, u32[]{:S(2)}) collective-permute-start(bf16[1024,640]{1,0:T(8,128)(2,1)S(1)} %get-tuple-element.2), channel_id=1, source_target_pairs={{0,2},{2,0},{3,1},{4,6},{6,4},{7,5},{8,10},{10,8},{11,9},{12,14},{... | collective-permute-start | bytes 3932168 | tf_op jit(solution)/shard_map/ppermute | solution.py:147
  121.0 29.4 %collective-permute-start.17 = (bf16[512,256]{1,0:T(8,128)(2,1)S(1)}, bf16[512,256]{1,0:T(8,128)(2,1)S(1)}, u32[]{:S(2)}, u32[]{:S(2)}) collective-permute-start(bf16[512,256]{1,0:T(8,128)(2,1)S(1)} %slice.63), channel_id=1, source_target_pairs={{11,3},{15,7},{16,24},{20,28}} | collective-permute-start | bytes 786440 | tf_op jit(solution)/shard_map/ppermute | solution.py:147
  124.6 52.5 %collective-permute-start.13 = (bf16[512,384]{1,0:T(8,128)(2,1)S(1)}, bf16[512,384]{1,0:T(8,128)(2,1)S(1)}, u32[]{:S(2)}, u32[]{:S(2)}) collective-permute-start(bf16[512,384]{1,0:T(8,128)(2,1)S(1)} %slice.60), channel_id=1, source_target_pairs={{11,3},{15,7},{16,24},{20,28}} | collective-permute-start | bytes 1179656 | tf_op jit(solution)/shard_map/ppermute | solution.py:147
  151.1 29.7 %collective-permute-start.25 = (bf16[512,256]{1,0:T(8,128)(2,1)}, bf16[512,256]{1,0:T(8,128)(2,1)}, u32[]{:S(2)}, u32[]{:S(2)}) collective-permute-start(bf16[512,256]{1,0:T(8,128)(2,1)} %get-tuple-element.13), channel_id=1, source_target_pairs={{11,15},{15,11},{16,20},{20,16}} | collective-permute-start | bytes 786440 | tf_op jit(solution)/shard_map/ppermute | solution.py:147
  152.5 28.8 %collective-permute-start.26 = (bf16[512,256]{1,0:T(8,128)(2,1)S(1)}, bf16[512,256]{1,0:T(8,128)(2,1)}, u32[]{:S(2)}, u32[]{:S(2)}) collective-permute-start(bf16[512,256]{1,0:T(8,128)(2,1)S(1)} %get-tuple-element.12), channel_id=1, source_target_pairs={{11,7},{15,3},{16,28},{20,24}} | collective-permute-start | bytes 786440 | tf_op jit(solution)/shard_map/ppermute | solution.py:147
  156.3 37.3 %collective-permute-start.27 = (bf16[512,640]{1,0:T(8,128)(2,1)S(1)}, bf16[512,640]{1,0:T(8,128)(2,1)S(1)}, u32[]{:S(2)}, u32[]{:S(2)}) collective-permute-start(bf16[512,640]{1,0:T(8,128)(2,1)S(1)} %slice.69), channel_id=1, source_target_pairs={{0,4},{1,5},{2,6},{4,0},{5,1},{6,2},{8,12},{9,13},{10,14},{12,8},{... | collective-permute-start | bytes 1966088 | tf_op jit(solution)/shard_map/ppermute | solution.py:147
  178.1 4.2 %collective-permute-start.23 = (bf16[512,384]{1,0:T(8,128)(2,1)}, bf16[512,384]{1,0:T(8,128)(2,1)}, u32[]{:S(2)}, u32[]{:S(2)}) collective-permute-start(bf16[512,384]{1,0:T(8,128)(2,1)} %get-tuple-element.8), channel_id=1, source_target_pairs={{11,15},{15,11},{16,20},{20,16}} | collective-permute-start | bytes 1179656 | tf_op jit(solution)/shard_map/ppermute | solution.py:147
  179.5 13.0 %collective-permute-start.24 = (bf16[512,384]{1,0:T(8,128)(2,1)}, bf16[512,384]{1,0:T(8,128)(2,1)}, u32[]{:S(2)}, u32[]{:S(2)}) collective-permute-start(bf16[512,384]{1,0:T(8,128)(2,1)} %get-tuple-element.7), channel_id=1, source_target_pairs={{11,7},{15,3},{16,28},{20,24}} | collective-permute-start | bytes 1179656 | tf_op jit(solution)/shard_map/ppermute | solution.py:147

commit v2 on v1

v2 whole, which is shorter than its diff:
```python
import functools

import jax
import jax.numpy as jnp
from jax import lax
from jax.experimental import pallas as pl
from jax.experimental.pallas import tpu as pltpu
from jax.sharding import PartitionSpec as P

BLK = 128
GROUP = 5
BOTH = ("seq", "head")
MIB = 1 << 20


def attention_kernel(slot_ref, probs_ref, old_ref, near_ref, far_ref, new_ref, held, total, old, near, far, arrived, loaded):
    blocks, heads, topk = probs_ref.shape[:3]
    values = heads // GROUP

    def copy(q, k):
        at = q * topk + k
        return pltpu.make_async_copy(probs_ref.at[q, :, k], held.at[at], arrived.at[at])

    loads = [
        pltpu.make_async_copy(source, target, loaded.at[i])
        for i, (source, target) in enumerate(((near_ref, near), (far_ref, far), (old_ref, old)))
    ]
    for load in loads:
        load.start()
    for q in range(blocks):
        for k in range(topk):

            @pl.when(slot_ref[q * topk + k] >= 0)
            def _():
                copy(q, k).start()

    for load in loads:
        load.wait()
    total[...] = old[...].astype(jnp.float32)

    @pl.loop(0, blocks)
    def _(q):
        rows = pl.ds(pl.multiple_of(q * BLK, BLK), BLK)

        @pl.loop(0, topk)
        def _(k):
            slot = slot_ref[q * topk + k]

            @pl.when(slot >= 0)
            def _():
                copy(q, k).wait()
                place = lax.shift_right_logical(slot, 1)
                change = jnp.where(lax.bitwise_and(slot, 1) == 1, far[place], near[place])
                for v in range(values):
                    weights = held[q * topk + k, v * GROUP:(v + 1) * GROUP].reshape(GROUP * BLK, BLK)
                    part = jnp.dot(weights, change[:, v * BLK:(v + 1) * BLK], preferred_element_type=jnp.float32)
                    for g in range(GROUP):
                        at = (v * GROUP + g) * BLK
                        total[rows, at:at + BLK] += part[g * BLK:(g + 1) * BLK]

    new_ref[...] = total[...].astype(jnp.bfloat16)


def refresh(slots, cached_probs, out_old, near, far):
    blocks, heads, topk = cached_probs.shape[:3]
    near = near.reshape(-1, BLK, near.shape[-1])
    far = far.reshape(-1, BLK, far.shape[-1])
    return pl.pallas_call(
        attention_kernel,
        out_shape=jax.ShapeDtypeStruct(out_old.shape, jnp.bfloat16),
        in_specs=[pl.BlockSpec(memory_space=pltpu.SMEM)] + [pl.BlockSpec(memory_space=pl.ANY)] * 4,
        out_specs=pl.BlockSpec(memory_space=pltpu.VMEM),
        scratch_shapes=[
            pltpu.VMEM((blocks * topk, heads, BLK, BLK), jnp.bfloat16),
            pltpu.VMEM(out_old.shape, jnp.float32),
            pltpu.VMEM(out_old.shape, jnp.bfloat16),
            pltpu.VMEM(near.shape, jnp.bfloat16),
            pltpu.VMEM(far.shape, jnp.bfloat16),
            pltpu.SemaphoreType.DMA((blocks * topk,)),
            pltpu.SemaphoreType.DMA((3,)),
        ],
        compiler_params=pltpu.CompilerParams(vmem_limit_bytes=56 * MIB),
        cost_estimate=pl.CostEstimate(flops=MIB, bytes_accessed=MIB, transcendentals=0),
        name="attention",
    )(slots, cached_probs, out_old, near, far)


def product_kernel(count, pick_ref, new_ref, over_ref, other_ref, *refs):
    sources, out_ref = refs[:2 * count], refs[2 * count]
    left, *rights, loaded = refs[2 * count + 1:]
    depth = new_ref.shape[1]
    halves = (slice(0, depth), slice(depth, 2 * depth))

    def load_left(i, source):
        return pltpu.make_async_copy(source, left.at[:, halves[i]], loaded.at[i])

    load_left(1, other_ref).start()

    @pl.when(pick_ref[0] == 1)
    def _():
        load_left(0, new_ref).start()

    @pl.when(pick_ref[0] == 0)
    def _():
        load_left(0, over_ref).start()

    loads = [
        pltpu.make_async_copy(sources[i], rights[i // 2].at[halves[i % 2], :], loaded.at[2 + i])
        for i in range(2 * count)
    ]
    for load in loads:
        load.start()
    load_left(0, over_ref).wait()
    load_left(1, other_ref).wait()
    column = 0
    for j in range(count):
        width = rights[j].shape[1]
        loads[2 * j].wait()
        loads[2 * j + 1].wait()
        out_ref[:, column:column + width] = jnp.dot(
            left[...], rights[j][...], preferred_element_type=jnp.float32
        ).astype(jnp.bfloat16)
        column += width


def product(pick, lefts, rights):
    rows, depth = lefts[0].shape
    width = sum(same.shape[1] for same, _ in rights)
    flat = [block for pair in rights for block in pair]
    return pl.pallas_call(
        functools.partial(product_kernel, len(rights)),
        out_shape=jax.ShapeDtypeStruct((rows, width), jnp.bfloat16),
        in_specs=[pl.BlockSpec(memory_space=pltpu.SMEM)]
        + [pl.BlockSpec(memory_space=pl.ANY)] * (len(lefts) + len(flat)),
        out_specs=pl.BlockSpec(memory_space=pltpu.VMEM),
        scratch_shapes=[pltpu.VMEM((rows, 2 * depth), jnp.bfloat16)]
        + [pltpu.VMEM((2 * depth, block.shape[1]), jnp.bfloat16) for block, _ in rights]
        + [pltpu.SemaphoreType.DMA((2 + len(flat),))],
        compiler_params=pltpu.CompilerParams(vmem_limit_bytes=56 * MIB),
        cost_estimate=pl.CostEstimate(flops=MIB, bytes_accessed=MIB, transcendentals=0),
        name="product",
    )(pick, *lefts, *flat)


def add(a, b):
    return (a.astype(jnp.float32) + b.astype(jnp.float32)).astype(jnp.bfloat16)


def slots_of(key_lists, changed_block_numbers, me):
    count = changed_block_numbers.shape[0]
    places = jnp.bitwise_xor(jnp.arange(count, dtype=jnp.int32), me)
    hit = key_lists.reshape(-1)[:, None] == changed_block_numbers[None, :]
    return jnp.max(jnp.where(hit, places[None, :], -1), axis=1)


def local_any(cached_probs, out_old, key_lists, changed_block_numbers, delta_v, w_out):
    every = lax.all_gather(delta_v, "seq", axis=0, tiled=True)
    every = every.reshape(-1, 2, BLK, every.shape[-1])
    slots = slots_of(key_lists, changed_block_numbers, jnp.int32(0))
    attn_new = refresh(slots, cached_probs, out_old, every[:, 0], every[:, 1])
    terms = jnp.dot(
        attn_new, lax.all_gather(w_out, "seq", axis=1, tiled=True), preferred_element_type=jnp.float32
    )
    out_proj = lax.psum_scatter(terms.astype(jnp.bfloat16), "head", scatter_dimension=1, tiled=True)
    return attn_new, out_proj


def move(value, where):
    pairs = []
    for z in range(4):
        for x in range(2):
            for y in range(2):
                for c in range(2):
                    to = where(z, x, y, c)
                    if to is not None:
                        tz, tx, ty, tc = to
                        pairs.append((((z * 2 + x) * 2 + y) * 2 + c, ((tz * 2 + tx) * 2 + ty) * 2 + tc))
    return lax.ppermute(value, BOTH, pairs)


def inner(z):
    return z in (1, 2)


CUTS = (384, 256)


def columns(value, cuts=CUTS):
    at, parts = 0, []
    for width in cuts:
        parts.append(value[:, at:at + width])
        at += width
    return parts


def tie(*values):
    return lax.optimization_barrier(values)


def local_line(cached_probs, out_old, key_lists, changed_block_numbers, delta_v, w_out):
    s, h = lax.axis_index("seq"), lax.axis_index("head")
    z, x, y, c = s // 2, s % 2, h // 2, h % 2
    half = z // 2
    is_inner = (z == 1) | (z == 2)

    def to_core(value):
        return move(value, lambda z, x, y, c: (z, x, y, 1 - c))

    def to_pair(value):
        return move(value, lambda z, x, y, c: (z ^ 1, x, y, c))

    def to_cross(value):
        return move(value, lambda z, x, y, c: (3 - z, x, y, c) if inner(z) else (z, x, y, 1 - c))

    def to_far_end(value):
        return move(value, lambda z, x, y, c: (z ^ 2 if inner(z) else z ^ 1, x, y, c))

    line = [move(delta_v, lambda z, x, y, c, k=k: (z ^ k, x, y, c)) for k in (1, 2, 3)]
    w_out, line = tie(w_out, line)
    near = jnp.concatenate([delta_v] + line, axis=0)
    far = move(near, lambda z, x, y, c: (z, 1 - x, y, c))
    pair, cross = to_pair(w_out), to_cross(w_out)
    cross_end = to_pair(cross)
    last = to_cross(pair)

    slots = slots_of(key_lists, changed_block_numbers, s.astype(jnp.int32))
    attn_new = refresh(slots, cached_probs, out_old, near, far)
    over_x = move(attn_new, lambda z, x, y, c: (z, 1 - x, y, c))
    other = to_core(jnp.where(x == c, over_x, attn_new))
    pick = (x == c).astype(jnp.int32).reshape(1)
    rows = [attn_new, over_x, other]

    def with_other(block):
        return block, to_core(block)

    def reduced(p_half, p_cross):
        over = move(jnp.where(y == half, p_cross, p_half), lambda z, x, y, c: (z, x, 1 - y, c))
        return add(jnp.where(y == half, p_half, p_cross), over)

    p_half = product(pick, rows, [with_other(v) for v in (w_out, pair)])
    p_own, p_pair = columns(p_half, (w_out.shape[1], w_out.shape[1]))
    parts = columns(pair)
    parts[0], p_half, last, cross_end = tie(parts[0], p_half, last, cross_end)
    block = jnp.where(is_inner, cross, cross_end)
    p_cross = product(pick, rows, [with_other(v) for v in columns(block)])
    last_end = [to_far_end(parts[0])]
    parts[1], p_cross = tie(parts[1], p_cross)
    last_end.append(to_far_end(parts[1]))
    last_end[0], p_cross = tie(last_end[0], p_cross)
    first = columns(reduced(p_own, p_cross))
    second = []
    for p_pair, inner_part, end_part in zip(columns(p_pair), columns(last), last_end, strict=True):
        if second:
            p_last, end_part = tie(p_last, end_part)
        p_last = product(pick, rows, [with_other(jnp.where(is_inner, inner_part, end_part))])
        second.append(reduced(p_pair, p_last))

    first_core = jnp.where(y == half, z % 2, half)
    out = []
    for mine, other in zip(first, second, strict=True):
        for_core = [jnp.where(first_core == j, mine, other) for j in (0, 1)]
        by_same = move(
            jnp.where(x == 0, for_core[0], for_core[1]),
            lambda z, x, y, c: (z, x, 1 - y, c) if x == c else (z, c, y, x),
        )
        by_other = move(
            jnp.where(x == 0, for_core[1], for_core[0]), lambda z, x, y, c: (z, c, y, 1 - x)
        )
        stays = jnp.where(c == 0, for_core[0], for_core[1])
        out.append((jnp.where(x == c, stays, by_same), by_other))
    left = jnp.concatenate([jnp.where(c == 0, a, b) for a, b in out], axis=1)
    right = jnp.concatenate([jnp.where(c == 0, b, a) for a, b in out], axis=1)
    return attn_new, jnp.concatenate([left, right], axis=1)


def solution(mesh):
    placed = (
        P("seq", "head", None, None, None),
        P("seq", "head"),
        P("seq", None),
        P(),
        P("seq", "head"),
        P("head", "seq"),
    )
    on_line = mesh.shape["seq"] == 8 and mesh.shape["head"] == 4
    return jax.shard_map(
        local_line if on_line else local_any,
        mesh=mesh,
        in_specs=placed,
        out_specs=(P("seq", "head"), P("seq", "head")),
        check_vma=False,
    )
```

time: 196 us -> 167 us (0.85)
  the two profiles are of different devices: /device:TPU:26 before, /device:TPU:1 now
where the time goes in v2:
time: 167 us
  waiting for transfers between devices  84.8 us (51%)
  Pallas kernels  30.7 us (18%)
  starting transfers between devices  27.8 us (17%)
  other arithmetic  13.6 us (8%)
  local copies, waits for them, and re-layouts  8.69 us (5%)
    ppermute x25, waiting for transfers between devices, move(): return lax.ppermute(value, BOTH, pairs)  84.8 us
    ppermute x25, starting transfers between devices, move(): return lax.ppermute(value, BOTH, pairs)  27.8 us
    pallas_call x4, Pallas kernels, product(): pl.pallas_call(functools.partial(product_kernel, len(rights)), out_shape=...  24.8 us
    pallas_call x1, Pallas kernels, refresh(): pl.pallas_call(attention_kernel, out_shape=jax.ShapeDtypeStruct(out_old.s...  5.93 us
    unnamed x31, local copies, waits for them, and re-layouts  4.51 us
    slice x4, local copies, waits for them, and re-layouts, columns(): parts.append(value[:, at:at + width])  3.42 us
  transfers between devices with their start and end apart: 25, of which 13 were waited for; matrix products, arithmetic and copies ran while one was open for 9% of the time, Pallas kernels for 18%

profile of v2, /device:TPU:1, one launch (start us, length us, event | category | flops | bytes accessed | tf_op | source)
XLA Modules:
  0.0 166.6 jit_solution(7503764380589911768)
XLA Ops:
  0.6 2.2 %collective-permute-start = (bf16[128,256]{1,0:T(8,128)(2,1)}, bf16[128,256]{1,0:T(8,128)(2,1)S(1)}, u32[]{:S(2)}, u32[]{:S(2)}) collective-permute-start(bf16[128,256]{1,0:T(8,128)(2,1)} %param.10), channel_id=1, source_target_pairs={{0,8},{1,9},{2,10},{3,11},{4,12},{5,13},{6,14},{7,15},{8,0},{9,1},... | collective-permute-start | bytes 196616 | tf_op jit(solution)/shard_map/ppermute | solution.py:178
  2.8 2.3 %collective-permute-start.1 = (bf16[128,256]{1,0:T(8,128)(2,1)}, bf16[128,256]{1,0:T(8,128)(2,1)S(1)}, u32[]{:S(2)}, u32[]{:S(2)}) collective-permute-start(bf16[128,256]{1,0:T(8,128)(2,1)} %param.10), channel_id=1, source_target_pairs={{0,16},{1,17},{2,18},{3,19},{4,20},{5,21},{6,22},{7,23},{8,24},{9,... | collective-permute-start | bytes 196616 | tf_op jit(solution)/shard_map/ppermute | solution.py:178
  5.1 0.9 constant_dynamic-update-slice_fusion.3
  6.0 1.6 collective-permute-done.1
  7.7 2.7 %collective-permute-done.2 = bf16[128,256]{1,0:T(8,128)(2,1)S(1)} collective-permute-done((bf16[128,256]{1,0:T(8,128)(2,1)}, bf16[128,256]{1,0:T(8,128)(2,1)S(1)}, u32[]{:S(2)}, u32[]{:S(2)}) %collective-permute-start.2) | collective-permute-done | bytes 65568 | tf_op jit(solution)/shard_map/ppermute | solution.py:178
  10.8 1.9 %collective-permute-start.10 = (bf16[1280,640]{1,0:T(8,128)(2,1)}, bf16[1280,640]{1,0:T(8,128)(2,1)}, u32[]{:S(2)}, u32[]{:S(2)}) collective-permute-start(bf16[1280,640]{1,0:T(8,128)(2,1)} %refs_0_), channel_id=1, source_target_pairs={{0,1},{1,0},{2,3},{3,2},{4,5},{5,4},{6,7},{7,6},{8,16},{9,17},{10,... | collective-permute-start | bytes 4915208 | tf_op jit(solution)/shard_map/ppermute | solution.py:178
  12.7 1.3 collective-permute-start.3
  14.8 1.3 select_reduce_fusion.slot_ref
  16.1 4.7 %collective-permute-done.3 = bf16[512,256]{1,0:T(8,128)(2,1)S(1)} collective-permute-done((bf16[512,256]{1,0:T(8,128)(2,1)S(1)}, bf16[512,256]{1,0:T(8,128)(2,1)S(1)}, u32[]{:S(2)}, u32[]{:S(2)}) %collective-permute-start.3) | collective-permute-done | bytes 262176 | tf_op jit(solution)/shard_map/ppermute | solution.py:178
  21.5 5.9 %attention.1.new_ref = bf16[512,1280]{1,0:T(8,128)(2,1)} custom-call(s32[32]{0:T(128)} %select_reduce_fusion.slot_ref, bf16[4,10,8,128,128]{4,3,2,1,0:T(8,128)(2,1)} %probs_ref.1, bf16[512,1280]{1,0:T(8,128)(2,1)} %old_ref.1, bf16[4,128,256]{2,1,0:T(8,128)(2,1)} %bitcast.3, bf16[4,128,256]{2,1,0:T(8,128)(2,1)} %bitcast.4), custom_call_target="tpu_custom_call" | custom-call | flops 1048576 | bytes 1048576 | tf_op jit(solution)/shard_map/attention/pallas_call | solution.py:68
  27.8 1.0 collective-permute-start.6
  28.8 16.9 %collective-permute-done.7.refs_2_ = bf16[1280,640]{1,0:T(8,128)(2,1)} collective-permute-done((bf16[1280,640]{1,0:T(8,128)(2,1)}, bf16[1280,640]{1,0:T(8,128)(2,1)}, u32[]{:S(2)}, u32[]{:S(2)}) %collective-permute-start.7) | collective-permute-done | bytes 1638432 | tf_op jit(solution)/shard_map/ppermute | solution.py:178
  45.6 3.2 %collective-permute-start.8 = (bf16[1280,640]{1,0:T(8,128)(2,1)}, bf16[1280,640]{1,0:T(8,128)(2,1)}, u32[]{:S(2)}, u32[]{:S(2)}) collective-permute-start(bf16[1280,640]{1,0:T(8,128)(2,1)} %collective-permute-done.7.refs_2_), channel_id=1, source_target_pairs={{0,1},{1,0},{2,3},{3,2},{4,5},{5,4},{6,7},{7,6},{8,9},{9,8},{10,11... | collective-permute-start | bytes 4915208 | tf_op jit(solution)/shard_map/ppermute | solution.py:178
  48.9 2.0 %collective-permute-start.11 = (bf16[1280,640]{1,0:T(8,128)(2,1)}, bf16[1280,640]{1,0:T(8,128)(2,1)}, u32[]{:S(2)}, u32[]{:S(2)}) collective-permute-start(bf16[1280,640]{1,0:T(8,128)(2,1)} %collective-permute-done.10), channel_id=1, source_target_pairs={{0,8},{1,9},{2,10},{3,11},{4,12},{5,13},{6,14},{7,15},{8,0},{9,1},... | collective-permute-start | bytes 4915208 | tf_op jit(solution)/shard_map/ppermute | solution.py:178
  50.9 6.5 %collective-permute-done.4.over_ref = bf16[512,1280]{1,0:T(8,128)(2,1)S(1)} collective-permute-done((bf16[512,1280]{1,0:T(8,128)(2,1)}, bf16[512,1280]{1,0:T(8,128)(2,1)S(1)}, u32[]{:S(2)}, u32[]{:S(2)}) %collective-permute-start.4) | collective-permute-done | bytes 1310752 | tf_op jit(solution)/shard_map/ppermute | solution.py:178
  57.4 3.0 %broadcast_select_fusion.1 = bf16[512,1280]{1,0:T(8,128)(2,1)} fusion(bf16[512,1280]{1,0:T(8,128)(2,1)S(1)} %collective-permute-done.4.over_ref, bf16[512,1280]{1,0:T(8,128)(2,1)} %attention.1.new_ref, pred[]{:T(512)S(6)} %eq.33), kind=kLoop, calls=%fused_computation.3 | loop fusion | flops 655360 | bytes 3932161 | tf_op jit(solution)/shard_map/jit(_where)/select_n | solution.py:229
  60.4 1.3 slice.48
  61.7 1.9 %collective-permute-done.5.other_ref = bf16[512,1280]{1,0:T(8,128)(2,1)S(1)} collective-permute-done((bf16[512,1280]{1,0:T(8,128)(2,1)}, bf16[512,1280]{1,0:T(8,128)(2,1)S(1)}, u32[]{:S(2)}, u32[]{:S(2)}) %collective-permute-start.5) | collective-permute-done | bytes 1310752 | tf_op jit(solution)/shard_map/ppermute | solution.py:178
  63.7 1.1 copy-done.1
  64.7 9.6 %product.4 = bf16[512,1280]{1,0:T(8,128)(2,1)} custom-call(s32[1]{0:T(128)} %bitcast.2.pick_ref, bf16[512,1280]{1,0:T(8,128)(2,1)} %attention.1.new_ref, bf16[512,1280]{1,0:T(8,128)(2,1)} %copy-done, bf16[512,1280]{1,0:T(8,128)(2,1)} %copy-done.1, bf16[1280,640]{1,0:T(8,128)(2,1)} %refs_0_, bf16[1280,640]{1,0:T(8,128)(2,1)} %collective-permute-done.6.refs_1_, ...), custom_call_target="tpu_custom_call" | custom-call | flops 1048576 | bytes 1048576 | tf_op jit(solution)/shard_map/product/pallas_call | solution.py:130
  74.4 12.8 %collective-permute-done.11 = bf16[1280,640]{1,0:T(8,128)(2,1)} collective-permute-done((bf16[1280,640]{1,0:T(8,128)(2,1)}, bf16[1280,640]{1,0:T(8,128)(2,1)}, u32[]{:S(2)}, u32[]{:S(2)}) %collective-permute-start.11) | collective-permute-done | bytes 1638432 | tf_op jit(solution)/shard_map/ppermute | solution.py:178
  87.2 1.6 broadcast_select_fusion
  89.8 1.5 collective-permute-start.12
  91.7 2.0 %slice.49 = bf16[1280,256]{1,0:T(8,128)(2,1)} slice(bf16[1280,640]{1,0:T(8,128)(2,1)} %collective-permute-done.7.refs_2_), slice={[0:1280], [384:640]} | slice | bytes 1310720 | tf_op jit(solution)/shard_map/slice | solution.py:191
  94.5 1.0 copy-done.10
  95.5 6.9 %product.5 = bf16[512,640]{1,0:T(8,128)(2,1)} custom-call(s32[1]{0:T(128)} %bitcast.2.pick_ref, bf16[512,1280]{1,0:T(8,128)(2,1)} %attention.1.new_ref, bf16[512,1280]{1,0:T(8,128)(2,1)} %copy-done, bf16[512,1280]{1,0:T(8,128)(2,1)} %copy-done.1, bf16[1280,384]{1,0:T(8,128)(2,1)} %copy-done.5, bf16[1280,384]{1,0:T(8,128)(2,1)} %copy-done.10, ...), custom_call_target="tpu_custom_call" | custom-call | flops 1048576 | bytes 1048576 | tf_op jit(solution)/shard_map/product/pallas_call | solution.py:130
  102.4 11.6 %collective-permute-done.12 = bf16[1280,384]{1,0:T(8,128)(2,1)S(1)} collective-permute-done((bf16[1280,384]{1,0:T(8,128)(2,1)S(1)}, bf16[1280,384]{1,0:T(8,128)(2,1)S(1)}, u32[]{:S(2)}, u32[]{:S(2)}) %collective-permute-start.12) | collective-permute-done | bytes 983072 | tf_op jit(solution)/shard_map/ppermute | solution.py:178
  114.0 1.3 slice_select_fusion.refs_0_
  115.3 0.9 collective-permute-start.16
  116.8 0.9 broadcast_select_fusion.2
  117.7 1.2 collective-permute-start.15
  119.0 4.6 %product.6 = bf16[512,384]{1,0:T(8,128)(2,1)} custom-call(s32[1]{0:T(128)} %bitcast.2.pick_ref, bf16[512,1280]{1,0:T(8,128)(2,1)} %attention.1.new_ref, bf16[512,1280]{1,0:T(8,128)(2,1)} %copy-done, bf16[512,1280]{1,0:T(8,128)(2,1)} %copy-done.1, bf16[1280,384]{1,0:T(8,128)(2,1)} %copy-done.4, bf16[1280,384]{1,0:T(8,128)(2,1)} %collective-permute-done.16.refs_1_), custom_call_target="tpu_custom_call" | custom-call | flops 1048576 | bytes 1048576 | tf_op jit(solution)/shard_map/product/pallas_call | solution.py:130
  123.6 10.2 %collective-permute-done.20 = bf16[1280,256]{1,0:T(8,128)(2,1)} collective-permute-done((bf16[1280,256]{1,0:T(8,128)(2,1)}, bf16[1280,256]{1,0:T(8,128)(2,1)}, u32[]{:S(2)}, u32[]{:S(2)}) %collective-permute-start.20) | collective-permute-done | bytes 655392 | tf_op jit(solution)/shard_map/ppermute | solution.py:178
  133.7 1.4 slice_select_fusion.1.refs_0_
  135.1 0.9 collective-permute-start.21
  136.1 1.3 collective-permute-start.17
  137.4 1.3 add_convert_fusion
  138.8 3.7 %product.7 = bf16[512,256]{1,0:T(8,128)(2,1)} custom-call(s32[1]{0:T(128)} %bitcast.2.pick_ref, bf16[512,1280]{1,0:T(8,128)(2,1)} %attention.1.new_ref, bf16[512,1280]{1,0:T(8,128)(2,1)} %copy-done, bf16[512,1280]{1,0:T(8,128)(2,1)} %copy-done.1, bf16[1280,256]{1,0:T(8,128)(2,1)} %copy-done.7, bf16[1280,256]{1,0:T(8,128)(2,1)} %collective-permute-done.21.refs_1_), custom_call_target="tpu_custom_call" | custom-call | flops 1048576 | bytes 1048576 | tf_op jit(solution)/shard_map/product/pallas_call | solution.py:130
  142.4 1.0 broadcast_select_fusion.13
  143.5 3.3 %collective-permute-done.17 = bf16[512,384]{1,0:T(8,128)(2,1)S(1)} collective-permute-done((bf16[512,384]{1,0:T(8,128)(2,1)S(1)}, bf16[512,384]{1,0:T(8,128)(2,1)S(1)}, u32[]{:S(2)}, u32[]{:S(2)}) %collective-permute-start.17) | collective-permute-done | bytes 393248 | tf_op jit(solution)/shard_map/ppermute | solution.py:178
  147.1 1.2 collective-permute-start.19
  148.3 1.7 %collective-permute-start.18 = (bf16[512,384]{1,0:T(8,128)(2,1)S(1)}, bf16[512,384]{1,0:T(8,128)(2,1)S(1)}, u32[]{:S(2)}, u32[]{:S(2)}) collective-permute-start(bf16[512,384]{1,0:T(8,128)(2,1)S(1)} %get-tuple-element.26), channel_id=1, source_target_pairs={{0,2},{1,4},{2,0},{3,6},{4,1},{5,7},{6,3},{7,5},{8,10},{9,12},{10,... | collective-permute-start | bytes 1179656 | tf_op jit(solution)/shard_map/ppermute | solution.py:178
  150.1 2.4 %collective-permute-done.22 = bf16[512,256]{1,0:T(8,128)(2,1)S(1)} collective-permute-done((bf16[512,256]{1,0:T(8,128)(2,1)S(1)}, bf16[512,256]{1,0:T(8,128)(2,1)S(1)}, u32[]{:S(2)}, u32[]{:S(2)}) %collective-permute-start.22) | collective-permute-done | bytes 262176 | tf_op jit(solution)/shard_map/ppermute | solution.py:178
  152.6 1.2 collective-permute-start.24
  153.8 1.3 collective-permute-start.23
  155.1 4.8 %collective-permute-done.18 = bf16[512,384]{1,0:T(8,128)(2,1)S(1)} collective-permute-done((bf16[512,384]{1,0:T(8,128)(2,1)S(1)}, bf16[512,384]{1,0:T(8,128)(2,1)S(1)}, u32[]{:S(2)}, u32[]{:S(2)}) %collective-permute-start.18) | collective-permute-done | bytes 393248 | tf_op jit(solution)/shard_map/ppermute | solution.py:178
  160.1 5.3 %collective-permute-done.23 = bf16[512,256]{1,0:T(8,128)(2,1)S(1)} collective-permute-done((bf16[512,256]{1,0:T(8,128)(2,1)S(1)}, bf16[512,256]{1,0:T(8,128)(2,1)S(1)}, u32[]{:S(2)}, u32[]{:S(2)}) %collective-permute-start.23) | collective-permute-done | bytes 262176 | tf_op jit(solution)/shard_map/ppermute | solution.py:178
  165.4 1.2 pad_maximum_fusion
  (61 shorter events, 5.8 us)
Async XLA Ops:
  0.6 5.4 %collective-permute-start = (bf16[128,256]{1,0:T(8,128)(2,1)}, bf16[128,256]{1,0:T(8,128)(2,1)S(1)}, u32[]{:S(2)}, u32[]{:S(2)}) collective-permute-start(bf16[128,256]{1,0:T(8,128)(2,1)} %param.10), channel_id=1, source_target_pairs={{0,8},{1,9},{2,10},{3,11},{4,12},{5,13},{6,14},{7,15},{8,0},{9,1},... | collective-permute-start | bytes 196616 | tf_op jit(solution)/shard_map/ppermute | solution.py:178
  2.8 4.9 %collective-permute-start.1 = (bf16[128,256]{1,0:T(8,128)(2,1)}, bf16[128,256]{1,0:T(8,128)(2,1)S(1)}, u32[]{:S(2)}, u32[]{:S(2)}) collective-permute-start(bf16[128,256]{1,0:T(8,128)(2,1)} %param.10), channel_id=1, source_target_pairs={{0,16},{1,17},{2,18},{3,19},{4,20},{5,21},{6,22},{7,23},{8,24},{9,... | collective-permute-start | bytes 196616 | tf_op jit(solution)/shard_map/ppermute | solution.py:178
  5.1 5.2 %collective-permute-start.2 = (bf16[128,256]{1,0:T(8,128)(2,1)}, bf16[128,256]{1,0:T(8,128)(2,1)S(1)}, u32[]{:S(2)}, u32[]{:S(2)}) collective-permute-start(bf16[128,256]{1,0:T(8,128)(2,1)} %param.10), channel_id=1, source_target_pairs={{0,24},{1,25},{2,26},{3,27},{4,28},{5,29},{6,30},{7,31},{8,16},{9,... | collective-permute-start | bytes 196616 | tf_op jit(solution)/shard_map/ppermute | solution.py:178
  10.4 35.3 %collective-permute-start.7 = (bf16[1280,640]{1,0:T(8,128)(2,1)}, bf16[1280,640]{1,0:T(8,128)(2,1)}, u32[]{:S(2)}, u32[]{:S(2)}) collective-permute-start(bf16[1280,640]{1,0:T(8,128)(2,1)} %refs_0_), channel_id=1, source_target_pairs={{0,8},{1,9},{2,10},{3,11},{4,12},{5,13},{6,14},{7,15},{8,0},{9,1},... | collective-permute-start | bytes 4915208 | tf_op jit(solution)/shard_map/ppermute | solution.py:178
  10.8 38.1 %collective-permute-start.10 = (bf16[1280,640]{1,0:T(8,128)(2,1)}, bf16[1280,640]{1,0:T(8,128)(2,1)}, u32[]{:S(2)}, u32[]{:S(2)}) collective-permute-start(bf16[1280,640]{1,0:T(8,128)(2,1)} %refs_0_), channel_id=1, source_target_pairs={{0,1},{1,0},{2,3},{3,2},{4,5},{5,4},{6,7},{7,6},{8,16},{9,17},{10,... | collective-permute-start | bytes 4915208 | tf_op jit(solution)/shard_map/ppermute | solution.py:178
  12.7 8.1 %copy-start.12 = (bf16[512,256]{1,0:T(8,128)(2,1)}, bf16[512,256]{1,0:T(8,128)(2,1)S(1)}, u32[]{:S(2)}) copy-start(bf16[512,256]{1,0:T(8,128)(2,1)S(1)} %constant_dynamic-update-slice_fusion) | copy-start | bytes 786436
  12.7 8.1 %collective-permute-start.3 = (bf16[512,256]{1,0:T(8,128)(2,1)S(1)}, bf16[512,256]{1,0:T(8,128)(2,1)S(1)}, u32[]{:S(2)}, u32[]{:S(2)}) collective-permute-start(bf16[512,256]{1,0:T(8,128)(2,1)S(1)} %constant_dynamic-update-slice_fusion), channel_id=1, source_target_pairs={{0,4},{1,5},{2,6},{3,7},{4,0},{5,1},{6,2},{7,3},{8,12},{9,13},{10,... | collective-permute-start | bytes 786440 | tf_op jit(solution)/shard_map/ppermute | solution.py:178
  20.8 0.7 copy-start.13
  27.5 30.0 %collective-permute-start.4 = (bf16[512,1280]{1,0:T(8,128)(2,1)}, bf16[512,1280]{1,0:T(8,128)(2,1)S(1)}, u32[]{:S(2)}, u32[]{:S(2)}) collective-permute-start(bf16[512,1280]{1,0:T(8,128)(2,1)} %attention.1.new_ref), channel_id=1, source_target_pairs={{0,4},{1,5},{2,6},{3,7},{4,0},{5,1},{6,2},{7,3},{8,12},{9,13},{10,... | collective-permute-start | bytes 3932168 | tf_op jit(solution)/shard_map/ppermute | solution.py:178
  27.8 34.0 %collective-permute-start.6 = (bf16[1280,640]{1,0:T(8,128)(2,1)}, bf16[1280,640]{1,0:T(8,128)(2,1)}, u32[]{:S(2)}, u32[]{:S(2)}) collective-permute-start(bf16[1280,640]{1,0:T(8,128)(2,1)} %refs_0_), channel_id=1, source_target_pairs={{0,1},{1,0},{2,3},{3,2},{4,5},{5,4},{6,7},{7,6},{8,9},{9,8},{10,11... | collective-permute-start | bytes 4915208 | tf_op jit(solution)/shard_map/ppermute | solution.py:178
  45.6 18.0 %collective-permute-start.8 = (bf16[1280,640]{1,0:T(8,128)(2,1)}, bf16[1280,640]{1,0:T(8,128)(2,1)}, u32[]{:S(2)}, u32[]{:S(2)}) collective-permute-start(bf16[1280,640]{1,0:T(8,128)(2,1)} %collective-permute-done.7.refs_2_), channel_id=1, source_target_pairs={{0,1},{1,0},{2,3},{3,2},{4,5},{5,4},{6,7},{7,6},{8,9},{9,8},{10,11... | collective-permute-start | bytes 4915208 | tf_op jit(solution)/shard_map/ppermute | solution.py:178
  48.9 25.5 %collective-permute-start.9 = (bf16[1280,640]{1,0:T(8,128)(2,1)}, bf16[1280,640]{1,0:T(8,128)(2,1)}, u32[]{:S(2)}, u32[]{:S(2)}) collective-permute-start(bf16[1280,640]{1,0:T(8,128)(2,1)} %collective-permute-done.7.refs_2_), channel_id=1, source_target_pairs={{0,1},{1,0},{2,3},{3,2},{4,5},{5,4},{6,7},{7,6},{8,16},{9,17},{10,... | collective-permute-start | bytes 4915208 | tf_op jit(solution)/shard_map/ppermute | solution.py:178
  48.9 38.3 %collective-permute-start.11 = (bf16[1280,640]{1,0:T(8,128)(2,1)}, bf16[1280,640]{1,0:T(8,128)(2,1)}, u32[]{:S(2)}, u32[]{:S(2)}) collective-permute-start(bf16[1280,640]{1,0:T(8,128)(2,1)} %collective-permute-done.10), channel_id=1, source_target_pairs={{0,8},{1,9},{2,10},{3,11},{4,12},{5,13},{6,14},{7,15},{8,0},{9,1},... | collective-permute-start | bytes 4915208 | tf_op jit(solution)/shard_map/ppermute | solution.py:178
  57.4 3.0 %copy-start = (bf16[512,1280]{1,0:T(8,128)(2,1)}, bf16[512,1280]{1,0:T(8,128)(2,1)S(1)}, u32[]{:S(2)}) copy-start(bf16[512,1280]{1,0:T(8,128)(2,1)S(1)} %collective-permute-done.4.over_ref) | copy-start | bytes 3932164
  60.4 3.2 %collective-permute-start.5 = (bf16[512,1280]{1,0:T(8,128)(2,1)}, bf16[512,1280]{1,0:T(8,128)(2,1)S(1)}, u32[]{:S(2)}, u32[]{:S(2)}) collective-permute-start(bf16[512,1280]{1,0:T(8,128)(2,1)} %broadcast_select_fusion.1), channel_id=1, source_target_pairs={{0,1},{1,0},{2,3},{3,2},{4,5},{5,4},{6,7},{7,6},{8,9},{9,8},{10,11... | collective-permute-start | bytes 3932168 | tf_op jit(solution)/shard_map/ppermute | solution.py:178
  63.7 1.1 copy-start.1
  88.9 4.8 %copy-start.5 = (bf16[1280,384]{1,0:T(8,128)(2,1)}, bf16[1280,384]{1,0:T(8,128)(2,1)S(1)}, u32[]{:S(2)}) copy-start(bf16[1280,384]{1,0:T(8,128)(2,1)S(1)} %slice.50.refs_0_) | copy-start | bytes 2949124
  88.9 4.8 %collective-permute-start.13 = (bf16[1280,384]{1,0:T(8,128)(2,1)S(1)}, bf16[1280,384]{1,0:T(8,128)(2,1)S(1)}, u32[]{:S(2)}, u32[]{:S(2)}) collective-permute-start(bf16[1280,384]{1,0:T(8,128)(2,1)S(1)} %slice.50.refs_0_), channel_id=1, source_target_pairs={{0,1},{1,0},{2,3},{3,2},{4,5},{5,4},{6,7},{7,6},{8,9},{9,8},{10,11... | collective-permute-start | bytes 2949128 | tf_op jit(solution)/shard_map/ppermute | solution.py:178
  89.8 24.2 %collective-permute-start.12 = (bf16[1280,384]{1,0:T(8,128)(2,1)S(1)}, bf16[1280,384]{1,0:T(8,128)(2,1)S(1)}, u32[]{:S(2)}, u32[]{:S(2)}) collective-permute-start(bf16[1280,384]{1,0:T(8,128)(2,1)S(1)} %slice.48), channel_id=1, source_target_pairs={{0,8},{1,9},{2,10},{3,11},{4,12},{5,13},{6,14},{7,15},{8,24},{9,25... | collective-permute-start | bytes 2949128 | tf_op jit(solution)/shard_map/ppermute | solution.py:178
  91.3 2.4 %copy-start.8 = (bf16[1280,256]{1,0:T(8,128)(2,1)}, bf16[1280,256]{1,0:T(8,128)(2,1)S(1)}, u32[]{:S(2)}) copy-start(bf16[1280,256]{1,0:T(8,128)(2,1)S(1)} %slice.51.refs_2_) | copy-start | bytes 1966084
  91.3 2.4 %collective-permute-start.14 = (bf16[1280,256]{1,0:T(8,128)(2,1)S(1)}, bf16[1280,256]{1,0:T(8,128)(2,1)S(1)}, u32[]{:S(2)}, u32[]{:S(2)}) collective-permute-start(bf16[1280,256]{1,0:T(8,128)(2,1)S(1)} %slice.51.refs_2_), channel_id=1, source_target_pairs={{0,1},{1,0},{2,3},{3,2},{4,5},{5,4},{6,7},{7,6},{8,9},{9,8},{10,11... | collective-permute-start | bytes 1966088 | tf_op jit(solution)/shard_map/ppermute | solution.py:178
  93.7 0.8 copy-start.11
  94.5 1.0 copy-start.10
  102.4 14.4 %copy-start.2 = (bf16[512,1280]{1,0:T(8,128)(2,1)S(1)}, bf16[512,1280]{1,0:T(8,128)(2,1)}, u32[]{:S(2)}) copy-start(bf16[512,1280]{1,0:T(8,128)(2,1)} %product.4) | copy-start | bytes 3932164
  102.4 14.4 %copy-start.3 = (bf16[512,640]{1,0:T(8,128)(2,1)S(1)}, bf16[512,640]{1,0:T(8,128)(2,1)}, u32[]{:S(2)}) copy-start(bf16[512,640]{1,0:T(8,128)(2,1)} %product.5) | copy-start | bytes 1966084
  115.3 3.7 %copy-start.4 = (bf16[1280,384]{1,0:T(8,128)(2,1)}, bf16[1280,384]{1,0:T(8,128)(2,1)S(1)}, u32[]{:S(2)}) copy-start(bf16[1280,384]{1,0:T(8,128)(2,1)S(1)} %slice_select_fusion.refs_0_) | copy-start | bytes 2949124
  115.3 3.6 %collective-permute-start.16 = (bf16[1280,384]{1,0:T(8,128)(2,1)S(1)}, bf16[1280,384]{1,0:T(8,128)(2,1)}, u32[]{:S(2)}, u32[]{:S(2)}) collective-permute-start(bf16[1280,384]{1,0:T(8,128)(2,1)S(1)} %slice_select_fusion.refs_0_), channel_id=1, source_target_pairs={{0,1},{1,0},{2,3},{3,2},{4,5},{5,4},{6,7},{7,6},{8,9},{9,8},{10,11... | collective-permute-start | bytes 2949128 | tf_op jit(solution)/shard_map/ppermute | solution.py:178
  116.2 17.5 %collective-permute-start.20 = (bf16[1280,256]{1,0:T(8,128)(2,1)}, bf16[1280,256]{1,0:T(8,128)(2,1)}, u32[]{:S(2)}, u32[]{:S(2)}) collective-permute-start(bf16[1280,256]{1,0:T(8,128)(2,1)} %slice.49), channel_id=1, source_target_pairs={{0,8},{1,9},{2,10},{3,11},{4,12},{5,13},{6,14},{7,15},{8,24},{9,25... | collective-permute-start | bytes 1966088 | tf_op jit(solution)/shard_map/ppermute | solution.py:178
  117.7 19.7 %collective-permute-start.15 = (bf16[512,640]{1,0:T(8,128)(2,1)}, bf16[512,640]{1,0:T(8,128)(2,1)}, u32[]{:S(2)}, u32[]{:S(2)}) collective-permute-start(bf16[512,640]{1,0:T(8,128)(2,1)} %broadcast_select_fusion.2), channel_id=1, source_target_pairs={{0,2},{1,3},{2,0},{3,1},{4,6},{5,7},{6,4},{7,5},{8,10},{9,11},{10,... | collective-permute-start | bytes 1966088 | tf_op jit(solution)/shard_map/ppermute | solution.py:178
  123.6 12.5 %copy-start.6 = (bf16[512,384]{1,0:T(8,128)(2,1)S(1)}, bf16[512,384]{1,0:T(8,128)(2,1)}, u32[]{:S(2)}) copy-start(bf16[512,384]{1,0:T(8,128)(2,1)} %product.6) | copy-start | bytes 1179652
  135.1 3.6 %copy-start.7 = (bf16[1280,256]{1,0:T(8,128)(2,1)}, bf16[1280,256]{1,0:T(8,128)(2,1)S(1)}, u32[]{:S(2)}) copy-start(bf16[1280,256]{1,0:T(8,128)(2,1)S(1)} %slice_select_fusion.1.refs_0_) | copy-start | bytes 1966084
  135.1 3.6 %collective-permute-start.21 = (bf16[1280,256]{1,0:T(8,128)(2,1)S(1)}, bf16[1280,256]{1,0:T(8,128)(2,1)}, u32[]{:S(2)}, u32[]{:S(2)}) collective-permute-start(bf16[1280,256]{1,0:T(8,128)(2,1)S(1)} %slice_select_fusion.1.refs_0_), channel_id=1, source_target_pairs={{0,1},{1,0},{2,3},{3,2},{4,5},{5,4},{6,7},{7,6},{8,9},{9,8},{10,11... | collective-permute-start | bytes 1966088 | tf_op jit(solution)/shard_map/ppermute | solution.py:178
  136.1 10.8 %collective-permute-start.17 = (bf16[512,384]{1,0:T(8,128)(2,1)S(1)}, bf16[512,384]{1,0:T(8,128)(2,1)S(1)}, u32[]{:S(2)}, u32[]{:S(2)}) collective-permute-start(bf16[512,384]{1,0:T(8,128)(2,1)S(1)} %broadcast_select_fusion.6), channel_id=1, source_target_pairs={{0,2},{1,3},{2,0},{3,1},{4,6},{5,7},{6,4},{7,5},{8,10},{9,11},{10,... | collective-permute-start | bytes 1179656 | tf_op jit(solution)/shard_map/ppermute | solution.py:178
  143.4 9.0 %copy-start.9 = (bf16[512,256]{1,0:T(8,128)(2,1)S(1)}, bf16[512,256]{1,0:T(8,128)(2,1)}, u32[]{:S(2)}) copy-start(bf16[512,256]{1,0:T(8,128)(2,1)} %product.7) | copy-start | bytes 786436
  143.4 9.0 %collective-permute-start.22 = (bf16[512,256]{1,0:T(8,128)(2,1)S(1)}, bf16[512,256]{1,0:T(8,128)(2,1)S(1)}, u32[]{:S(2)}, u32[]{:S(2)}) collective-permute-start(bf16[512,256]{1,0:T(8,128)(2,1)S(1)} %broadcast_select_fusion.13), channel_id=1, source_target_pairs={{0,2},{1,3},{2,0},{3,1},{4,6},{5,7},{6,4},{7,5},{8,10},{9,11},{10,... | collective-permute-start | bytes 786440 | tf_op jit(solution)/shard_map/ppermute | solution.py:178
  147.1 8.0 %collective-permute-start.19 = (bf16[512,384]{1,0:T(8,128)(2,1)S(1)}, bf16[512,384]{1,0:T(8,128)(2,1)S(1)}, u32[]{:S(2)}, u32[]{:S(2)}) collective-permute-start(bf16[512,384]{1,0:T(8,128)(2,1)S(1)} %broadcast_select_fusion.3), channel_id=1, source_target_pairs={{0,1},{1,5},{2,3},{3,7},{4,0},{5,4},{6,2},{7,6},{8,9},{9,13},{10,1... | collective-permute-start | bytes 1179656 | tf_op jit(solution)/shard_map/ppermute | solution.py:178
  148.3 11.6 %collective-permute-start.18 = (bf16[512,384]{1,0:T(8,128)(2,1)S(1)}, bf16[512,384]{1,0:T(8,128)(2,1)S(1)}, u32[]{:S(2)}, u32[]{:S(2)}) collective-permute-start(bf16[512,384]{1,0:T(8,128)(2,1)S(1)} %get-tuple-element.26), channel_id=1, source_target_pairs={{0,2},{1,4},{2,0},{3,6},{4,1},{5,7},{6,3},{7,5},{8,10},{9,12},{10,... | collective-permute-start | bytes 1179656 | tf_op jit(solution)/shard_map/ppermute | solution.py:178
  152.6 7.5 %collective-permute-start.24 = (bf16[512,256]{1,0:T(8,128)(2,1)S(1)}, bf16[512,256]{1,0:T(8,128)(2,1)S(1)}, u32[]{:S(2)}, u32[]{:S(2)}) collective-permute-start(bf16[512,256]{1,0:T(8,128)(2,1)S(1)} %broadcast_select_fusion.10), channel_id=1, source_target_pairs={{0,1},{1,5},{2,3},{3,7},{4,0},{5,4},{6,2},{7,6},{8,9},{9,13},{10,1... | collective-permute-start | bytes 786440 | tf_op jit(solution)/shard_map/ppermute | solution.py:178
  153.8 11.5 %collective-permute-start.23 = (bf16[512,256]{1,0:T(8,128)(2,1)S(1)}, bf16[512,256]{1,0:T(8,128)(2,1)S(1)}, u32[]{:S(2)}, u32[]{:S(2)}) collective-permute-start(bf16[512,256]{1,0:T(8,128)(2,1)S(1)} %get-tuple-element.29), channel_id=1, source_target_pairs={{0,2},{1,4},{2,0},{3,6},{4,1},{5,7},{6,3},{7,5},{8,10},{9,12},{10,... | collective-permute-start | bytes 786440 | tf_op jit(solution)/shard_map/ppermute | solution.py:178

commit v3 on v2

--- a/solution.py
+++ b/solution.py
@@ -86,8 +86,7 @@
 
 
 def product_kernel(count, pick_ref, new_ref, over_ref, other_ref, *refs):
-    sources, out_ref = refs[:2 * count], refs[2 * count]
-    left, *rights, loaded = refs[2 * count + 1:]
+    sources, out_ref, left, right, loaded = refs[:2 * count], *refs[2 * count:]
     depth = new_ref.shape[1]
     halves = (slice(0, depth), slice(depth, 2 * depth))
 
@@ -104,23 +103,19 @@
     def _():
         load_left(0, over_ref).start()
 
-    loads = [
-        pltpu.make_async_copy(sources[i], rights[i // 2].at[halves[i % 2], :], loaded.at[2 + i])
-        for i in range(2 * count)
-    ]
-    for load in loads:
-        load.start()
+    loads, column = [], 0
+    for j in range(count):
+        width = sources[2 * j].shape[1]
+        for i in (0, 1):
+            target = right.at[halves[i], column:column + width]
+            loads.append(pltpu.make_async_copy(sources[2 * j + i], target, loaded.at[2 + 2 * j + i]))
+            loads[-1].start()
+        column += width
     load_left(0, over_ref).wait()
     load_left(1, other_ref).wait()
-    column = 0
-    for j in range(count):
-        width = rights[j].shape[1]
-        loads[2 * j].wait()
-        loads[2 * j + 1].wait()
-        out_ref[:, column:column + width] = jnp.dot(
-            left[...], rights[j][...], preferred_element_type=jnp.float32
-        ).astype(jnp.bfloat16)
-        column += width
+    for load in loads:
+        load.wait()
+    out_ref[...] = jnp.dot(left[...], right[...], preferred_element_type=jnp.float32).astype(jnp.bfloat16)
 
 
 def product(pick, lefts, rights):
@@ -133,9 +128,11 @@
         in_specs=[pl.BlockSpec(memory_space=pltpu.SMEM)]
         + [pl.BlockSpec(memory_space=pl.ANY)] * (len(lefts) + len(flat)),
         out_specs=pl.BlockSpec(memory_space=pltpu.VMEM),
-        scratch_shapes=[pltpu.VMEM((rows, 2 * depth), jnp.bfloat16)]
-        + [pltpu.VMEM((2 * depth, block.shape[1]), jnp.bfloat16) for block, _ in rights]
-        + [pltpu.SemaphoreType.DMA((2 + len(flat),))],
+        scratch_shapes=[
+            pltpu.VMEM((rows, 2 * depth), jnp.bfloat16),
+            pltpu.VMEM((2 * depth, width), jnp.bfloat16),
+            pltpu.SemaphoreType.DMA((2 + len(flat),)),
+        ],
         compiler_params=pltpu.CompilerParams(vmem_limit_bytes=56 * MIB),
         cost_estimate=pl.CostEstimate(flops=MIB, bytes_accessed=MIB, transcendentals=0),
         name="product",
@@ -193,6 +190,10 @@
     return parts
 
 
+def narrow(value):
+    return columns(value, [BLK] * (value.shape[1] // BLK))
+
+
 def tie(*values):
     return lax.optimization_barrier(values)
 
@@ -216,7 +217,6 @@
         return move(value, lambda z, x, y, c: (z ^ 2 if inner(z) else z ^ 1, x, y, c))
 
     line = [move(delta_v, lambda z, x, y, c, k=k: (z ^ k, x, y, c)) for k in (1, 2, 3)]
-    w_out, line = tie(w_out, line)
     near = jnp.concatenate([delta_v] + line, axis=0)
     far = move(near, lambda z, x, y, c: (z, 1 - x, y, c))
     pair, cross = to_pair(w_out), to_cross(w_out)
@@ -233,9 +233,11 @@
     def with_other(block):
         return block, to_core(block)
 
-    def reduced(p_half, p_cross):
-        over = move(jnp.where(y == half, p_cross, p_half), lambda z, x, y, c: (z, x, 1 - y, c))
-        return add(jnp.where(y == half, p_half, p_cross), over)
+    def to_sum(p_half, p_cross):
+        return jnp.where(y == half, p_cross, p_half), jnp.where(y == half, p_half, p_cross)
+
+    def summed(sent, kept):
+        return add(kept, move(sent, lambda z, x, y, c: (z, x, 1 - y, c)))
 
     p_half = product(pick, rows, [with_other(v) for v in (w_out, pair)])
     p_own, p_pair = columns(p_half, (w_out.shape[1], w_out.shape[1]))
@@ -244,16 +246,20 @@
     block = jnp.where(is_inner, cross, cross_end)
     p_cross = product(pick, rows, [with_other(v) for v in columns(block)])
     last_end = [to_far_end(parts[0])]
-    parts[1], p_cross = tie(parts[1], p_cross)
+    parts[1], block = tie(parts[1], block)
     last_end.append(to_far_end(parts[1]))
-    last_end[0], p_cross = tie(last_end[0], p_cross)
-    first = columns(reduced(p_own, p_cross))
-    second = []
+    first = summed(*to_sum(p_own, p_cross))
+    last_end[0], first = tie(last_end[0], first)
+    first = columns(first)
+    second, terms = [], None
     for p_pair, inner_part, end_part in zip(columns(p_pair), columns(last), last_end, strict=True):
-        if second:
-            p_last, end_part = tie(p_last, end_part)
-        p_last = product(pick, rows, [with_other(jnp.where(is_inner, inner_part, end_part))])
-        second.append(reduced(p_pair, p_last))
+        if terms:
+            *terms, end_part = tie(*terms, end_part)
+            second.append(summed(*terms))
+        pieces = [jnp.where(is_inner, *v) for v in zip(narrow(inner_part), narrow(end_part), strict=True)]
+        p_last = product(pick, rows, [with_other(v) for v in pieces])
+        terms = to_sum(p_pair, p_last)
+    second.append(summed(*terms))
 
     first_core = jnp.where(y == half, z % 2, half)
     out = []

time: 167 us -> 159 us (0.952)
  waiting for transfers between devices: 84.8 us -> 71.1 us
  starting transfers between devices: 27.8 us -> 33.8 us
    ppermute x25 -> x28, waiting for transfers between devices: 84.8 us -> 71.1 us  [move(): return lax.ppermute(value, BOTH, pairs)]
    ppermute x25 -> x28, starting transfers between devices: 27.8 us -> 33.8 us  [move(): return lax.ppermute(value, BOTH, pairs)]
    pallas_call x4, Pallas kernels: 24.8 us -> 22.4 us  [product(): pl.pallas_call(functools.partial(product_kernel, len(rights)), out_shape=...]
    pallas_call x1, Pallas kernels: 5.93 us -> 7.89 us  [refresh(): pl.pallas_call(attention_kernel, out_shape=jax.ShapeDtypeStruct(out_old.s...]
    select_n x5, other arithmetic: 4.63 us -> 6.5 us  [the longest x2 2.45 us: local_line(): jnp.where(is_inner, *v)]
    unnamed x31 -> x37, local copies, waits for them, and re-layouts: 4.51 us -> 3.68 us
  transfers between devices with their start and end apart: 25 -> 28, of which waited for: 13 -> 17; matrix products, arithmetic and copies ran while one was open for 9% -> 10% of each run, Pallas kernels for 18% -> 19%
where the time goes in v3:
time: 159 us
  waiting for transfers between devices  71.1 us (45%)
  starting transfers between devices  33.8 us (21%)
  Pallas kernels  30.3 us (19%)
  other arithmetic  14.4 us (9%)
  local copies, waits for them, and re-layouts  7.96 us (5%)
    ppermute x28, waiting for transfers between devices, move(): return lax.ppermute(value, BOTH, pairs)  71.1 us
    ppermute x28, starting transfers between devices, move(): return lax.ppermute(value, BOTH, pairs)  33.8 us
    pallas_call x4, Pallas kernels, product(): pl.pallas_call(functools.partial(product_kernel, len(rights)), out_shape=...  22.4 us
    pallas_call x1, Pallas kernels, refresh(): pl.pallas_call(attention_kernel, out_shape=jax.ShapeDtypeStruct(out_old.s...  7.89 us
    unnamed x37, local copies, waits for them, and re-layouts  3.68 us
    slice x4, local copies, waits for them, and re-layouts, columns(): parts.append(value[:, at:at + width])  3.51 us
  transfers between devices with their start and end apart: 28, of which 17 were waited for; matrix products, arithmetic and copies ran while one was open for 10% of the time, Pallas kernels for 19%

profile of v3, /device:TPU:1, one launch (start us, length us, event | category | flops | bytes accessed | tf_op | source)
XLA Modules:
  0.0 158.5 jit_solution(1244924440972796255)
XLA Ops:
  0.6 3.2 %collective-permute-start.1 = (bf16[128,256]{1,0:T(8,128)(2,1)}, bf16[128,256]{1,0:T(8,128)(2,1)S(1)}, u32[]{:S(2)}, u32[]{:S(2)}) collective-permute-start(bf16[128,256]{1,0:T(8,128)(2,1)} %param.10), channel_id=1, source_target_pairs={{0,16},{1,17},{2,18},{3,19},{4,20},{5,21},{6,22},{7,23},{8,24},{9,... | collective-permute-start | bytes 196616 | tf_op jit(solution)/shard_map/ppermute | solution.py:175
  3.8 1.3 collective-permute-start
  5.5 1.8 %collective-permute-start.10 = (bf16[1280,640]{1,0:T(8,128)(2,1)}, bf16[1280,640]{1,0:T(8,128)(2,1)}, u32[]{:S(2)}, u32[]{:S(2)}) collective-permute-start(bf16[1280,640]{1,0:T(8,128)(2,1)} %refs_0_.1), channel_id=1, source_target_pairs={{0,1},{1,0},{2,3},{3,2},{4,5},{5,4},{6,7},{7,6},{8,16},{9,17},{10,... | collective-permute-start | bytes 4915208 | tf_op jit(solution)/shard_map/ppermute | solution.py:175
  7.3 0.8 constant_dynamic-update-slice_fusion.3
  8.1 2.3 %collective-permute-done.2 = bf16[128,256]{1,0:T(8,128)(2,1)S(1)} collective-permute-done((bf16[128,256]{1,0:T(8,128)(2,1)}, bf16[128,256]{1,0:T(8,128)(2,1)S(1)}, u32[]{:S(2)}, u32[]{:S(2)}) %collective-permute-start.2) | collective-permute-done | bytes 65568 | tf_op jit(solution)/shard_map/ppermute | solution.py:175
  10.4 1.3 collective-permute-start.3
  11.7 0.8 eq.28
  12.5 1.3 select_reduce_fusion.slot_ref
  13.7 2.4 %collective-permute-done.3 = bf16[512,256]{1,0:T(8,128)(2,1)S(1)} collective-permute-done((bf16[512,256]{1,0:T(8,128)(2,1)S(1)}, bf16[512,256]{1,0:T(8,128)(2,1)S(1)}, u32[]{:S(2)}, u32[]{:S(2)}) %collective-permute-start.3) | collective-permute-done | bytes 262176 | tf_op jit(solution)/shard_map/ppermute | solution.py:175
  16.8 7.9 %attention.1.new_ref = bf16[512,1280]{1,0:T(8,128)(2,1)} custom-call(s32[32]{0:T(128)} %select_reduce_fusion.slot_ref, bf16[4,10,8,128,128]{4,3,2,1,0:T(8,128)(2,1)} %probs_ref.1, bf16[512,1280]{1,0:T(8,128)(2,1)} %old_ref.1, bf16[4,128,256]{2,1,0:T(8,128)(2,1)} %bitcast.3, bf16[4,128,256]{2,1,0:T(8,128)(2,1)} %bitcast.4), custom_call_target="tpu_custom_call" | custom-call | flops 1048576 | bytes 1048576 | tf_op jit(solution)/shard_map/attention/pallas_call | solution.py:68
  24.8 3.8 %collective-permute-start.7 = (bf16[1280,640]{1,0:T(8,128)(2,1)}, bf16[1280,640]{1,0:T(8,128)(2,1)}, u32[]{:S(2)}, u32[]{:S(2)}) collective-permute-start(bf16[1280,640]{1,0:T(8,128)(2,1)} %refs_0_.1), channel_id=1, source_target_pairs={{0,1},{1,0},{2,3},{3,2},{4,5},{5,4},{6,7},{7,6},{8,9},{9,8},{10,11... | collective-permute-start | bytes 4915208 | tf_op jit(solution)/shard_map/ppermute | solution.py:175
  28.6 15.7 %collective-permute-done.4.refs_2_ = bf16[1280,640]{1,0:T(8,128)(2,1)} collective-permute-done((bf16[1280,640]{1,0:T(8,128)(2,1)}, bf16[1280,640]{1,0:T(8,128)(2,1)}, u32[]{:S(2)}, u32[]{:S(2)}) %collective-permute-start.4) | collective-permute-done | bytes 1638432 | tf_op jit(solution)/shard_map/ppermute | solution.py:175
  44.3 1.5 collective-permute-start.9
  45.8 1.9 %collective-permute-start.11 = (bf16[1280,640]{1,0:T(8,128)(2,1)}, bf16[1280,640]{1,0:T(8,128)(2,1)}, u32[]{:S(2)}, u32[]{:S(2)}) collective-permute-start(bf16[1280,640]{1,0:T(8,128)(2,1)} %collective-permute-done.10), channel_id=1, source_target_pairs={{0,8},{1,9},{2,10},{3,11},{4,12},{5,13},{6,14},{7,15},{8,0},{9,1},... | collective-permute-start | bytes 4915208 | tf_op jit(solution)/shard_map/ppermute | solution.py:175
  47.7 3.9 %collective-permute-done.5.over_ref = bf16[512,1280]{1,0:T(8,128)(2,1)S(1)} collective-permute-done((bf16[512,1280]{1,0:T(8,128)(2,1)}, bf16[512,1280]{1,0:T(8,128)(2,1)S(1)}, u32[]{:S(2)}, u32[]{:S(2)}) %collective-permute-start.5) | collective-permute-done | bytes 1310752 | tf_op jit(solution)/shard_map/ppermute | solution.py:175
  51.6 3.0 %broadcast_select_fusion.1 = bf16[512,1280]{1,0:T(8,128)(2,1)} fusion(bf16[512,1280]{1,0:T(8,128)(2,1)S(1)} %collective-permute-done.5.over_ref, bf16[512,1280]{1,0:T(8,128)(2,1)} %attention.1.new_ref, pred[]{:T(512)S(6)} %eq.33), kind=kLoop, calls=%fused_computation.3 | loop fusion | flops 655360 | bytes 3932161 | tf_op jit(solution)/shard_map/jit(_where)/select_n | solution.py:229
  54.6 3.0 %collective-permute-start.6 = (bf16[512,1280]{1,0:T(8,128)(2,1)}, bf16[512,1280]{1,0:T(8,128)(2,1)S(1)}, u32[]{:S(2)}, u32[]{:S(2)}) collective-permute-start(bf16[512,1280]{1,0:T(8,128)(2,1)} %broadcast_select_fusion.1), channel_id=1, source_target_pairs={{0,1},{1,0},{2,3},{3,2},{4,5},{5,4},{6,7},{7,6},{8,9},{9,8},{10,11... | collective-permute-start | bytes 3932168 | tf_op jit(solution)/shard_map/ppermute | solution.py:175
  57.7 2.2 %slice.86 = bf16[1280,384]{1,0:T(8,128)(2,1)} slice(bf16[1280,640]{1,0:T(8,128)(2,1)} %collective-permute-done.4.refs_2_), slice={[0:1280], [0:384]} | slice | bytes 1966080 | tf_op jit(solution)/shard_map/slice | solution.py:188
  60.5 1.1 copy-done.1
  61.6 8.4 %product.4 = bf16[512,1280]{1,0:T(8,128)(2,1)} custom-call(s32[1]{0:T(128)} %bitcast.2.pick_ref, bf16[512,1280]{1,0:T(8,128)(2,1)} %attention.1.new_ref, bf16[512,1280]{1,0:T(8,128)(2,1)} %copy-done, bf16[512,1280]{1,0:T(8,128)(2,1)} %copy-done.1, bf16[1280,640]{1,0:T(8,128)(2,1)} %refs_0_.1, bf16[1280,640]{1,0:T(8,128)(2,1)} %collective-permute-done.7.refs_1_, ...), custom_call_target="tpu_custom_call" | custom-call | flops 1048576 | bytes 1048576 | tf_op jit(solution)/shard_map/product/pallas_call | solution.py:125
  70.0 14.0 %collective-permute-done.11 = bf16[1280,640]{1,0:T(8,128)(2,1)} collective-permute-done((bf16[1280,640]{1,0:T(8,128)(2,1)}, bf16[1280,640]{1,0:T(8,128)(2,1)}, u32[]{:S(2)}, u32[]{:S(2)}) %collective-permute-start.11) | collective-permute-done | bytes 1638432 | tf_op jit(solution)/shard_map/ppermute | solution.py:175
  84.0 1.6 %broadcast_select_fusion = bf16[1280,640]{1,0:T(8,128)(2,1)S(1)} fusion(bf16[1280,640]{1,0:T(8,128)(2,1)} %collective-permute-done.10, bf16[1280,640]{1,0:T(8,128)(2,1)} %collective-permute-done.11, pred[]{:T(512)S(6)} %or.3), kind=kLoop, calls=%fused_computation | loop fusion | flops 819200 | bytes 4915201 | tf_op jit(solution)/shard_map/jit(_where)/select_n | solution.py:246
  85.7 0.9 collective-permute-start.13
  86.8 1.5 collective-permute-start.12
  88.3 1.6 collective-permute-done.14.refs_3_
  89.8 5.8 %product.5 = bf16[512,640]{1,0:T(8,128)(2,1)} custom-call(s32[1]{0:T(128)} %bitcast.2.pick_ref, bf16[512,1280]{1,0:T(8,128)(2,1)} %attention.1.new_ref, bf16[512,1280]{1,0:T(8,128)(2,1)} %copy-done, bf16[512,1280]{1,0:T(8,128)(2,1)} %copy-done.1, bf16[1280,384]{1,0:T(8,128)(2,1)} %copy-done.4, bf16[1280,384]{1,0:T(8,128)(2,1)} %collective-permute-done.13.refs_1_, ...), custom_call_target="tpu_custom_call" | custom-call | flops 1048576 | bytes 1048576 | tf_op jit(solution)/shard_map/product/pallas_call | solution.py:125
  95.6 1.2 broadcast_select_fusion.2
  97.0 1.1 slice.91
  98.2 1.5 collective-permute-start.19
  99.7 13.2 %collective-permute-done.15 = bf16[512,640]{1,0:T(8,128)(2,1)S(1)} collective-permute-done((bf16[512,640]{1,0:T(8,128)(2,1)S(1)}, bf16[512,640]{1,0:T(8,128)(2,1)S(1)}, u32[]{:S(2)}, u32[]{:S(2)}) %collective-permute-start.15) | collective-permute-done | bytes 655392 | tf_op jit(solution)/shard_map/ppermute | solution.py:175
  113.1 1.3 slice_select_fusion.2
  114.5 1.3 collective-permute-start.18
  119.0 4.6 %product.6 = bf16[512,384]{1,0:T(8,128)(2,1)} custom-call(s32[1]{0:T(128)} %bitcast.2.pick_ref, bf16[512,1280]{1,0:T(8,128)(2,1)} %attention.1.new_ref, bf16[512,1280]{1,0:T(8,128)(2,1)} %copy-done, bf16[512,1280]{1,0:T(8,128)(2,1)} %copy-done.1, bf16[1280,128]{1,0:T(8,128)(2,1)} %copy-done.9, bf16[1280,128]{1,0:T(8,128)(2,1)} %copy-done.15, ...), custom_call_target="tpu_custom_call" | custom-call | flops 1048576 | bytes 1048576 | tf_op jit(solution)/shard_map/product/pallas_call | solution.py:125
  123.5 1.8 %broadcast_select_fusion.6 = (bf16[512,384]{1,0:T(8,128)(2,1)S(1)}, bf16[512,384]{1,0:T(8,128)(2,1)}) fusion(bf16[512,384]{1,0:T(8,128)(2,1)} %product.6, pred[]{:T(512)S(6)} %eq.34, bf16[512,1280]{1,0:T(8,128)(2,1)S(1)} %copy-done.2), kind=kLoop, calls=%fused_computation.11 | loop fusion | flops 393216 | bytes 1572865 | tf_op jit(solution)/shard_map/jit(_where)/select_n | solution.py:237
  125.4 1.1 slice_select_fusion
  126.5 0.8 collective-permute-start.24
  127.5 1.2 collective-permute-start.20
  129.2 3.7 %product.7 = bf16[512,256]{1,0:T(8,128)(2,1)} custom-call(s32[1]{0:T(128)} %bitcast.2.pick_ref, bf16[512,1280]{1,0:T(8,128)(2,1)} %attention.1.new_ref, bf16[512,1280]{1,0:T(8,128)(2,1)} %copy-done, bf16[512,1280]{1,0:T(8,128)(2,1)} %copy-done.1, bf16[1280,128]{1,0:T(8,128)(2,1)} %copy-done.11, bf16[1280,128]{1,0:T(8,128)(2,1)} %collective-permute-done.23.refs_1_, ...), custom_call_target="tpu_custom_call" | custom-call | flops 1048576 | bytes 1048576 | tf_op jit(solution)/shard_map/product/pallas_call | solution.py:125
  132.9 1.0 broadcast_select_fusion.14
  134.3 3.6 %collective-permute-done.20 = bf16[512,384]{1,0:T(8,128)(2,1)S(1)} collective-permute-done((bf16[512,384]{1,0:T(8,128)(2,1)}, bf16[512,384]{1,0:T(8,128)(2,1)S(1)}, u32[]{:S(2)}, u32[]{:S(2)}) %collective-permute-start.20) | collective-permute-done | bytes 393248 | tf_op jit(solution)/shard_map/ppermute | solution.py:175
  138.2 1.2 collective-permute-start.22
  139.5 2.6 %collective-permute-start.21 = (bf16[512,384]{1,0:T(8,128)(2,1)S(1)}, bf16[512,384]{1,0:T(8,128)(2,1)S(1)}, u32[]{:S(2)}, u32[]{:S(2)}) collective-permute-start(bf16[512,384]{1,0:T(8,128)(2,1)S(1)} %get-tuple-element.20), channel_id=1, source_target_pairs={{0,2},{1,4},{2,0},{3,6},{4,1},{5,7},{6,3},{7,5},{8,10},{9,12},{10,... | collective-permute-start | bytes 1179656 | tf_op jit(solution)/shard_map/ppermute | solution.py:175
  142.0 1.5 collective-permute-done.25
  143.7 1.2 collective-permute-start.27
  144.9 2.1 %collective-permute-start.26 = (bf16[512,256]{1,0:T(8,128)(2,1)S(1)}, bf16[512,256]{1,0:T(8,128)(2,1)S(1)}, u32[]{:S(2)}, u32[]{:S(2)}) collective-permute-start(bf16[512,256]{1,0:T(8,128)(2,1)S(1)} %get-tuple-element.23), channel_id=1, source_target_pairs={{0,2},{1,4},{2,0},{3,6},{4,1},{5,7},{6,3},{7,5},{8,10},{9,12},{10,... | collective-permute-start | bytes 786440 | tf_op jit(solution)/shard_map/ppermute | solution.py:175
  147.0 4.7 %collective-permute-done.21 = bf16[512,384]{1,0:T(8,128)(2,1)S(1)} collective-permute-done((bf16[512,384]{1,0:T(8,128)(2,1)S(1)}, bf16[512,384]{1,0:T(8,128)(2,1)S(1)}, u32[]{:S(2)}, u32[]{:S(2)}) %collective-permute-start.21) | collective-permute-done | bytes 393248 | tf_op jit(solution)/shard_map/ppermute | solution.py:175
  151.8 5.5 %collective-permute-done.26 = bf16[512,256]{1,0:T(8,128)(2,1)S(1)} collective-permute-done((bf16[512,256]{1,0:T(8,128)(2,1)S(1)}, bf16[512,256]{1,0:T(8,128)(2,1)S(1)}, u32[]{:S(2)}, u32[]{:S(2)}) %collective-permute-start.26) | collective-permute-done | bytes 262176 | tf_op jit(solution)/shard_map/ppermute | solution.py:175
  157.4 1.2 pad_maximum_fusion
  (73 shorter events, 7.3 us)
Async XLA Ops:
  0.6 7.5 %collective-permute-start.1 = (bf16[128,256]{1,0:T(8,128)(2,1)}, bf16[128,256]{1,0:T(8,128)(2,1)S(1)}, u32[]{:S(2)}, u32[]{:S(2)}) collective-permute-start(bf16[128,256]{1,0:T(8,128)(2,1)} %param.10), channel_id=1, source_target_pairs={{0,16},{1,17},{2,18},{3,19},{4,20},{5,21},{6,22},{7,23},{8,24},{9,... | collective-permute-start | bytes 196616 | tf_op jit(solution)/shard_map/ppermute | solution.py:175
  3.8 4.3 %collective-permute-start = (bf16[128,256]{1,0:T(8,128)(2,1)}, bf16[128,256]{1,0:T(8,128)(2,1)S(1)}, u32[]{:S(2)}, u32[]{:S(2)}) collective-permute-start(bf16[128,256]{1,0:T(8,128)(2,1)} %param.10), channel_id=1, source_target_pairs={{0,8},{1,9},{2,10},{3,11},{4,12},{5,13},{6,14},{7,15},{8,0},{9,1},... | collective-permute-start | bytes 196616 | tf_op jit(solution)/shard_map/ppermute | solution.py:175
  5.1 5.3 %collective-permute-start.2 = (bf16[128,256]{1,0:T(8,128)(2,1)}, bf16[128,256]{1,0:T(8,128)(2,1)S(1)}, u32[]{:S(2)}, u32[]{:S(2)}) collective-permute-start(bf16[128,256]{1,0:T(8,128)(2,1)} %param.10), channel_id=1, source_target_pairs={{0,24},{1,25},{2,26},{3,27},{4,28},{5,29},{6,30},{7,31},{8,16},{9,... | collective-permute-start | bytes 196616 | tf_op jit(solution)/shard_map/ppermute | solution.py:175
  5.1 39.2 %collective-permute-start.4 = (bf16[1280,640]{1,0:T(8,128)(2,1)}, bf16[1280,640]{1,0:T(8,128)(2,1)}, u32[]{:S(2)}, u32[]{:S(2)}) collective-permute-start(bf16[1280,640]{1,0:T(8,128)(2,1)} %refs_0_.1), channel_id=1, source_target_pairs={{0,8},{1,9},{2,10},{3,11},{4,12},{5,13},{6,14},{7,15},{8,0},{9,1},... | collective-permute-start | bytes 4915208 | tf_op jit(solution)/shard_map/ppermute | solution.py:175
  5.5 40.3 %collective-permute-start.10 = (bf16[1280,640]{1,0:T(8,128)(2,1)}, bf16[1280,640]{1,0:T(8,128)(2,1)}, u32[]{:S(2)}, u32[]{:S(2)}) collective-permute-start(bf16[1280,640]{1,0:T(8,128)(2,1)} %refs_0_.1), channel_id=1, source_target_pairs={{0,1},{1,0},{2,3},{3,2},{4,5},{5,4},{6,7},{7,6},{8,16},{9,17},{10,... | collective-permute-start | bytes 4915208 | tf_op jit(solution)/shard_map/ppermute | solution.py:175
  10.4 5.7 %copy-start.12 = (bf16[512,256]{1,0:T(8,128)(2,1)}, bf16[512,256]{1,0:T(8,128)(2,1)S(1)}, u32[]{:S(2)}) copy-start(bf16[512,256]{1,0:T(8,128)(2,1)S(1)} %constant_dynamic-update-slice_fusion) | copy-start | bytes 786436
  10.4 5.7 %collective-permute-start.3 = (bf16[512,256]{1,0:T(8,128)(2,1)S(1)}, bf16[512,256]{1,0:T(8,128)(2,1)S(1)}, u32[]{:S(2)}, u32[]{:S(2)}) collective-permute-start(bf16[512,256]{1,0:T(8,128)(2,1)S(1)} %constant_dynamic-update-slice_fusion), channel_id=1, source_target_pairs={{0,4},{1,5},{2,6},{3,7},{4,0},{5,1},{6,2},{7,3},{8,12},{9,13},{10,... | collective-permute-start | bytes 786440 | tf_op jit(solution)/shard_map/ppermute | solution.py:175
  16.1 0.7 copy-start.16
  24.7 26.9 %collective-permute-start.5 = (bf16[512,1280]{1,0:T(8,128)(2,1)}, bf16[512,1280]{1,0:T(8,128)(2,1)S(1)}, u32[]{:S(2)}, u32[]{:S(2)}) collective-permute-start(bf16[512,1280]{1,0:T(8,128)(2,1)} %attention.1.new_ref), channel_id=1, source_target_pairs={{0,4},{1,5},{2,6},{3,7},{4,0},{5,1},{6,2},{7,3},{8,12},{9,13},{10,... | collective-permute-start | bytes 3932168 | tf_op jit(solution)/shard_map/ppermute | solution.py:175
  24.8 35.1 %collective-permute-start.7 = (bf16[1280,640]{1,0:T(8,128)(2,1)}, bf16[1280,640]{1,0:T(8,128)(2,1)}, u32[]{:S(2)}, u32[]{:S(2)}) collective-permute-start(bf16[1280,640]{1,0:T(8,128)(2,1)} %refs_0_.1), channel_id=1, source_target_pairs={{0,1},{1,0},{2,3},{3,2},{4,5},{5,4},{6,7},{7,6},{8,9},{9,8},{10,11... | collective-permute-start | bytes 4915208 | tf_op jit(solution)/shard_map/ppermute | solution.py:175
  44.3 25.7 %collective-permute-start.9 = (bf16[1280,640]{1,0:T(8,128)(2,1)}, bf16[1280,640]{1,0:T(8,128)(2,1)}, u32[]{:S(2)}, u32[]{:S(2)}) collective-permute-start(bf16[1280,640]{1,0:T(8,128)(2,1)} %collective-permute-done.4.refs_2_), channel_id=1, source_target_pairs={{0,1},{1,0},{2,3},{3,2},{4,5},{5,4},{6,7},{7,6},{8,16},{9,17},{10,... | collective-permute-start | bytes 4915208 | tf_op jit(solution)/shard_map/ppermute | solution.py:175
  45.8 14.8 %collective-permute-start.8 = (bf16[1280,640]{1,0:T(8,128)(2,1)}, bf16[1280,640]{1,0:T(8,128)(2,1)}, u32[]{:S(2)}, u32[]{:S(2)}) collective-permute-start(bf16[1280,640]{1,0:T(8,128)(2,1)} %collective-permute-done.4.refs_2_), channel_id=1, source_target_pairs={{0,1},{1,0},{2,3},{3,2},{4,5},{5,4},{6,7},{7,6},{8,9},{9,8},{10,11... | collective-permute-start | bytes 4915208 | tf_op jit(solution)/shard_map/ppermute | solution.py:175
  45.8 38.2 %collective-permute-start.11 = (bf16[1280,640]{1,0:T(8,128)(2,1)}, bf16[1280,640]{1,0:T(8,128)(2,1)}, u32[]{:S(2)}, u32[]{:S(2)}) collective-permute-start(bf16[1280,640]{1,0:T(8,128)(2,1)} %collective-permute-done.10), channel_id=1, source_target_pairs={{0,8},{1,9},{2,10},{3,11},{4,12},{5,13},{6,14},{7,15},{8,0},{9,1},... | collective-permute-start | bytes 4915208 | tf_op jit(solution)/shard_map/ppermute | solution.py:175
  51.6 3.0 %copy-start = (bf16[512,1280]{1,0:T(8,128)(2,1)}, bf16[512,1280]{1,0:T(8,128)(2,1)S(1)}, u32[]{:S(2)}) copy-start(bf16[512,1280]{1,0:T(8,128)(2,1)S(1)} %collective-permute-done.5.over_ref) | copy-start | bytes 3932164
  54.6 5.9 %collective-permute-start.6 = (bf16[512,1280]{1,0:T(8,128)(2,1)}, bf16[512,1280]{1,0:T(8,128)(2,1)S(1)}, u32[]{:S(2)}, u32[]{:S(2)}) collective-permute-start(bf16[512,1280]{1,0:T(8,128)(2,1)} %broadcast_select_fusion.1), channel_id=1, source_target_pairs={{0,1},{1,0},{2,3},{3,2},{4,5},{5,4},{6,7},{7,6},{8,9},{9,8},{10,11... | collective-permute-start | bytes 3932168 | tf_op jit(solution)/shard_map/ppermute | solution.py:175
  60.5 1.1 copy-start.1
  85.7 4.2 %copy-start.4 = (bf16[1280,384]{1,0:T(8,128)(2,1)}, bf16[1280,384]{1,0:T(8,128)(2,1)S(1)}, u32[]{:S(2)}) copy-start(bf16[1280,384]{1,0:T(8,128)(2,1)S(1)} %slice.88.refs_0_) | copy-start | bytes 2949124
  85.7 4.1 %collective-permute-start.13 = (bf16[1280,384]{1,0:T(8,128)(2,1)S(1)}, bf16[1280,384]{1,0:T(8,128)(2,1)}, u32[]{:S(2)}, u32[]{:S(2)}) collective-permute-start(bf16[1280,384]{1,0:T(8,128)(2,1)S(1)} %slice.88.refs_0_), channel_id=1, source_target_pairs={{0,1},{1,0},{2,3},{3,2},{4,5},{5,4},{6,7},{7,6},{8,9},{9,8},{10,11... | collective-permute-start | bytes 2949128 | tf_op jit(solution)/shard_map/ppermute | solution.py:175
  86.6 3.2 %copy-start.5 = (bf16[1280,256]{1,0:T(8,128)(2,1)}, bf16[1280,256]{1,0:T(8,128)(2,1)S(1)}, u32[]{:S(2)}) copy-start(bf16[1280,256]{1,0:T(8,128)(2,1)S(1)} %slice.89.refs_2_) | copy-start | bytes 1966084
  86.6 3.2 %collective-permute-start.14 = (bf16[1280,256]{1,0:T(8,128)(2,1)S(1)}, bf16[1280,256]{1,0:T(8,128)(2,1)}, u32[]{:S(2)}, u32[]{:S(2)}) collective-permute-start(bf16[1280,256]{1,0:T(8,128)(2,1)S(1)} %slice.89.refs_2_), channel_id=1, source_target_pairs={{0,1},{1,0},{2,3},{3,2},{4,5},{5,4},{6,7},{7,6},{8,9},{9,8},{10,11... | collective-permute-start | bytes 1966088 | tf_op jit(solution)/shard_map/ppermute | solution.py:175
  86.8 8.9 %copy-start.2 = (bf16[512,1280]{1,0:T(8,128)(2,1)S(1)}, bf16[512,1280]{1,0:T(8,128)(2,1)}, u32[]{:S(2)}) copy-start(bf16[512,1280]{1,0:T(8,128)(2,1)} %product.4) | copy-start | bytes 3932164
  86.8 26.4 %collective-permute-start.12 = (bf16[1280,384]{1,0:T(8,128)(2,1)}, bf16[1280,384]{1,0:T(8,128)(2,1)S(1)}, u32[]{:S(2)}, u32[]{:S(2)}) collective-permute-start(bf16[1280,384]{1,0:T(8,128)(2,1)} %slice.86), channel_id=1, source_target_pairs={{0,8},{1,9},{2,10},{3,11},{4,12},{5,13},{6,14},{7,15},{8,24},{9,25... | collective-permute-start | bytes 2949128 | tf_op jit(solution)/shard_map/ppermute | solution.py:175
  95.6 17.2 %copy-start.3 = (bf16[512,640]{1,0:T(8,128)(2,1)S(1)}, bf16[512,640]{1,0:T(8,128)(2,1)}, u32[]{:S(2)}) copy-start(bf16[512,640]{1,0:T(8,128)(2,1)} %product.5) | copy-start | bytes 1966084
  96.9 16.0 %collective-permute-start.15 = (bf16[512,640]{1,0:T(8,128)(2,1)S(1)}, bf16[512,640]{1,0:T(8,128)(2,1)S(1)}, u32[]{:S(2)}, u32[]{:S(2)}) collective-permute-start(bf16[512,640]{1,0:T(8,128)(2,1)S(1)} %broadcast_select_fusion.2), channel_id=1, source_target_pairs={{0,2},{1,3},{2,0},{3,1},{4,6},{5,7},{6,4},{7,5},{8,10},{9,11},{10,... | collective-permute-start | bytes 1966088 | tf_op jit(solution)/shard_map/ppermute | solution.py:175
  98.2 27.2 %collective-permute-start.19 = (bf16[1280,256]{1,0:T(8,128)(2,1)S(1)}, bf16[1280,256]{1,0:T(8,128)(2,1)S(1)}, u32[]{:S(2)}, u32[]{:S(2)}) collective-permute-start(bf16[1280,256]{1,0:T(8,128)(2,1)S(1)} %slice.91), channel_id=1, source_target_pairs={{0,8},{1,9},{2,10},{3,11},{4,12},{5,13},{6,14},{7,15},{8,24},{9,25... | collective-permute-start | bytes 1966088 | tf_op jit(solution)/shard_map/ppermute | solution.py:175
  114.4 3.5 %copy-start.7 = (bf16[1280,128]{1,0:T(8,128)(2,1)}, bf16[1280,128]{1,0:T(8,128)(2,1)S(1)}, u32[]{:S(2)}) copy-start(bf16[1280,128]{1,0:T(8,128)(2,1)S(1)} %get-tuple-element.26.refs_4_) | copy-start | bytes 983044
  114.5 3.5 %copy-start.8 = (bf16[1280,128]{1,0:T(8,128)(2,1)}, bf16[1280,128]{1,0:T(8,128)(2,1)S(1)}, u32[]{:S(2)}) copy-start(bf16[1280,128]{1,0:T(8,128)(2,1)S(1)} %get-tuple-element.27.refs_2_) | copy-start | bytes 983044
  114.5 3.5 %copy-start.9 = (bf16[1280,128]{1,0:T(8,128)(2,1)}, bf16[1280,128]{1,0:T(8,128)(2,1)S(1)}, u32[]{:S(2)}) copy-start(bf16[1280,128]{1,0:T(8,128)(2,1)S(1)} %get-tuple-element.28.refs_0_) | copy-start | bytes 983044
  114.5 2.5 %collective-permute-start.18 = (bf16[1280,128]{1,0:T(8,128)(2,1)S(1)}, bf16[1280,128]{1,0:T(8,128)(2,1)S(1)}, u32[]{:S(2)}, u32[]{:S(2)}) collective-permute-start(bf16[1280,128]{1,0:T(8,128)(2,1)S(1)} %get-tuple-element.26.refs_4_), channel_id=1, source_target_pairs={{0,1},{1,0},{2,3},{3,2},{4,5},{5,4},{6,7},{7,6},{8,9},{9,8},{10,11... | collective-permute-start | bytes 983048 | tf_op jit(solution)/shard_map/ppermute | solution.py:175
  115.8 1.7 %collective-permute-start.17 = (bf16[1280,128]{1,0:T(8,128)(2,1)S(1)}, bf16[1280,128]{1,0:T(8,128)(2,1)S(1)}, u32[]{:S(2)}, u32[]{:S(2)}) collective-permute-start(bf16[1280,128]{1,0:T(8,128)(2,1)S(1)} %get-tuple-element.27.refs_2_), channel_id=1, source_target_pairs={{0,1},{1,0},{2,3},{3,2},{4,5},{5,4},{6,7},{7,6},{8,9},{9,8},{10,11... | collective-permute-start | bytes 983048 | tf_op jit(solution)/shard_map/ppermute | solution.py:175
  115.8 2.1 %collective-permute-start.16 = (bf16[1280,128]{1,0:T(8,128)(2,1)S(1)}, bf16[1280,128]{1,0:T(8,128)(2,1)S(1)}, u32[]{:S(2)}, u32[]{:S(2)}) collective-permute-start(bf16[1280,128]{1,0:T(8,128)(2,1)S(1)} %get-tuple-element.28.refs_0_), channel_id=1, source_target_pairs={{0,1},{1,0},{2,3},{3,2},{4,5},{5,4},{6,7},{7,6},{8,9},{9,8},{10,11... | collective-permute-start | bytes 983048 | tf_op jit(solution)/shard_map/ppermute | solution.py:175
  117.0 0.9 copy-start.13
  117.5 0.7 copy-start.14
  118.2 0.7 copy-start.15
  126.5 2.7 %copy-start.10 = (bf16[1280,128]{1,0:T(8,128)(2,1)}, bf16[1280,128]{1,0:T(8,128)(2,1)S(1)}, u32[]{:S(2)}) copy-start(bf16[1280,128]{1,0:T(8,128)(2,1)S(1)} %get-tuple-element.29.refs_2_) | copy-start | bytes 983044
  126.5 2.7 %copy-start.11 = (bf16[1280,128]{1,0:T(8,128)(2,1)}, bf16[1280,128]{1,0:T(8,128)(2,1)S(1)}, u32[]{:S(2)}) copy-start(bf16[1280,128]{1,0:T(8,128)(2,1)S(1)} %get-tuple-element.30.refs_0_) | copy-start | bytes 983044
  126.5 2.2 %collective-permute-start.24 = (bf16[1280,128]{1,0:T(8,128)(2,1)S(1)}, bf16[1280,128]{1,0:T(8,128)(2,1)}, u32[]{:S(2)}, u32[]{:S(2)}) collective-permute-start(bf16[1280,128]{1,0:T(8,128)(2,1)S(1)} %get-tuple-element.29.refs_2_), channel_id=1, source_target_pairs={{0,1},{1,0},{2,3},{3,2},{4,5},{5,4},{6,7},{7,6},{8,9},{9,8},{10,11... | collective-permute-start | bytes 983048 | tf_op jit(solution)/shard_map/ppermute | solution.py:175
  127.4 1.9 %collective-permute-start.23 = (bf16[1280,128]{1,0:T(8,128)(2,1)S(1)}, bf16[1280,128]{1,0:T(8,128)(2,1)}, u32[]{:S(2)}, u32[]{:S(2)}) collective-permute-start(bf16[1280,128]{1,0:T(8,128)(2,1)S(1)} %get-tuple-element.30.refs_0_), channel_id=1, source_target_pairs={{0,1},{1,0},{2,3},{3,2},{4,5},{5,4},{6,7},{7,6},{8,9},{9,8},{10,11... | collective-permute-start | bytes 983048 | tf_op jit(solution)/shard_map/ppermute | solution.py:175
  127.5 10.5 %collective-permute-start.20 = (bf16[512,384]{1,0:T(8,128)(2,1)}, bf16[512,384]{1,0:T(8,128)(2,1)S(1)}, u32[]{:S(2)}, u32[]{:S(2)}) collective-permute-start(bf16[512,384]{1,0:T(8,128)(2,1)} %get-tuple-element.18), channel_id=1, source_target_pairs={{0,2},{1,3},{2,0},{3,1},{4,6},{5,7},{6,4},{7,5},{8,10},{9,11},{10,... | collective-permute-start | bytes 1179656 | tf_op jit(solution)/shard_map/ppermute | solution.py:175
  133.9 9.6 %copy-start.6 = (bf16[512,256]{1,0:T(8,128)(2,1)S(1)}, bf16[512,256]{1,0:T(8,128)(2,1)}, u32[]{:S(2)}) copy-start(bf16[512,256]{1,0:T(8,128)(2,1)} %product.7) | copy-start | bytes 786436
  133.9 9.6 %collective-permute-start.25 = (bf16[512,256]{1,0:T(8,128)(2,1)S(1)}, bf16[512,256]{1,0:T(8,128)(2,1)S(1)}, u32[]{:S(2)}, u32[]{:S(2)}) collective-permute-start(bf16[512,256]{1,0:T(8,128)(2,1)S(1)} %broadcast_select_fusion.14), channel_id=1, source_target_pairs={{0,2},{1,3},{2,0},{3,1},{4,6},{5,7},{6,4},{7,5},{8,10},{9,11},{10,... | collective-permute-start | bytes 786440 | tf_op jit(solution)/shard_map/ppermute | solution.py:175
  138.2 8.8 %collective-permute-start.22 = (bf16[512,384]{1,0:T(8,128)(2,1)S(1)}, bf16[512,384]{1,0:T(8,128)(2,1)S(1)}, u32[]{:S(2)}, u32[]{:S(2)}) collective-permute-start(bf16[512,384]{1,0:T(8,128)(2,1)S(1)} %broadcast_select_fusion.3), channel_id=1, source_target_pairs={{0,1},{1,5},{2,3},{3,7},{4,0},{5,4},{6,2},{7,6},{8,9},{9,13},{10,1... | collective-permute-start | bytes 1179656 | tf_op jit(solution)/shard_map/ppermute | solution.py:175
  139.5 12.2 %collective-permute-start.21 = (bf16[512,384]{1,0:T(8,128)(2,1)S(1)}, bf16[512,384]{1,0:T(8,128)(2,1)S(1)}, u32[]{:S(2)}, u32[]{:S(2)}) collective-permute-start(bf16[512,384]{1,0:T(8,128)(2,1)S(1)} %get-tuple-element.20), channel_id=1, source_target_pairs={{0,2},{1,4},{2,0},{3,6},{4,1},{5,7},{6,3},{7,5},{8,10},{9,12},{10,... | collective-permute-start | bytes 1179656 | tf_op jit(solution)/shard_map/ppermute | solution.py:175
  143.7 8.1 %collective-permute-start.27 = (bf16[512,256]{1,0:T(8,128)(2,1)S(1)}, bf16[512,256]{1,0:T(8,128)(2,1)S(1)}, u32[]{:S(2)}, u32[]{:S(2)}) collective-permute-start(bf16[512,256]{1,0:T(8,128)(2,1)S(1)} %broadcast_select_fusion.11), channel_id=1, source_target_pairs={{0,1},{1,5},{2,3},{3,7},{4,0},{5,4},{6,2},{7,6},{8,9},{9,13},{10,1... | collective-permute-start | bytes 786440 | tf_op jit(solution)/shard_map/ppermute | solution.py:175
  144.9 12.4 %collective-permute-start.26 = (bf16[512,256]{1,0:T(8,128)(2,1)S(1)}, bf16[512,256]{1,0:T(8,128)(2,1)S(1)}, u32[]{:S(2)}, u32[]{:S(2)}) collective-permute-start(bf16[512,256]{1,0:T(8,128)(2,1)S(1)} %get-tuple-element.23), channel_id=1, source_target_pairs={{0,2},{1,4},{2,0},{3,6},{4,1},{5,7},{6,3},{7,5},{8,10},{9,12},{10,... | collective-permute-start | bytes 786440 | tf_op jit(solution)/shard_map/ppermute | solution.py:175

commit v4 on v3

--- a/solution.py
+++ b/solution.py
@@ -139,6 +139,65 @@
     )(pick, *lefts, *flat)
 
 
+def split_product_kernel(column, flag_ref, new_ref, over_ref, inner_ref, end_ref, keep_ref, *refs):
+    *pass_refs, left, right, loaded = refs
+    width = end_ref.shape[1]
+
+    def load_left(i, source):
+        return pltpu.make_async_copy(source, left.at[i], loaded.at[i])
+
+    def load_right(source):
+        return pltpu.make_async_copy(source, right, loaded.at[2])
+
+    @pl.when(flag_ref[0] == 1)
+    def _():
+        load_left(0, new_ref).start()
+        load_left(1, over_ref).start()
+
+    @pl.when(flag_ref[0] == 0)
+    def _():
+        load_left(0, over_ref).start()
+        load_left(1, new_ref).start()
+
+    inner_part = inner_ref.at[:, column:column + width]
+
+    @pl.when(flag_ref[1] == 1)
+    def _():
+        load_right(inner_part).start()
+
+    @pl.when(flag_ref[1] == 0)
+    def _():
+        load_right(end_ref).start()
+
+    load_right(end_ref).wait()
+    load_left(1, new_ref).wait()
+    passed = jnp.dot(left[1], right[...], preferred_element_type=jnp.float32).astype(jnp.bfloat16)
+    for i, pass_ref in enumerate(pass_refs):
+        pass_ref[...] = passed[:, i * BLK:(i + 1) * BLK]
+    load_left(0, new_ref).wait()
+    keep_ref[...] = jnp.dot(left[0], right[...], preferred_element_type=jnp.float32).astype(jnp.bfloat16)
+
+
+def split_product(flags, lefts, inner_block, end_block, column):
+    rows, depth = lefts[0].shape
+    width = end_block.shape[1]
+    return pl.pallas_call(
+        functools.partial(split_product_kernel, column),
+        out_shape=[jax.ShapeDtypeStruct((rows, width), jnp.bfloat16)]
+        + [jax.ShapeDtypeStruct((rows, BLK), jnp.bfloat16)] * (width // BLK),
+        in_specs=[pl.BlockSpec(memory_space=pltpu.SMEM)] + [pl.BlockSpec(memory_space=pl.ANY)] * 4,
+        out_specs=[pl.BlockSpec(memory_space=pltpu.VMEM)] * (1 + width // BLK),
+        scratch_shapes=[
+            pltpu.VMEM((2, rows, depth), jnp.bfloat16),
+            pltpu.VMEM((depth, width), jnp.bfloat16),
+            pltpu.SemaphoreType.DMA((3,)),
+        ],
+        compiler_params=pltpu.CompilerParams(vmem_limit_bytes=56 * MIB),
+        cost_estimate=pl.CostEstimate(flops=MIB, bytes_accessed=MIB, transcendentals=0),
+        name="split_product",
+    )(flags, *lefts, inner_block, end_block)
+
+
 def add(a, b):
     return (a.astype(jnp.float32) + b.astype(jnp.float32)).astype(jnp.bfloat16)
 
@@ -190,10 +249,6 @@
     return parts
 
 
-def narrow(value):
-    return columns(value, [BLK] * (value.shape[1] // BLK))
-
-
 def tie(*values):
     return lax.optimization_barrier(values)
 
@@ -228,10 +283,15 @@
     over_x = move(attn_new, lambda z, x, y, c: (z, 1 - x, y, c))
     other = to_core(jnp.where(x == c, over_x, attn_new))
     pick = (x == c).astype(jnp.int32).reshape(1)
+    flags = jnp.stack([x == c, is_inner]).astype(jnp.int32)
     rows = [attn_new, over_x, other]
 
     def with_other(block):
         return block, to_core(block)
+
+    def both_cores(inner_block, end_block, column):
+        kept, *passed = split_product(flags, rows[:2], inner_block, end_block, column)
+        return add(kept, jnp.concatenate([to_core(v) for v in passed], axis=1))
 
     def to_sum(p_half, p_cross):
         return jnp.where(y == half, p_cross, p_half), jnp.where(y == half, p_half, p_cross)
@@ -251,13 +311,15 @@
     first = summed(*to_sum(p_own, p_cross))
     last_end[0], first = tie(last_end[0], first)
     first = columns(first)
-    second, terms = [], None
-    for p_pair, inner_part, end_part in zip(columns(p_pair), columns(last), last_end, strict=True):
+    second, terms, column = [], None, 0
+    for p_pair, end_part in zip(columns(p_pair), last_end, strict=True):
         if terms:
             *terms, end_part = tie(*terms, end_part)
             second.append(summed(*terms))
-        pieces = [jnp.where(is_inner, *v) for v in zip(narrow(inner_part), narrow(end_part), strict=True)]
-        p_last = product(pick, rows, [with_other(v) for v in pieces])
+        p_last = both_cores(last, end_part, column)
+        column += end_part.shape[1]
+        if second:
+            second[0], p_last = tie(second[0], p_last)
         terms = to_sum(p_pair, p_last)
     second.append(summed(*terms))
 

time: 159 us -> 157 us (0.987)
  starting transfers between devices: 33.8 us -> 36.5 us
  waiting for transfers between devices: 71.1 us -> 68.4 us
  other arithmetic: 14.4 us -> 12.1 us
    pallas_call x0 -> x2, Pallas kernels: none -> 10.1 us  [split_product(): pl.pallas_call(functools.partial(split_product_kernel, column), out_shape...]
    pallas_call x4 -> x2, Pallas kernels: 22.4 us -> 14.2 us  [product(): pl.pallas_call(functools.partial(product_kernel, len(rights)), out_shape=...]
    ppermute x28, waiting for transfers between devices: 71.1 us -> 68.4 us  [move(): return lax.ppermute(value, BOTH, pairs)]
    ppermute x28, starting transfers between devices: 33.8 us -> 36.5 us  [move(): return lax.ppermute(value, BOTH, pairs)]
    select_n x2 -> x0, other arithmetic: 2.45 us -> none  [local_line(): jnp.where(is_inner, *v)]
    pallas_call x1, Pallas kernels: 7.89 us -> 6.25 us  [refresh(): pl.pallas_call(attention_kernel, out_shape=jax.ShapeDtypeStruct(out_old.s...]
    unnamed x37 -> x23, local copies, waits for them, and re-layouts: 3.68 us -> 2.74 us
  transfers between devices with their start and end apart: 28 -> 28, of which waited for: 17 -> 17; matrix products, arithmetic and copies ran while one was open for 10% -> 9% of each run, Pallas kernels for 19% -> 19%
where the time goes in v4:
time: 157 us; the launch traced here: 156 us
  waiting for transfers between devices  68.4 us (44%)
  starting transfers between devices  36.5 us (23%)
  Pallas kernels  30.5 us (19%)
  other arithmetic  12.1 us (8%)
  local copies, waits for them, and re-layouts  7.98 us (5%)
    ppermute x28, waiting for transfers between devices, move(): return lax.ppermute(value, BOTH, pairs)  68.4 us
    ppermute x28, starting transfers between devices, move(): return lax.ppermute(value, BOTH, pairs)  36.5 us
    pallas_call x2, Pallas kernels, product(): pl.pallas_call(functools.partial(product_kernel, len(rights)), out_shape=...  14.2 us
    pallas_call x2, Pallas kernels, split_product(): pl.pallas_call(functools.partial(split_product_kernel, column), out_shape...  10.1 us
    pallas_call x1, Pallas kernels, refresh(): pl.pallas_call(attention_kernel, out_shape=jax.ShapeDtypeStruct(out_old.s...  6.25 us
    slice x4, local copies, waits for them, and re-layouts, columns(): parts.append(value[:, at:at + width])  4.47 us
  transfers between devices with their start and end apart: 28, of which 17 were waited for; matrix products, arithmetic and copies ran while one was open for 9% of the time, Pallas kernels for 19%

profile of v4, /device:TPU:1, one launch (start us, length us, event | category | flops | bytes accessed | tf_op | source)
XLA Modules:
  0.0 156.4 jit_solution(15338624468560684038)
XLA Ops:
  0.6 3.2 %collective-permute-start.1 = (bf16[128,256]{1,0:T(8,128)(2,1)}, bf16[128,256]{1,0:T(8,128)(2,1)S(1)}, u32[]{:S(2)}, u32[]{:S(2)}) collective-permute-start(bf16[128,256]{1,0:T(8,128)(2,1)} %param.10), channel_id=1, source_target_pairs={{0,16},{1,17},{2,18},{3,19},{4,20},{5,21},{6,22},{7,23},{8,24},{9,... | collective-permute-start | bytes 196616 | tf_op jit(solution)/shard_map/ppermute | solution.py:234
  3.8 1.3 collective-permute-start
  5.5 1.8 %collective-permute-start.10 = (bf16[1280,640]{1,0:T(8,128)(2,1)}, bf16[1280,640]{1,0:T(8,128)(2,1)}, u32[]{:S(2)}, u32[]{:S(2)}) collective-permute-start(bf16[1280,640]{1,0:T(8,128)(2,1)} %refs_0_.1), channel_id=1, source_target_pairs={{0,1},{1,0},{2,3},{3,2},{4,5},{5,4},{6,7},{7,6},{8,16},{9,17},{10,... | collective-permute-start | bytes 4915208 | tf_op jit(solution)/shard_map/ppermute | solution.py:234
  7.3 0.8 constant_dynamic-update-slice_fusion.3
  8.1 2.3 %collective-permute-done.2 = bf16[128,256]{1,0:T(8,128)(2,1)S(1)} collective-permute-done((bf16[128,256]{1,0:T(8,128)(2,1)}, bf16[128,256]{1,0:T(8,128)(2,1)S(1)}, u32[]{:S(2)}, u32[]{:S(2)}) %collective-permute-start.2) | collective-permute-done | bytes 65568 | tf_op jit(solution)/shard_map/ppermute | solution.py:234
  10.4 1.3 collective-permute-start.3
  12.5 1.3 select_reduce_fusion.slot_ref
  13.8 2.3 %collective-permute-done.3 = bf16[512,256]{1,0:T(8,128)(2,1)S(1)} collective-permute-done((bf16[512,256]{1,0:T(8,128)(2,1)S(1)}, bf16[512,256]{1,0:T(8,128)(2,1)S(1)}, u32[]{:S(2)}, u32[]{:S(2)}) %collective-permute-start.3) | collective-permute-done | bytes 262176 | tf_op jit(solution)/shard_map/ppermute | solution.py:234
  16.8 6.3 %attention.1.new_ref = bf16[512,1280]{1,0:T(8,128)(2,1)} custom-call(s32[32]{0:T(128)} %select_reduce_fusion.slot_ref, bf16[4,10,8,128,128]{4,3,2,1,0:T(8,128)(2,1)} %probs_ref.1, bf16[512,1280]{1,0:T(8,128)(2,1)} %old_ref.1, bf16[4,128,256]{2,1,0:T(8,128)(2,1)} %bitcast.4, bf16[4,128,256]{2,1,0:T(8,128)(2,1)} %bitcast.5), custom_call_target="tpu_custom_call" | custom-call | flops 1048576 | bytes 1048576 | tf_op jit(solution)/shard_map/attention/pallas_call | solution.py:68
  23.1 2.0 %collective-permute-start.5 = (bf16[512,1280]{1,0:T(8,128)(2,1)}, bf16[512,1280]{1,0:T(8,128)(2,1)S(1)}, u32[]{:S(2)}, u32[]{:S(2)}) collective-permute-start(bf16[512,1280]{1,0:T(8,128)(2,1)} %attention.1.new_ref), channel_id=1, source_target_pairs={{0,4},{1,5},{2,6},{3,7},{4,0},{5,1},{6,2},{7,3},{8,12},{9,13},{10,... | collective-permute-start | bytes 3932168 | tf_op jit(solution)/shard_map/ppermute | solution.py:234
  25.1 4.1 %collective-permute-start.7 = (bf16[1280,640]{1,0:T(8,128)(2,1)}, bf16[1280,640]{1,0:T(8,128)(2,1)}, u32[]{:S(2)}, u32[]{:S(2)}) collective-permute-start(bf16[1280,640]{1,0:T(8,128)(2,1)} %refs_0_.1), channel_id=1, source_target_pairs={{0,1},{1,0},{2,3},{3,2},{4,5},{5,4},{6,7},{7,6},{8,9},{9,8},{10,11... | collective-permute-start | bytes 4915208 | tf_op jit(solution)/shard_map/ppermute | solution.py:234
  29.2 15.1 %collective-permute-done.4.refs_2_ = bf16[1280,640]{1,0:T(8,128)(2,1)} collective-permute-done((bf16[1280,640]{1,0:T(8,128)(2,1)}, bf16[1280,640]{1,0:T(8,128)(2,1)}, u32[]{:S(2)}, u32[]{:S(2)}) %collective-permute-start.4) | collective-permute-done | bytes 1638432 | tf_op jit(solution)/shard_map/ppermute | solution.py:234
  44.3 1.5 collective-permute-start.9
  45.8 1.9 %collective-permute-start.11 = (bf16[1280,640]{1,0:T(8,128)(2,1)}, bf16[1280,640]{1,0:T(8,128)(2,1)}, u32[]{:S(2)}, u32[]{:S(2)}) collective-permute-start(bf16[1280,640]{1,0:T(8,128)(2,1)} %collective-permute-done.10), channel_id=1, source_target_pairs={{0,8},{1,9},{2,10},{3,11},{4,12},{5,13},{6,14},{7,15},{8,0},{9,1},... | collective-permute-start | bytes 4915208 | tf_op jit(solution)/shard_map/ppermute | solution.py:234
  47.7 3.0 %collective-permute-done.5.over_ref = bf16[512,1280]{1,0:T(8,128)(2,1)S(1)} collective-permute-done((bf16[512,1280]{1,0:T(8,128)(2,1)}, bf16[512,1280]{1,0:T(8,128)(2,1)S(1)}, u32[]{:S(2)}, u32[]{:S(2)}) %collective-permute-start.5) | collective-permute-done | bytes 1310752 | tf_op jit(solution)/shard_map/ppermute | solution.py:234
  50.7 3.0 %broadcast_select_fusion.1 = bf16[512,1280]{1,0:T(8,128)(2,1)} fusion(bf16[512,1280]{1,0:T(8,128)(2,1)S(1)} %collective-permute-done.5.over_ref, bf16[512,1280]{1,0:T(8,128)(2,1)} %attention.1.new_ref, pred[]{:T(512)} %eq.33), kind=kLoop, calls=%fused_computation.3 | loop fusion | flops 655360 | bytes 3932161 | tf_op jit(solution)/shard_map/jit(_where)/select_n | solution.py:284
  53.8 2.8 %collective-permute-start.6 = (bf16[512,1280]{1,0:T(8,128)(2,1)}, bf16[512,1280]{1,0:T(8,128)(2,1)}, u32[]{:S(2)}, u32[]{:S(2)}) collective-permute-start(bf16[512,1280]{1,0:T(8,128)(2,1)} %broadcast_select_fusion.1), channel_id=1, source_target_pairs={{0,1},{1,0},{2,3},{3,2},{4,5},{5,4},{6,7},{7,6},{8,9},{9,8},{10,11... | collective-permute-start | bytes 3932168 | tf_op jit(solution)/shard_map/ppermute | solution.py:234
  56.6 2.2 %slice.39 = bf16[1280,384]{1,0:T(8,128)(2,1)} slice(bf16[1280,640]{1,0:T(8,128)(2,1)} %collective-permute-done.4.refs_2_), slice={[0:1280], [0:384]} | slice | bytes 1966080 | tf_op jit(solution)/shard_map/slice | solution.py:247
  58.8 0.8 collective-permute-done.6.other_ref
  59.6 8.4 %product.2 = bf16[512,1280]{1,0:T(8,128)(2,1)} custom-call(s32[1]{0:T(128)S(6)} %reshape.24.pick_ref, bf16[512,1280]{1,0:T(8,128)(2,1)} %attention.1.new_ref, bf16[512,1280]{1,0:T(8,128)(2,1)} %copy-done, bf16[512,1280]{1,0:T(8,128)(2,1)} %collective-permute-done.6.other_ref, bf16[1280,640]{1,0:T(8,128)(2,1)} %refs_0_.1, ...), custom_call_target="tpu_custom_call" | custom-call | flops 1048576 | bytes 1048576 | tf_op jit(solution)/shard_map/product/pallas_call | solution.py:125
  68.0 16.0 %collective-permute-done.11 = bf16[1280,640]{1,0:T(8,128)(2,1)} collective-permute-done((bf16[1280,640]{1,0:T(8,128)(2,1)}, bf16[1280,640]{1,0:T(8,128)(2,1)}, u32[]{:S(2)}, u32[]{:S(2)}) %collective-permute-start.11) | collective-permute-done | bytes 1638432 | tf_op jit(solution)/shard_map/ppermute | solution.py:234
  84.0 1.6 %broadcast_select_fusion = bf16[1280,640]{1,0:T(8,128)(2,1)S(1)} fusion(bf16[1280,640]{1,0:T(8,128)(2,1)} %collective-permute-done.10, bf16[1280,640]{1,0:T(8,128)(2,1)} %collective-permute-done.11, pred[]{:T(512)} %or.3), kind=kLoop, calls=%fused_computation | loop fusion | flops 819200 | bytes 4915201 | tf_op jit(solution)/shard_map/jit(_where)/select_n | solution.py:306
  85.6 1.1 slice.41.refs_0_
  86.6 0.8 collective-permute-start.13
  87.9 1.5 collective-permute-start.12
  89.3 1.4 collective-permute-done.14.refs_3_
  90.7 5.8 %product.3 = bf16[512,640]{1,0:T(8,128)(2,1)} custom-call(s32[1]{0:T(128)S(6)} %reshape.24.pick_ref, bf16[512,1280]{1,0:T(8,128)(2,1)} %attention.1.new_ref, bf16[512,1280]{1,0:T(8,128)(2,1)} %copy-done, bf16[512,1280]{1,0:T(8,128)(2,1)} %collective-permute-done.6.other_ref, bf16[1280,384]{1,0:T(8,128)(2,1)} %slice.41.refs_0_, ...), custom_call_target="tpu_custom_call" | custom-call | flops 1048576 | bytes 1048576 | tf_op jit(solution)/shard_map/product/pallas_call | solution.py:125
  96.5 1.2 broadcast_select_fusion.2
  98.6 1.1 slice.44
  99.7 1.5 collective-permute-start.19
  101.2 12.5 %collective-permute-done.15 = bf16[512,640]{1,0:T(8,128)(2,1)S(1)} collective-permute-done((bf16[512,640]{1,0:T(8,128)(2,1)S(1)}, bf16[512,640]{1,0:T(8,128)(2,1)S(1)}, u32[]{:S(2)}, u32[]{:S(2)}) %collective-permute-start.15) | collective-permute-done | bytes 655392 | tf_op jit(solution)/shard_map/ppermute | solution.py:234
  114.1 0.9 copy-done.6
  115.0 5.1 %split_product.2 = (bf16[512,384]{1,0:T(8,128)(2,1)}, bf16[512,128]{1,0:T(8,128)(2,1)}, bf16[512,128]{1,0:T(8,128)(2,1)}, bf16[512,128]{1,0:T(8,128)(2,1)}) custom-call(s32[2]{0:T(128)} %add_convert_fusion.5.flag_ref, bf16[512,1280]{1,0:T(8,128)(2,1)} %attention.1.new_ref, bf16[512,1280]{1,0:T(8,128)(2,1)} %copy-done, bf16[1280,640]{1,0:T(8,128)(2,1)} %copy-done.2, ...), custom_call_target="tpu_custom_call" | custom-call | flops 1048576 | bytes 1048576 | tf_op jit(solution)/shard_map/split_product/pallas_call | solution.py:184
  120.2 1.3 collective-permute-start.16
  123.2 1.2 broadcast_select_fusion.6
  125.0 1.1 collective-permute-start.20
  126.0 4.9 %split_product.3 = (bf16[512,256]{1,0:T(8,128)(2,1)}, bf16[512,128]{1,0:T(8,128)(2,1)}, bf16[512,128]{1,0:T(8,128)(2,1)}) custom-call(s32[2]{0:T(128)} %add_convert_fusion.5.flag_ref, bf16[512,1280]{1,0:T(8,128)(2,1)} %attention.1.new_ref, bf16[512,1280]{1,0:T(8,128)(2,1)} %copy-done, bf16[1280,640]{1,0:T(8,128)(2,1)} %copy-done.2, bf16[1280,256]{1,0:T(8,128)(2,1)} %copy-done.7), custom_call_target="tpu_custom_call" | custom-call | flops 1048576 | bytes 1048576 | tf_op jit(solution)/shard_map/split_product/pallas_call | solution.py:184
  131.0 2.4 %collective-permute-start.21 = (bf16[512,128]{1,0:T(8,128)(2,1)}, bf16[512,128]{1,0:T(8,128)(2,1)S(1)}, u32[]{:S(2)}, u32[]{:S(2)}) collective-permute-start(bf16[512,128]{1,0:T(8,128)(2,1)} %get-tuple-element.34), channel_id=1, source_target_pairs={{0,1},{1,0},{2,3},{3,2},{4,5},{5,4},{6,7},{7,6},{8,9},{9,8},{10,11... | collective-permute-start | bytes 393224 | tf_op jit(solution)/shard_map/ppermute | solution.py:234
  133.5 1.1 collective-permute-done.21
  135.0 1.0 add_convert_fusion.4
  136.9 1.2 collective-permute-start.24
  138.2 1.7 %collective-permute-start.23 = (bf16[512,384]{1,0:T(8,128)(2,1)S(1)}, bf16[512,384]{1,0:T(8,128)(2,1)S(1)}, u32[]{:S(2)}, u32[]{:S(2)}) collective-permute-start(bf16[512,384]{1,0:T(8,128)(2,1)S(1)} %get-tuple-element.38), channel_id=1, source_target_pairs={{0,2},{1,4},{2,0},{3,6},{4,1},{5,7},{6,3},{7,5},{8,10},{9,12},{10,... | collective-permute-start | bytes 1179656 | tf_op jit(solution)/shard_map/ppermute | solution.py:234
  139.9 3.7 %collective-permute-done.25 = bf16[512,256]{1,0:T(8,128)(2,1)S(1)} collective-permute-done((bf16[512,256]{1,0:T(8,128)(2,1)S(1)}, bf16[512,256]{1,0:T(8,128)(2,1)S(1)}, u32[]{:S(2)}, u32[]{:S(2)}) %collective-permute-start.25) | collective-permute-done | bytes 262176 | tf_op jit(solution)/shard_map/ppermute | solution.py:234
  143.7 1.4 collective-permute-start.27
  145.1 1.9 %collective-permute-start.26 = (bf16[512,256]{1,0:T(8,128)(2,1)S(1)}, bf16[512,256]{1,0:T(8,128)(2,1)S(1)}, u32[]{:S(2)}, u32[]{:S(2)}) collective-permute-start(bf16[512,256]{1,0:T(8,128)(2,1)S(1)} %get-tuple-element.41), channel_id=1, source_target_pairs={{0,2},{1,4},{2,0},{3,6},{4,1},{5,7},{6,3},{7,5},{8,10},{9,12},{10,... | collective-permute-start | bytes 786440 | tf_op jit(solution)/shard_map/ppermute | solution.py:234
  147.0 2.8 %collective-permute-done.23 = bf16[512,384]{1,0:T(8,128)(2,1)S(1)} collective-permute-done((bf16[512,384]{1,0:T(8,128)(2,1)S(1)}, bf16[512,384]{1,0:T(8,128)(2,1)S(1)}, u32[]{:S(2)}, u32[]{:S(2)}) %collective-permute-start.23) | collective-permute-done | bytes 393248 | tf_op jit(solution)/shard_map/ppermute | solution.py:234
  150.0 5.2 %collective-permute-done.26 = bf16[512,256]{1,0:T(8,128)(2,1)S(1)} collective-permute-done((bf16[512,256]{1,0:T(8,128)(2,1)S(1)}, bf16[512,256]{1,0:T(8,128)(2,1)S(1)}, u32[]{:S(2)}, u32[]{:S(2)}) %collective-permute-start.26) | collective-permute-done | bytes 262176 | tf_op jit(solution)/shard_map/ppermute | solution.py:234
  155.2 1.2 pad_maximum_fusion
  (60 shorter events, 7.3 us)
Async XLA Ops:
  0.6 7.5 %collective-permute-start.1 = (bf16[128,256]{1,0:T(8,128)(2,1)}, bf16[128,256]{1,0:T(8,128)(2,1)S(1)}, u32[]{:S(2)}, u32[]{:S(2)}) collective-permute-start(bf16[128,256]{1,0:T(8,128)(2,1)} %param.10), channel_id=1, source_target_pairs={{0,16},{1,17},{2,18},{3,19},{4,20},{5,21},{6,22},{7,23},{8,24},{9,... | collective-permute-start | bytes 196616 | tf_op jit(solution)/shard_map/ppermute | solution.py:234
  3.8 4.3 %collective-permute-start = (bf16[128,256]{1,0:T(8,128)(2,1)}, bf16[128,256]{1,0:T(8,128)(2,1)S(1)}, u32[]{:S(2)}, u32[]{:S(2)}) collective-permute-start(bf16[128,256]{1,0:T(8,128)(2,1)} %param.10), channel_id=1, source_target_pairs={{0,8},{1,9},{2,10},{3,11},{4,12},{5,13},{6,14},{7,15},{8,0},{9,1},... | collective-permute-start | bytes 196616 | tf_op jit(solution)/shard_map/ppermute | solution.py:234
  5.1 5.3 %collective-permute-start.2 = (bf16[128,256]{1,0:T(8,128)(2,1)}, bf16[128,256]{1,0:T(8,128)(2,1)S(1)}, u32[]{:S(2)}, u32[]{:S(2)}) collective-permute-start(bf16[128,256]{1,0:T(8,128)(2,1)} %param.10), channel_id=1, source_target_pairs={{0,24},{1,25},{2,26},{3,27},{4,28},{5,29},{6,30},{7,31},{8,16},{9,... | collective-permute-start | bytes 196616 | tf_op jit(solution)/shard_map/ppermute | solution.py:234
  5.1 39.2 %collective-permute-start.4 = (bf16[1280,640]{1,0:T(8,128)(2,1)}, bf16[1280,640]{1,0:T(8,128)(2,1)}, u32[]{:S(2)}, u32[]{:S(2)}) collective-permute-start(bf16[1280,640]{1,0:T(8,128)(2,1)} %refs_0_.1), channel_id=1, source_target_pairs={{0,8},{1,9},{2,10},{3,11},{4,12},{5,13},{6,14},{7,15},{8,0},{9,1},... | collective-permute-start | bytes 4915208 | tf_op jit(solution)/shard_map/ppermute | solution.py:234
  5.5 40.3 %collective-permute-start.10 = (bf16[1280,640]{1,0:T(8,128)(2,1)}, bf16[1280,640]{1,0:T(8,128)(2,1)}, u32[]{:S(2)}, u32[]{:S(2)}) collective-permute-start(bf16[1280,640]{1,0:T(8,128)(2,1)} %refs_0_.1), channel_id=1, source_target_pairs={{0,1},{1,0},{2,3},{3,2},{4,5},{5,4},{6,7},{7,6},{8,16},{9,17},{10,... | collective-permute-start | bytes 4915208 | tf_op jit(solution)/shard_map/ppermute | solution.py:234
  10.4 5.7 %copy-start.8 = (bf16[512,256]{1,0:T(8,128)(2,1)}, bf16[512,256]{1,0:T(8,128)(2,1)S(1)}, u32[]{:S(2)}) copy-start(bf16[512,256]{1,0:T(8,128)(2,1)S(1)} %constant_dynamic-update-slice_fusion) | copy-start | bytes 786436
  10.4 5.7 %collective-permute-start.3 = (bf16[512,256]{1,0:T(8,128)(2,1)S(1)}, bf16[512,256]{1,0:T(8,128)(2,1)S(1)}, u32[]{:S(2)}, u32[]{:S(2)}) collective-permute-start(bf16[512,256]{1,0:T(8,128)(2,1)S(1)} %constant_dynamic-update-slice_fusion), channel_id=1, source_target_pairs={{0,4},{1,5},{2,6},{3,7},{4,0},{5,1},{6,2},{7,3},{8,12},{9,13},{10,... | collective-permute-start | bytes 786440 | tf_op jit(solution)/shard_map/ppermute | solution.py:234
  16.1 0.7 copy-start.9
  23.1 27.6 %collective-permute-start.5 = (bf16[512,1280]{1,0:T(8,128)(2,1)}, bf16[512,1280]{1,0:T(8,128)(2,1)S(1)}, u32[]{:S(2)}, u32[]{:S(2)}) collective-permute-start(bf16[512,1280]{1,0:T(8,128)(2,1)} %attention.1.new_ref), channel_id=1, source_target_pairs={{0,4},{1,5},{2,6},{3,7},{4,0},{5,1},{6,2},{7,3},{8,12},{9,13},{10,... | collective-permute-start | bytes 3932168 | tf_op jit(solution)/shard_map/ppermute | solution.py:234
  25.1 33.7 %collective-permute-start.7 = (bf16[1280,640]{1,0:T(8,128)(2,1)}, bf16[1280,640]{1,0:T(8,128)(2,1)}, u32[]{:S(2)}, u32[]{:S(2)}) collective-permute-start(bf16[1280,640]{1,0:T(8,128)(2,1)} %refs_0_.1), channel_id=1, source_target_pairs={{0,1},{1,0},{2,3},{3,2},{4,5},{5,4},{6,7},{7,6},{8,9},{9,8},{10,11... | collective-permute-start | bytes 4915208 | tf_op jit(solution)/shard_map/ppermute | solution.py:234
  44.3 23.6 %collective-permute-start.9 = (bf16[1280,640]{1,0:T(8,128)(2,1)}, bf16[1280,640]{1,0:T(8,128)(2,1)S(1)}, u32[]{:S(2)}, u32[]{:S(2)}) collective-permute-start(bf16[1280,640]{1,0:T(8,128)(2,1)} %collective-permute-done.4.refs_2_), channel_id=1, source_target_pairs={{0,1},{1,0},{2,3},{3,2},{4,5},{5,4},{6,7},{7,6},{8,16},{9,17},{10,... | collective-permute-start | bytes 4915208 | tf_op jit(solution)/shard_map/ppermute | solution.py:234
  45.8 13.8 %collective-permute-start.8 = (bf16[1280,640]{1,0:T(8,128)(2,1)}, bf16[1280,640]{1,0:T(8,128)(2,1)}, u32[]{:S(2)}, u32[]{:S(2)}) collective-permute-start(bf16[1280,640]{1,0:T(8,128)(2,1)} %collective-permute-done.4.refs_2_), channel_id=1, source_target_pairs={{0,1},{1,0},{2,3},{3,2},{4,5},{5,4},{6,7},{7,6},{8,9},{9,8},{10,11... | collective-permute-start | bytes 4915208 | tf_op jit(solution)/shard_map/ppermute | solution.py:234
  45.8 38.2 %collective-permute-start.11 = (bf16[1280,640]{1,0:T(8,128)(2,1)}, bf16[1280,640]{1,0:T(8,128)(2,1)}, u32[]{:S(2)}, u32[]{:S(2)}) collective-permute-start(bf16[1280,640]{1,0:T(8,128)(2,1)} %collective-permute-done.10), channel_id=1, source_target_pairs={{0,8},{1,9},{2,10},{3,11},{4,12},{5,13},{6,14},{7,15},{8,0},{9,1},... | collective-permute-start | bytes 4915208 | tf_op jit(solution)/shard_map/ppermute | solution.py:234
  50.7 3.1 %copy-start = (bf16[512,1280]{1,0:T(8,128)(2,1)}, bf16[512,1280]{1,0:T(8,128)(2,1)S(1)}, u32[]{:S(2)}) copy-start(bf16[512,1280]{1,0:T(8,128)(2,1)S(1)} %collective-permute-done.5.over_ref) | copy-start | bytes 3932164
  53.8 5.8 %collective-permute-start.6 = (bf16[512,1280]{1,0:T(8,128)(2,1)}, bf16[512,1280]{1,0:T(8,128)(2,1)}, u32[]{:S(2)}, u32[]{:S(2)}) collective-permute-start(bf16[512,1280]{1,0:T(8,128)(2,1)} %broadcast_select_fusion.1), channel_id=1, source_target_pairs={{0,1},{1,0},{2,3},{3,2},{4,5},{5,4},{6,7},{7,6},{8,9},{9,8},{10,11... | collective-permute-start | bytes 3932168 | tf_op jit(solution)/shard_map/ppermute | solution.py:234
  68.0 17.6 %copy-start.2 = (bf16[1280,640]{1,0:T(8,128)(2,1)}, bf16[1280,640]{1,0:T(8,128)(2,1)S(1)}, u32[]{:S(2)}) copy-start(bf16[1280,640]{1,0:T(8,128)(2,1)S(1)} %collective-permute-done.9.inner_ref) | copy-start | bytes 4915204
  86.6 1.2 copy-start.5
  86.6 4.1 %collective-permute-start.13 = (bf16[1280,384]{1,0:T(8,128)(2,1)}, bf16[1280,384]{1,0:T(8,128)(2,1)}, u32[]{:S(2)}, u32[]{:S(2)}) collective-permute-start(bf16[1280,384]{1,0:T(8,128)(2,1)} %slice.41.refs_0_), channel_id=1, source_target_pairs={{0,1},{1,0},{2,3},{3,2},{4,5},{5,4},{6,7},{7,6},{8,9},{9,8},{10,11... | collective-permute-start | bytes 2949128 | tf_op jit(solution)/shard_map/ppermute | solution.py:234
  87.5 3.2 %copy-start.4 = (bf16[1280,256]{1,0:T(8,128)(2,1)}, bf16[1280,256]{1,0:T(8,128)(2,1)S(1)}, u32[]{:S(2)}) copy-start(bf16[1280,256]{1,0:T(8,128)(2,1)S(1)} %slice.42.refs_2_) | copy-start | bytes 1966084
  87.5 3.2 %collective-permute-start.14 = (bf16[1280,256]{1,0:T(8,128)(2,1)S(1)}, bf16[1280,256]{1,0:T(8,128)(2,1)}, u32[]{:S(2)}, u32[]{:S(2)}) collective-permute-start(bf16[1280,256]{1,0:T(8,128)(2,1)S(1)} %slice.42.refs_2_), channel_id=1, source_target_pairs={{0,1},{1,0},{2,3},{3,2},{4,5},{5,4},{6,7},{7,6},{8,9},{9,8},{10,11... | collective-permute-start | bytes 1966088 | tf_op jit(solution)/shard_map/ppermute | solution.py:234
  87.8 8.7 %copy-start.1 = (bf16[512,1280]{1,0:T(8,128)(2,1)S(1)}, bf16[512,1280]{1,0:T(8,128)(2,1)}, u32[]{:S(2)}) copy-start(bf16[512,1280]{1,0:T(8,128)(2,1)} %product.2) | copy-start | bytes 3932164
  87.9 26.2 %collective-permute-start.12 = (bf16[1280,384]{1,0:T(8,128)(2,1)S(1)}, bf16[1280,384]{1,0:T(8,128)(2,1)S(1)}, u32[]{:S(2)}, u32[]{:S(2)}) collective-permute-start(bf16[1280,384]{1,0:T(8,128)(2,1)S(1)} %copy-done.5), channel_id=1, source_target_pairs={{0,8},{1,9},{2,10},{3,11},{4,12},{5,13},{6,14},{7,15},{8,24},{9,25... | collective-permute-start | bytes 2949128 | tf_op jit(solution)/shard_map/ppermute | solution.py:234
  96.5 17.3 %copy-start.3 = (bf16[512,640]{1,0:T(8,128)(2,1)S(1)}, bf16[512,640]{1,0:T(8,128)(2,1)}, u32[]{:S(2)}) copy-start(bf16[512,640]{1,0:T(8,128)(2,1)} %product.3) | copy-start | bytes 1966084
  97.8 16.0 %collective-permute-start.15 = (bf16[512,640]{1,0:T(8,128)(2,1)S(1)}, bf16[512,640]{1,0:T(8,128)(2,1)S(1)}, u32[]{:S(2)}, u32[]{:S(2)}) collective-permute-start(bf16[512,640]{1,0:T(8,128)(2,1)S(1)} %broadcast_select_fusion.2), channel_id=1, source_target_pairs={{0,2},{1,3},{2,0},{3,1},{4,6},{5,7},{6,4},{7,5},{8,10},{9,11},{10,... | collective-permute-start | bytes 1966088 | tf_op jit(solution)/shard_map/ppermute | solution.py:234
  99.7 25.3 %collective-permute-start.19 = (bf16[1280,256]{1,0:T(8,128)(2,1)S(1)}, bf16[1280,256]{1,0:T(8,128)(2,1)S(1)}, u32[]{:S(2)}, u32[]{:S(2)}) collective-permute-start(bf16[1280,256]{1,0:T(8,128)(2,1)S(1)} %slice.44), channel_id=1, source_target_pairs={{0,8},{1,9},{2,10},{3,11},{4,12},{5,13},{6,14},{7,15},{8,24},{9,25... | collective-permute-start | bytes 1966088 | tf_op jit(solution)/shard_map/ppermute | solution.py:234
  114.1 0.9 copy-start.6
  120.2 2.5 %collective-permute-start.16 = (bf16[512,128]{1,0:T(8,128)(2,1)}, bf16[512,128]{1,0:T(8,128)(2,1)S(1)}, u32[]{:S(2)}, u32[]{:S(2)}) collective-permute-start(bf16[512,128]{1,0:T(8,128)(2,1)} %get-tuple-element.26), channel_id=1, source_target_pairs={{0,1},{1,0},{2,3},{3,2},{4,5},{5,4},{6,7},{7,6},{8,9},{9,8},{10,11... | collective-permute-start | bytes 393224 | tf_op jit(solution)/shard_map/ppermute | solution.py:234
  121.4 1.6 collective-permute-start.17
  121.5 1.7 %collective-permute-start.18 = (bf16[512,128]{1,0:T(8,128)(2,1)}, bf16[512,128]{1,0:T(8,128)(2,1)S(1)}, u32[]{:S(2)}, u32[]{:S(2)}) collective-permute-start(bf16[512,128]{1,0:T(8,128)(2,1)} %get-tuple-element.28), channel_id=1, source_target_pairs={{0,1},{1,0},{2,3},{3,2},{4,5},{5,4},{6,7},{7,6},{8,9},{9,8},{10,11... | collective-permute-start | bytes 393224 | tf_op jit(solution)/shard_map/ppermute | solution.py:234
  125.0 1.1 copy-start.7
  125.0 11.0 %collective-permute-start.20 = (bf16[512,384]{1,0:T(8,128)(2,1)S(1)}, bf16[512,384]{1,0:T(8,128)(2,1)S(1)}, u32[]{:S(2)}, u32[]{:S(2)}) collective-permute-start(bf16[512,384]{1,0:T(8,128)(2,1)S(1)} %get-tuple-element.31), channel_id=1, source_target_pairs={{0,2},{1,3},{2,0},{3,1},{4,6},{5,7},{6,4},{7,5},{8,10},{9,11},{10,... | collective-permute-start | bytes 1179656 | tf_op jit(solution)/shard_map/ppermute | solution.py:234
  131.0 3.6 %collective-permute-start.21 = (bf16[512,128]{1,0:T(8,128)(2,1)}, bf16[512,128]{1,0:T(8,128)(2,1)S(1)}, u32[]{:S(2)}, u32[]{:S(2)}) collective-permute-start(bf16[512,128]{1,0:T(8,128)(2,1)} %get-tuple-element.34), channel_id=1, source_target_pairs={{0,1},{1,0},{2,3},{3,2},{4,5},{5,4},{6,7},{7,6},{8,9},{9,8},{10,11... | collective-permute-start | bytes 393224 | tf_op jit(solution)/shard_map/ppermute | solution.py:234
  133.4 1.6 collective-permute-start.22
  136.1 7.4 %collective-permute-start.25 = (bf16[512,256]{1,0:T(8,128)(2,1)S(1)}, bf16[512,256]{1,0:T(8,128)(2,1)S(1)}, u32[]{:S(2)}, u32[]{:S(2)}) collective-permute-start(bf16[512,256]{1,0:T(8,128)(2,1)S(1)} %broadcast_select_fusion.14), channel_id=1, source_target_pairs={{0,2},{1,3},{2,0},{3,1},{4,6},{5,7},{6,4},{7,5},{8,10},{9,11},{10,... | collective-permute-start | bytes 786440 | tf_op jit(solution)/shard_map/ppermute | solution.py:234
  136.9 10.1 %collective-permute-start.24 = (bf16[512,384]{1,0:T(8,128)(2,1)S(1)}, bf16[512,384]{1,0:T(8,128)(2,1)S(1)}, u32[]{:S(2)}, u32[]{:S(2)}) collective-permute-start(bf16[512,384]{1,0:T(8,128)(2,1)S(1)} %broadcast_select_fusion.3), channel_id=1, source_target_pairs={{0,1},{1,5},{2,3},{3,7},{4,0},{5,4},{6,2},{7,6},{8,9},{9,13},{10,1... | collective-permute-start | bytes 1179656 | tf_op jit(solution)/shard_map/ppermute | solution.py:234
  138.2 11.7 %collective-permute-start.23 = (bf16[512,384]{1,0:T(8,128)(2,1)S(1)}, bf16[512,384]{1,0:T(8,128)(2,1)S(1)}, u32[]{:S(2)}, u32[]{:S(2)}) collective-permute-start(bf16[512,384]{1,0:T(8,128)(2,1)S(1)} %get-tuple-element.38), channel_id=1, source_target_pairs={{0,2},{1,4},{2,0},{3,6},{4,1},{5,7},{6,3},{7,5},{8,10},{9,12},{10,... | collective-permute-start | bytes 1179656 | tf_op jit(solution)/shard_map/ppermute | solution.py:234
  143.7 6.3 %collective-permute-start.27 = (bf16[512,256]{1,0:T(8,128)(2,1)S(1)}, bf16[512,256]{1,0:T(8,128)(2,1)S(1)}, u32[]{:S(2)}, u32[]{:S(2)}) collective-permute-start(bf16[512,256]{1,0:T(8,128)(2,1)S(1)} %broadcast_select_fusion.11), channel_id=1, source_target_pairs={{0,1},{1,5},{2,3},{3,7},{4,0},{5,4},{6,2},{7,6},{8,9},{9,13},{10,1... | collective-permute-start | bytes 786440 | tf_op jit(solution)/shard_map/ppermute | solution.py:234
  145.1 10.1 %collective-permute-start.26 = (bf16[512,256]{1,0:T(8,128)(2,1)S(1)}, bf16[512,256]{1,0:T(8,128)(2,1)S(1)}, u32[]{:S(2)}, u32[]{:S(2)}) collective-permute-start(bf16[512,256]{1,0:T(8,128)(2,1)S(1)} %get-tuple-element.41), channel_id=1, source_target_pairs={{0,2},{1,4},{2,0},{3,6},{4,1},{5,7},{6,3},{7,5},{8,10},{9,12},{10,... | collective-permute-start | bytes 786440 | tf_op jit(solution)/shard_map/ppermute | solution.py:234

commit v5 on v4

--- a/solution.py
+++ b/solution.py
@@ -141,10 +141,10 @@
 
 def split_product_kernel(column, flag_ref, new_ref, over_ref, inner_ref, end_ref, keep_ref, *refs):
     *pass_refs, left, right, loaded = refs
-    width = end_ref.shape[1]
+    rows, width = new_ref.shape[0], end_ref.shape[1]
 
     def load_left(i, source):
-        return pltpu.make_async_copy(source, left.at[i], loaded.at[i])
+        return pltpu.make_async_copy(source, left.at[i * rows:(i + 1) * rows], loaded.at[i])
 
     def load_right(source):
         return pltpu.make_async_copy(source, right, loaded.at[2])
@@ -170,25 +170,26 @@
         load_right(end_ref).start()
 
     load_right(end_ref).wait()
+    load_left(0, new_ref).wait()
     load_left(1, new_ref).wait()
-    passed = jnp.dot(left[1], right[...], preferred_element_type=jnp.float32).astype(jnp.bfloat16)
+    both = jnp.dot(left[...], right[...], preferred_element_type=jnp.float32).astype(jnp.bfloat16)
+    keep_ref[...] = both[:rows]
     for i, pass_ref in enumerate(pass_refs):
-        pass_ref[...] = passed[:, i * BLK:(i + 1) * BLK]
-    load_left(0, new_ref).wait()
-    keep_ref[...] = jnp.dot(left[0], right[...], preferred_element_type=jnp.float32).astype(jnp.bfloat16)
-
-
-def split_product(flags, lefts, inner_block, end_block, column):
+        piece = pass_ref.shape[1]
+        pass_ref[...] = both[rows:, i * piece:(i + 1) * piece]
+
+
+def split_product(flags, lefts, inner_block, end_block, column, piece):
     rows, depth = lefts[0].shape
     width = end_block.shape[1]
     return pl.pallas_call(
         functools.partial(split_product_kernel, column),
         out_shape=[jax.ShapeDtypeStruct((rows, width), jnp.bfloat16)]
-        + [jax.ShapeDtypeStruct((rows, BLK), jnp.bfloat16)] * (width // BLK),
+        + [jax.ShapeDtypeStruct((rows, piece), jnp.bfloat16)] * (width // piece),
         in_specs=[pl.BlockSpec(memory_space=pltpu.SMEM)] + [pl.BlockSpec(memory_space=pl.ANY)] * 4,
-        out_specs=[pl.BlockSpec(memory_space=pltpu.VMEM)] * (1 + width // BLK),
+        out_specs=[pl.BlockSpec(memory_space=pltpu.VMEM)] * (1 + width // piece),
         scratch_shapes=[
-            pltpu.VMEM((2, rows, depth), jnp.bfloat16),
+            pltpu.VMEM((2 * rows, depth), jnp.bfloat16),
             pltpu.VMEM((depth, width), jnp.bfloat16),
             pltpu.SemaphoreType.DMA((3,)),
         ],
@@ -290,7 +291,7 @@
         return block, to_core(block)
 
     def both_cores(inner_block, end_block, column):
-        kept, *passed = split_product(flags, rows[:2], inner_block, end_block, column)
+        kept, *passed = split_product(flags, rows[:2], inner_block, end_block, column, BLK if column == 0 else end_block.shape[1])
         return add(kept, jnp.concatenate([to_core(v) for v in passed], axis=1))
 
     def to_sum(p_half, p_cross):

time: 157 us -> 164 us (1.045)
  waiting for transfers between devices: 68.4 us -> 75.1 us
  Pallas kernels: 30.5 us -> 28.5 us
  starting transfers between devices: 36.5 us -> 38.3 us
    ppermute x28 -> x27, waiting for transfers between devices: 68.4 us -> 75.1 us  [move(): return lax.ppermute(value, BOTH, pairs)]
    ppermute x28 -> x27, starting transfers between devices: 36.5 us -> 38.3 us  [move(): return lax.ppermute(value, BOTH, pairs)]
  transfers between devices with their start and end apart: 28 -> 27, of which waited for: 17 -> 18; matrix products, arithmetic and copies ran while one was open for 9% -> 9% of each run, Pallas kernels for 19% -> 15%
where the time goes in v5:
time: 164 us
  waiting for transfers between devices  75.1 us (46%)
  starting transfers between devices  38.3 us (23%)
  Pallas kernels  28.5 us (17%)
  other arithmetic  11.9 us (7%)
  local copies, waits for them, and re-layouts  8.8 us (5%)
    ppermute x27, waiting for transfers between devices, move(): return lax.ppermute(value, BOTH, pairs)  75.1 us
    ppermute x27, starting transfers between devices, move(): return lax.ppermute(value, BOTH, pairs)  38.3 us
    pallas_call x2, Pallas kernels, product(): pl.pallas_call(functools.partial(product_kernel, len(rights)), out_shape=...  14.1 us
    pallas_call x2, Pallas kernels, split_product(): pl.pallas_call(functools.partial(split_product_kernel, column), out_shape...  9.09 us
    pallas_call x1, Pallas kernels, refresh(): pl.pallas_call(attention_kernel, out_shape=jax.ShapeDtypeStruct(out_old.s...  5.29 us
    slice x4, local copies, waits for them, and re-layouts, columns(): parts.append(value[:, at:at + width])  4.46 us
    unnamed x23, local copies, waits for them, and re-layouts  3.57 us
  transfers between devices with their start and end apart: 27, of which 18 were waited for; matrix products, arithmetic and copies ran while one was open for 9% of the time, Pallas kernels for 15%

profile of v5, /device:TPU:1, one launch (start us, length us, event | category | flops | bytes accessed | tf_op | source)
XLA Modules:
  0.0 163.5 jit_solution(768408121727336446)
XLA Ops:
  0.6 3.2 %collective-permute-start.1 = (bf16[128,256]{1,0:T(8,128)(2,1)}, bf16[128,256]{1,0:T(8,128)(2,1)S(1)}, u32[]{:S(2)}, u32[]{:S(2)}) collective-permute-start(bf16[128,256]{1,0:T(8,128)(2,1)} %param.10), channel_id=1, source_target_pairs={{0,16},{1,17},{2,18},{3,19},{4,20},{5,21},{6,22},{7,23},{8,24},{9,... | collective-permute-start | bytes 196616 | tf_op jit(solution)/shard_map/ppermute | solution.py:235
  3.8 1.3 collective-permute-start
  5.5 1.8 %collective-permute-start.10 = (bf16[1280,640]{1,0:T(8,128)(2,1)}, bf16[1280,640]{1,0:T(8,128)(2,1)}, u32[]{:S(2)}, u32[]{:S(2)}) collective-permute-start(bf16[1280,640]{1,0:T(8,128)(2,1)} %refs_0_.1), channel_id=1, source_target_pairs={{0,1},{1,0},{2,3},{3,2},{4,5},{5,4},{6,7},{7,6},{8,16},{9,17},{10,... | collective-permute-start | bytes 4915208 | tf_op jit(solution)/shard_map/ppermute | solution.py:235
  7.3 0.8 constant_dynamic-update-slice_fusion.3
  8.1 2.3 %collective-permute-done.2 = bf16[128,256]{1,0:T(8,128)(2,1)S(1)} collective-permute-done((bf16[128,256]{1,0:T(8,128)(2,1)}, bf16[128,256]{1,0:T(8,128)(2,1)S(1)}, u32[]{:S(2)}, u32[]{:S(2)}) %collective-permute-start.2) | collective-permute-done | bytes 65568 | tf_op jit(solution)/shard_map/ppermute | solution.py:235
  10.4 1.3 collective-permute-start.3
  12.5 1.2 select_reduce_fusion.slot_ref
  13.7 2.4 %collective-permute-done.3 = bf16[512,256]{1,0:T(8,128)(2,1)S(1)} collective-permute-done((bf16[512,256]{1,0:T(8,128)(2,1)S(1)}, bf16[512,256]{1,0:T(8,128)(2,1)S(1)}, u32[]{:S(2)}, u32[]{:S(2)}) %collective-permute-start.3) | collective-permute-done | bytes 262176 | tf_op jit(solution)/shard_map/ppermute | solution.py:235
  16.8 5.3 %attention.1.new_ref = bf16[512,1280]{1,0:T(8,128)(2,1)} custom-call(s32[32]{0:T(128)} %select_reduce_fusion.slot_ref, bf16[4,10,8,128,128]{4,3,2,1,0:T(8,128)(2,1)} %probs_ref.1, bf16[512,1280]{1,0:T(8,128)(2,1)} %old_ref.1, bf16[4,128,256]{2,1,0:T(8,128)(2,1)} %bitcast.4, bf16[4,128,256]{2,1,0:T(8,128)(2,1)} %bitcast.5), custom_call_target="tpu_custom_call" | custom-call | flops 1048576 | bytes 1048576 | tf_op jit(solution)/shard_map/attention/pallas_call | solution.py:68
  22.1 3.0 %collective-permute-start.5 = (bf16[512,1280]{1,0:T(8,128)(2,1)}, bf16[512,1280]{1,0:T(8,128)(2,1)S(1)}, u32[]{:S(2)}, u32[]{:S(2)}) collective-permute-start(bf16[512,1280]{1,0:T(8,128)(2,1)} %attention.1.new_ref), channel_id=1, source_target_pairs={{0,4},{1,5},{2,6},{3,7},{4,0},{5,1},{6,2},{7,3},{8,12},{9,13},{10,... | collective-permute-start | bytes 3932168 | tf_op jit(solution)/shard_map/ppermute | solution.py:235
  25.1 4.0 %collective-permute-start.7 = (bf16[1280,640]{1,0:T(8,128)(2,1)}, bf16[1280,640]{1,0:T(8,128)(2,1)}, u32[]{:S(2)}, u32[]{:S(2)}) collective-permute-start(bf16[1280,640]{1,0:T(8,128)(2,1)} %refs_0_.1), channel_id=1, source_target_pairs={{0,1},{1,0},{2,3},{3,2},{4,5},{5,4},{6,7},{7,6},{8,9},{9,8},{10,11... | collective-permute-start | bytes 4915208 | tf_op jit(solution)/shard_map/ppermute | solution.py:235
  29.1 15.2 %collective-permute-done.4.refs_2_ = bf16[1280,640]{1,0:T(8,128)(2,1)} collective-permute-done((bf16[1280,640]{1,0:T(8,128)(2,1)}, bf16[1280,640]{1,0:T(8,128)(2,1)}, u32[]{:S(2)}, u32[]{:S(2)}) %collective-permute-start.4) | collective-permute-done | bytes 1638432 | tf_op jit(solution)/shard_map/ppermute | solution.py:235
  44.3 1.5 collective-permute-start.9
  45.8 1.9 %collective-permute-start.11 = (bf16[1280,640]{1,0:T(8,128)(2,1)}, bf16[1280,640]{1,0:T(8,128)(2,1)}, u32[]{:S(2)}, u32[]{:S(2)}) collective-permute-start(bf16[1280,640]{1,0:T(8,128)(2,1)} %collective-permute-done.10), channel_id=1, source_target_pairs={{0,8},{1,9},{2,10},{3,11},{4,12},{5,13},{6,14},{7,15},{8,0},{9,1},... | collective-permute-start | bytes 4915208 | tf_op jit(solution)/shard_map/ppermute | solution.py:235
  47.7 3.1 %collective-permute-done.5.over_ref = bf16[512,1280]{1,0:T(8,128)(2,1)S(1)} collective-permute-done((bf16[512,1280]{1,0:T(8,128)(2,1)}, bf16[512,1280]{1,0:T(8,128)(2,1)S(1)}, u32[]{:S(2)}, u32[]{:S(2)}) %collective-permute-start.5) | collective-permute-done | bytes 1310752 | tf_op jit(solution)/shard_map/ppermute | solution.py:235
  50.8 3.0 %broadcast_select_fusion.1 = bf16[512,1280]{1,0:T(8,128)(2,1)} fusion(bf16[512,1280]{1,0:T(8,128)(2,1)S(1)} %collective-permute-done.5.over_ref, bf16[512,1280]{1,0:T(8,128)(2,1)} %attention.1.new_ref, pred[]{:T(512)} %eq.33), kind=kLoop, calls=%fused_computation.3 | loop fusion | flops 655360 | bytes 3932161 | tf_op jit(solution)/shard_map/jit(_where)/select_n | solution.py:285
  53.8 2.7 %collective-permute-start.6 = (bf16[512,1280]{1,0:T(8,128)(2,1)}, bf16[512,1280]{1,0:T(8,128)(2,1)}, u32[]{:S(2)}, u32[]{:S(2)}) collective-permute-start(bf16[512,1280]{1,0:T(8,128)(2,1)} %broadcast_select_fusion.1), channel_id=1, source_target_pairs={{0,1},{1,0},{2,3},{3,2},{4,5},{5,4},{6,7},{7,6},{8,9},{9,8},{10,11... | collective-permute-start | bytes 3932168 | tf_op jit(solution)/shard_map/ppermute | solution.py:235
  56.6 2.2 %slice.39 = bf16[1280,384]{1,0:T(8,128)(2,1)} slice(bf16[1280,640]{1,0:T(8,128)(2,1)} %collective-permute-done.4.refs_2_), slice={[0:1280], [0:384]} | slice | bytes 1966080 | tf_op jit(solution)/shard_map/slice | solution.py:248
  59.6 8.4 %product.2 = bf16[512,1280]{1,0:T(8,128)(2,1)} custom-call(s32[1]{0:T(128)S(6)} %reshape.24.pick_ref, bf16[512,1280]{1,0:T(8,128)(2,1)} %attention.1.new_ref, bf16[512,1280]{1,0:T(8,128)(2,1)} %copy-done, bf16[512,1280]{1,0:T(8,128)(2,1)} %collective-permute-done.6.other_ref, bf16[1280,640]{1,0:T(8,128)(2,1)} %refs_0_.1, ...), custom_call_target="tpu_custom_call" | custom-call | flops 1048576 | bytes 1048576 | tf_op jit(solution)/shard_map/product/pallas_call | solution.py:125
  68.0 16.0 %collective-permute-done.11 = bf16[1280,640]{1,0:T(8,128)(2,1)} collective-permute-done((bf16[1280,640]{1,0:T(8,128)(2,1)}, bf16[1280,640]{1,0:T(8,128)(2,1)}, u32[]{:S(2)}, u32[]{:S(2)}) %collective-permute-start.11) | collective-permute-done | bytes 1638432 | tf_op jit(solution)/shard_map/ppermute | solution.py:235
  84.0 1.6 broadcast_select_fusion
  85.6 1.0 slice.41.refs_0_
  87.8 1.5 collective-permute-start.12
  89.3 1.4 collective-permute-done.14.refs_3_
  90.7 5.8 %product.3 = bf16[512,640]{1,0:T(8,128)(2,1)} custom-call(s32[1]{0:T(128)S(6)} %reshape.24.pick_ref, bf16[512,1280]{1,0:T(8,128)(2,1)} %attention.1.new_ref, bf16[512,1280]{1,0:T(8,128)(2,1)} %copy-done, bf16[512,1280]{1,0:T(8,128)(2,1)} %collective-permute-done.6.other_ref, bf16[1280,384]{1,0:T(8,128)(2,1)} %slice.41.refs_0_, ...), custom_call_target="tpu_custom_call" | custom-call | flops 1048576 | bytes 1048576 | tf_op jit(solution)/shard_map/product/pallas_call | solution.py:125
  96.5 1.2 broadcast_select_fusion.2
  98.5 1.1 slice.44
  99.6 1.5 collective-permute-start.19
  101.1 12.6 %collective-permute-done.15 = bf16[512,640]{1,0:T(8,128)(2,1)S(1)} collective-permute-done((bf16[512,640]{1,0:T(8,128)(2,1)S(1)}, bf16[512,640]{1,0:T(8,128)(2,1)S(1)}, u32[]{:S(2)}, u32[]{:S(2)}) %collective-permute-start.15) | collective-permute-done | bytes 655392 | tf_op jit(solution)/shard_map/ppermute | solution.py:235
  114.0 0.9 copy-done.6
  115.0 5.0 %split_product.2 = (bf16[512,384]{1,0:T(8,128)(2,1)}, bf16[512,128]{1,0:T(8,128)(2,1)}, bf16[512,128]{1,0:T(8,128)(2,1)}, bf16[512,128]{1,0:T(8,128)(2,1)}) custom-call(s32[2]{0:T(128)} %add_convert_fusion.5.flag_ref, bf16[512,1280]{1,0:T(8,128)(2,1)} %attention.1.new_ref, bf16[512,1280]{1,0:T(8,128)(2,1)} %copy-done, bf16[1280,640]{1,0:T(8,128)(2,1)} %copy-done.2, ...), custom_call_target="tpu_custom_call" | custom-call | flops 1048576 | bytes 1048576 | tf_op jit(solution)/shard_map/split_product/pallas_call | solution.py:185
  120.0 1.3 collective-permute-start.16
  123.0 1.2 broadcast_select_fusion.6
  125.0 0.8 copy-done.7
  125.8 4.1 %split_product.3 = (bf16[512,256]{1,0:T(8,128)(2,1)}, bf16[512,256]{1,0:T(8,128)(2,1)}) custom-call(s32[2]{0:T(128)} %add_convert_fusion.5.flag_ref, bf16[512,1280]{1,0:T(8,128)(2,1)} %attention.1.new_ref, bf16[512,1280]{1,0:T(8,128)(2,1)} %copy-done, bf16[1280,640]{1,0:T(8,128)(2,1)} %copy-done.2, bf16[1280,256]{1,0:T(8,128)(2,1)} %copy-done.7), custom_call_target="tpu_custom_call" | custom-call | flops 1048576 | bytes 1048576 | tf_op jit(solution)/shard_map/split_product/pallas_call | solution.py:185
  130.0 2.0 %collective-permute-start.21 = (bf16[512,256]{1,0:T(8,128)(2,1)}, bf16[512,256]{1,0:T(8,128)(2,1)S(1)}, u32[]{:S(2)}, u32[]{:S(2)}) collective-permute-start(bf16[512,256]{1,0:T(8,128)(2,1)} %get-tuple-element.33), channel_id=1, source_target_pairs={{0,1},{1,0},{2,3},{3,2},{4,5},{5,4},{6,7},{7,6},{8,9},{9,8},{10,11... | collective-permute-start | bytes 786440 | tf_op jit(solution)/shard_map/ppermute | solution.py:235
  132.0 1.2 collective-permute-start.20
  133.4 1.0 add_convert_fusion.4
  134.4 8.3 %collective-permute-done.20 = bf16[512,384]{1,0:T(8,128)(2,1)S(1)} collective-permute-done((bf16[512,384]{1,0:T(8,128)(2,1)S(1)}, bf16[512,384]{1,0:T(8,128)(2,1)S(1)}, u32[]{:S(2)}, u32[]{:S(2)}) %collective-permute-start.20) | collective-permute-done | bytes 393248 | tf_op jit(solution)/shard_map/ppermute | solution.py:235
  142.8 1.2 collective-permute-start.24
  144.2 1.2 collective-permute-start.23
  145.4 1.5 collective-permute-start.22
  147.0 2.9 %collective-permute-done.24 = bf16[512,256]{1,0:T(8,128)(2,1)S(1)} collective-permute-done((bf16[512,256]{1,0:T(8,128)(2,1)S(1)}, bf16[512,256]{1,0:T(8,128)(2,1)S(1)}, u32[]{:S(2)}, u32[]{:S(2)}) %collective-permute-start.24) | collective-permute-done | bytes 262176 | tf_op jit(solution)/shard_map/ppermute | solution.py:235
  150.0 1.1 collective-permute-start.26
  151.1 3.1 %collective-permute-start.25 = (bf16[512,256]{1,0:T(8,128)(2,1)S(1)}, bf16[512,256]{1,0:T(8,128)(2,1)S(1)}, u32[]{:S(2)}, u32[]{:S(2)}) collective-permute-start(bf16[512,256]{1,0:T(8,128)(2,1)S(1)} %get-tuple-element.39), channel_id=1, source_target_pairs={{0,2},{1,4},{2,0},{3,6},{4,1},{5,7},{6,3},{7,5},{8,10},{9,12},{10,... | collective-permute-start | bytes 786440 | tf_op jit(solution)/shard_map/ppermute | solution.py:235
  154.2 2.8 %collective-permute-done.22 = bf16[512,384]{1,0:T(8,128)(2,1)S(1)} collective-permute-done((bf16[512,384]{1,0:T(8,128)(2,1)S(1)}, bf16[512,384]{1,0:T(8,128)(2,1)S(1)}, u32[]{:S(2)}, u32[]{:S(2)}) %collective-permute-start.22) | collective-permute-done | bytes 393248 | tf_op jit(solution)/shard_map/ppermute | solution.py:235
  157.2 5.1 %collective-permute-done.25 = bf16[512,256]{1,0:T(8,128)(2,1)S(1)} collective-permute-done((bf16[512,256]{1,0:T(8,128)(2,1)S(1)}, bf16[512,256]{1,0:T(8,128)(2,1)S(1)}, u32[]{:S(2)}, u32[]{:S(2)}) %collective-permute-start.25) | collective-permute-done | bytes 262176 | tf_op jit(solution)/shard_map/ppermute | solution.py:235
  162.3 1.2 pad_maximum_fusion
  (58 shorter events, 8.2 us)
Async XLA Ops:
  0.6 7.5 %collective-permute-start.1 = (bf16[128,256]{1,0:T(8,128)(2,1)}, bf16[128,256]{1,0:T(8,128)(2,1)S(1)}, u32[]{:S(2)}, u32[]{:S(2)}) collective-permute-start(bf16[128,256]{1,0:T(8,128)(2,1)} %param.10), channel_id=1, source_target_pairs={{0,16},{1,17},{2,18},{3,19},{4,20},{5,21},{6,22},{7,23},{8,24},{9,... | collective-permute-start | bytes 196616 | tf_op jit(solution)/shard_map/ppermute | solution.py:235
  3.8 4.3 %collective-permute-start = (bf16[128,256]{1,0:T(8,128)(2,1)}, bf16[128,256]{1,0:T(8,128)(2,1)S(1)}, u32[]{:S(2)}, u32[]{:S(2)}) collective-permute-start(bf16[128,256]{1,0:T(8,128)(2,1)} %param.10), channel_id=1, source_target_pairs={{0,8},{1,9},{2,10},{3,11},{4,12},{5,13},{6,14},{7,15},{8,0},{9,1},... | collective-permute-start | bytes 196616 | tf_op jit(solution)/shard_map/ppermute | solution.py:235
  5.1 5.3 %collective-permute-start.2 = (bf16[128,256]{1,0:T(8,128)(2,1)}, bf16[128,256]{1,0:T(8,128)(2,1)S(1)}, u32[]{:S(2)}, u32[]{:S(2)}) collective-permute-start(bf16[128,256]{1,0:T(8,128)(2,1)} %param.10), channel_id=1, source_target_pairs={{0,24},{1,25},{2,26},{3,27},{4,28},{5,29},{6,30},{7,31},{8,16},{9,... | collective-permute-start | bytes 196616 | tf_op jit(solution)/shard_map/ppermute | solution.py:235
  5.1 39.2 %collective-permute-start.4 = (bf16[1280,640]{1,0:T(8,128)(2,1)}, bf16[1280,640]{1,0:T(8,128)(2,1)}, u32[]{:S(2)}, u32[]{:S(2)}) collective-permute-start(bf16[1280,640]{1,0:T(8,128)(2,1)} %refs_0_.1), channel_id=1, source_target_pairs={{0,8},{1,9},{2,10},{3,11},{4,12},{5,13},{6,14},{7,15},{8,0},{9,1},... | collective-permute-start | bytes 4915208 | tf_op jit(solution)/shard_map/ppermute | solution.py:235
  5.5 40.3 %collective-permute-start.10 = (bf16[1280,640]{1,0:T(8,128)(2,1)}, bf16[1280,640]{1,0:T(8,128)(2,1)}, u32[]{:S(2)}, u32[]{:S(2)}) collective-permute-start(bf16[1280,640]{1,0:T(8,128)(2,1)} %refs_0_.1), channel_id=1, source_target_pairs={{0,1},{1,0},{2,3},{3,2},{4,5},{5,4},{6,7},{7,6},{8,16},{9,17},{10,... | collective-permute-start | bytes 4915208 | tf_op jit(solution)/shard_map/ppermute | solution.py:235
  10.4 5.7 %copy-start.8 = (bf16[512,256]{1,0:T(8,128)(2,1)}, bf16[512,256]{1,0:T(8,128)(2,1)S(1)}, u32[]{:S(2)}) copy-start(bf16[512,256]{1,0:T(8,128)(2,1)S(1)} %constant_dynamic-update-slice_fusion) | copy-start | bytes 786436
  10.4 5.7 %collective-permute-start.3 = (bf16[512,256]{1,0:T(8,128)(2,1)S(1)}, bf16[512,256]{1,0:T(8,128)(2,1)S(1)}, u32[]{:S(2)}, u32[]{:S(2)}) collective-permute-start(bf16[512,256]{1,0:T(8,128)(2,1)S(1)} %constant_dynamic-update-slice_fusion), channel_id=1, source_target_pairs={{0,4},{1,5},{2,6},{3,7},{4,0},{5,1},{6,2},{7,3},{8,12},{9,13},{10,... | collective-permute-start | bytes 786440 | tf_op jit(solution)/shard_map/ppermute | solution.py:235
  16.1 0.7 copy-start.9
  22.1 28.7 %collective-permute-start.5 = (bf16[512,1280]{1,0:T(8,128)(2,1)}, bf16[512,1280]{1,0:T(8,128)(2,1)S(1)}, u32[]{:S(2)}, u32[]{:S(2)}) collective-permute-start(bf16[512,1280]{1,0:T(8,128)(2,1)} %attention.1.new_ref), channel_id=1, source_target_pairs={{0,4},{1,5},{2,6},{3,7},{4,0},{5,1},{6,2},{7,3},{8,12},{9,13},{10,... | collective-permute-start | bytes 3932168 | tf_op jit(solution)/shard_map/ppermute | solution.py:235
  25.1 33.7 %collective-permute-start.7 = (bf16[1280,640]{1,0:T(8,128)(2,1)}, bf16[1280,640]{1,0:T(8,128)(2,1)}, u32[]{:S(2)}, u32[]{:S(2)}) collective-permute-start(bf16[1280,640]{1,0:T(8,128)(2,1)} %refs_0_.1), channel_id=1, source_target_pairs={{0,1},{1,0},{2,3},{3,2},{4,5},{5,4},{6,7},{7,6},{8,9},{9,8},{10,11... | collective-permute-start | bytes 4915208 | tf_op jit(solution)/shard_map/ppermute | solution.py:235
  44.3 23.6 %collective-permute-start.9 = (bf16[1280,640]{1,0:T(8,128)(2,1)}, bf16[1280,640]{1,0:T(8,128)(2,1)S(1)}, u32[]{:S(2)}, u32[]{:S(2)}) collective-permute-start(bf16[1280,640]{1,0:T(8,128)(2,1)} %collective-permute-done.4.refs_2_), channel_id=1, source_target_pairs={{0,1},{1,0},{2,3},{3,2},{4,5},{5,4},{6,7},{7,6},{8,16},{9,17},{10,... | collective-permute-start | bytes 4915208 | tf_op jit(solution)/shard_map/ppermute | solution.py:235
  45.8 13.8 %collective-permute-start.8 = (bf16[1280,640]{1,0:T(8,128)(2,1)}, bf16[1280,640]{1,0:T(8,128)(2,1)}, u32[]{:S(2)}, u32[]{:S(2)}) collective-permute-start(bf16[1280,640]{1,0:T(8,128)(2,1)} %collective-permute-done.4.refs_2_), channel_id=1, source_target_pairs={{0,1},{1,0},{2,3},{3,2},{4,5},{5,4},{6,7},{7,6},{8,9},{9,8},{10,11... | collective-permute-start | bytes 4915208 | tf_op jit(solution)/shard_map/ppermute | solution.py:235
  45.8 38.2 %collective-permute-start.11 = (bf16[1280,640]{1,0:T(8,128)(2,1)}, bf16[1280,640]{1,0:T(8,128)(2,1)}, u32[]{:S(2)}, u32[]{:S(2)}) collective-permute-start(bf16[1280,640]{1,0:T(8,128)(2,1)} %collective-permute-done.10), channel_id=1, source_target_pairs={{0,8},{1,9},{2,10},{3,11},{4,12},{5,13},{6,14},{7,15},{8,0},{9,1},... | collective-permute-start | bytes 4915208 | tf_op jit(solution)/shard_map/ppermute | solution.py:235
  50.8 3.0 %copy-start = (bf16[512,1280]{1,0:T(8,128)(2,1)}, bf16[512,1280]{1,0:T(8,128)(2,1)S(1)}, u32[]{:S(2)}) copy-start(bf16[512,1280]{1,0:T(8,128)(2,1)S(1)} %collective-permute-done.5.over_ref) | copy-start | bytes 3932164
  53.8 5.7 %collective-permute-start.6 = (bf16[512,1280]{1,0:T(8,128)(2,1)}, bf16[512,1280]{1,0:T(8,128)(2,1)}, u32[]{:S(2)}, u32[]{:S(2)}) collective-permute-start(bf16[512,1280]{1,0:T(8,128)(2,1)} %broadcast_select_fusion.1), channel_id=1, source_target_pairs={{0,1},{1,0},{2,3},{3,2},{4,5},{5,4},{6,7},{7,6},{8,9},{9,8},{10,11... | collective-permute-start | bytes 3932168 | tf_op jit(solution)/shard_map/ppermute | solution.py:235
  67.9 17.6 %copy-start.2 = (bf16[1280,640]{1,0:T(8,128)(2,1)}, bf16[1280,640]{1,0:T(8,128)(2,1)S(1)}, u32[]{:S(2)}) copy-start(bf16[1280,640]{1,0:T(8,128)(2,1)S(1)} %collective-permute-done.9.inner_ref) | copy-start | bytes 4915204
  86.6 1.2 copy-start.5
  86.6 4.1 %collective-permute-start.13 = (bf16[1280,384]{1,0:T(8,128)(2,1)}, bf16[1280,384]{1,0:T(8,128)(2,1)}, u32[]{:S(2)}, u32[]{:S(2)}) collective-permute-start(bf16[1280,384]{1,0:T(8,128)(2,1)} %slice.41.refs_0_), channel_id=1, source_target_pairs={{0,1},{1,0},{2,3},{3,2},{4,5},{5,4},{6,7},{7,6},{8,9},{9,8},{10,11... | collective-permute-start | bytes 2949128 | tf_op jit(solution)/shard_map/ppermute | solution.py:235
  87.5 3.2 %copy-start.4 = (bf16[1280,256]{1,0:T(8,128)(2,1)}, bf16[1280,256]{1,0:T(8,128)(2,1)S(1)}, u32[]{:S(2)}) copy-start(bf16[1280,256]{1,0:T(8,128)(2,1)S(1)} %slice.42.refs_2_) | copy-start | bytes 1966084
  87.5 3.2 %collective-permute-start.14 = (bf16[1280,256]{1,0:T(8,128)(2,1)S(1)}, bf16[1280,256]{1,0:T(8,128)(2,1)}, u32[]{:S(2)}, u32[]{:S(2)}) collective-permute-start(bf16[1280,256]{1,0:T(8,128)(2,1)S(1)} %slice.42.refs_2_), channel_id=1, source_target_pairs={{0,1},{1,0},{2,3},{3,2},{4,5},{5,4},{6,7},{7,6},{8,9},{9,8},{10,11... | collective-permute-start | bytes 1966088 | tf_op jit(solution)/shard_map/ppermute | solution.py:235
  87.8 8.7 %copy-start.1 = (bf16[512,1280]{1,0:T(8,128)(2,1)S(1)}, bf16[512,1280]{1,0:T(8,128)(2,1)}, u32[]{:S(2)}) copy-start(bf16[512,1280]{1,0:T(8,128)(2,1)} %product.2) | copy-start | bytes 3932164
  87.8 26.2 %collective-permute-start.12 = (bf16[1280,384]{1,0:T(8,128)(2,1)S(1)}, bf16[1280,384]{1,0:T(8,128)(2,1)S(1)}, u32[]{:S(2)}, u32[]{:S(2)}) collective-permute-start(bf16[1280,384]{1,0:T(8,128)(2,1)S(1)} %copy-done.5), channel_id=1, source_target_pairs={{0,8},{1,9},{2,10},{3,11},{4,12},{5,13},{6,14},{7,15},{8,24},{9,25... | collective-permute-start | bytes 2949128 | tf_op jit(solution)/shard_map/ppermute | solution.py:235
  96.5 17.3 %copy-start.3 = (bf16[512,640]{1,0:T(8,128)(2,1)S(1)}, bf16[512,640]{1,0:T(8,128)(2,1)}, u32[]{:S(2)}) copy-start(bf16[512,640]{1,0:T(8,128)(2,1)} %product.3) | copy-start | bytes 1966084
  97.7 16.0 %collective-permute-start.15 = (bf16[512,640]{1,0:T(8,128)(2,1)S(1)}, bf16[512,640]{1,0:T(8,128)(2,1)S(1)}, u32[]{:S(2)}, u32[]{:S(2)}) collective-permute-start(bf16[512,640]{1,0:T(8,128)(2,1)S(1)} %broadcast_select_fusion.2), channel_id=1, source_target_pairs={{0,2},{1,3},{2,0},{3,1},{4,6},{5,7},{6,4},{7,5},{8,10},{9,11},{10,... | collective-permute-start | bytes 1966088 | tf_op jit(solution)/shard_map/ppermute | solution.py:235
  99.6 25.4 %collective-permute-start.19 = (bf16[1280,256]{1,0:T(8,128)(2,1)S(1)}, bf16[1280,256]{1,0:T(8,128)(2,1)S(1)}, u32[]{:S(2)}, u32[]{:S(2)}) collective-permute-start(bf16[1280,256]{1,0:T(8,128)(2,1)S(1)} %slice.44), channel_id=1, source_target_pairs={{0,8},{1,9},{2,10},{3,11},{4,12},{5,13},{6,14},{7,15},{8,24},{9,25... | collective-permute-start | bytes 1966088 | tf_op jit(solution)/shard_map/ppermute | solution.py:235
  114.0 1.0 copy-start.6
  120.0 2.5 %collective-permute-start.16 = (bf16[512,128]{1,0:T(8,128)(2,1)}, bf16[512,128]{1,0:T(8,128)(2,1)S(1)}, u32[]{:S(2)}, u32[]{:S(2)}) collective-permute-start(bf16[512,128]{1,0:T(8,128)(2,1)} %get-tuple-element.25), channel_id=1, source_target_pairs={{0,1},{1,0},{2,3},{3,2},{4,5},{5,4},{6,7},{7,6},{8,9},{9,8},{10,11... | collective-permute-start | bytes 393224 | tf_op jit(solution)/shard_map/ppermute | solution.py:235
  121.3 1.6 collective-permute-start.17
  121.3 1.7 %collective-permute-start.18 = (bf16[512,128]{1,0:T(8,128)(2,1)}, bf16[512,128]{1,0:T(8,128)(2,1)S(1)}, u32[]{:S(2)}, u32[]{:S(2)}) collective-permute-start(bf16[512,128]{1,0:T(8,128)(2,1)} %get-tuple-element.27), channel_id=1, source_target_pairs={{0,1},{1,0},{2,3},{3,2},{4,5},{5,4},{6,7},{7,6},{8,9},{9,8},{10,11... | collective-permute-start | bytes 393224 | tf_op jit(solution)/shard_map/ppermute | solution.py:235
  125.0 0.9 copy-start.7
  130.0 3.4 %collective-permute-start.21 = (bf16[512,256]{1,0:T(8,128)(2,1)}, bf16[512,256]{1,0:T(8,128)(2,1)S(1)}, u32[]{:S(2)}, u32[]{:S(2)}) collective-permute-start(bf16[512,256]{1,0:T(8,128)(2,1)} %get-tuple-element.33), channel_id=1, source_target_pairs={{0,1},{1,0},{2,3},{3,2},{4,5},{5,4},{6,7},{7,6},{8,9},{9,8},{10,11... | collective-permute-start | bytes 786440 | tf_op jit(solution)/shard_map/ppermute | solution.py:235
  132.0 10.7 %collective-permute-start.20 = (bf16[512,384]{1,0:T(8,128)(2,1)S(1)}, bf16[512,384]{1,0:T(8,128)(2,1)S(1)}, u32[]{:S(2)}, u32[]{:S(2)}) collective-permute-start(bf16[512,384]{1,0:T(8,128)(2,1)S(1)} %get-tuple-element.30), channel_id=1, source_target_pairs={{0,2},{1,3},{2,0},{3,1},{4,6},{5,7},{6,4},{7,5},{8,10},{9,11},{10,... | collective-permute-start | bytes 1179656 | tf_op jit(solution)/shard_map/ppermute | solution.py:235
  142.8 7.0 %collective-permute-start.24 = (bf16[512,256]{1,0:T(8,128)(2,1)S(1)}, bf16[512,256]{1,0:T(8,128)(2,1)S(1)}, u32[]{:S(2)}, u32[]{:S(2)}) collective-permute-start(bf16[512,256]{1,0:T(8,128)(2,1)S(1)} %broadcast_select_fusion.14), channel_id=1, source_target_pairs={{0,2},{1,3},{2,0},{3,1},{4,6},{5,7},{6,4},{7,5},{8,10},{9,11},{10,... | collective-permute-start | bytes 786440 | tf_op jit(solution)/shard_map/ppermute | solution.py:235
  144.2 10.0 %collective-permute-start.23 = (bf16[512,384]{1,0:T(8,128)(2,1)S(1)}, bf16[512,384]{1,0:T(8,128)(2,1)S(1)}, u32[]{:S(2)}, u32[]{:S(2)}) collective-permute-start(bf16[512,384]{1,0:T(8,128)(2,1)S(1)} %broadcast_select_fusion.3), channel_id=1, source_target_pairs={{0,1},{1,5},{2,3},{3,7},{4,0},{5,4},{6,2},{7,6},{8,9},{9,13},{10,1... | collective-permute-start | bytes 1179656 | tf_op jit(solution)/shard_map/ppermute | solution.py:235
  145.4 11.5 %collective-permute-start.22 = (bf16[512,384]{1,0:T(8,128)(2,1)S(1)}, bf16[512,384]{1,0:T(8,128)(2,1)S(1)}, u32[]{:S(2)}, u32[]{:S(2)}) collective-permute-start(bf16[512,384]{1,0:T(8,128)(2,1)S(1)} %get-tuple-element.36), channel_id=1, source_target_pairs={{0,2},{1,4},{2,0},{3,6},{4,1},{5,7},{6,3},{7,5},{8,10},{9,12},{10,... | collective-permute-start | bytes 1179656 | tf_op jit(solution)/shard_map/ppermute | solution.py:235
  150.0 7.2 %collective-permute-start.26 = (bf16[512,256]{1,0:T(8,128)(2,1)S(1)}, bf16[512,256]{1,0:T(8,128)(2,1)S(1)}, u32[]{:S(2)}, u32[]{:S(2)}) collective-permute-start(bf16[512,256]{1,0:T(8,128)(2,1)S(1)} %broadcast_select_fusion.11), channel_id=1, source_target_pairs={{0,1},{1,5},{2,3},{3,7},{4,0},{5,4},{6,2},{7,6},{8,9},{9,13},{10,1... | collective-permute-start | bytes 786440 | tf_op jit(solution)/shard_map/ppermute | solution.py:235
  151.1 11.1 %collective-permute-start.25 = (bf16[512,256]{1,0:T(8,128)(2,1)S(1)}, bf16[512,256]{1,0:T(8,128)(2,1)S(1)}, u32[]{:S(2)}, u32[]{:S(2)}) collective-permute-start(bf16[512,256]{1,0:T(8,128)(2,1)S(1)} %get-tuple-element.39), channel_id=1, source_target_pairs={{0,2},{1,4},{2,0},{3,6},{4,1},{5,7},{6,3},{7,5},{8,10},{9,12},{10,... | collective-permute-start | bytes 786440 | tf_op jit(solution)/shard_map/ppermute | solution.py:235
